TPU v7x, 1024 devices: a whole 8x8x8 slice. The times are simulated.
1024 devices in a mesh: section: 16 (over z_lo, x), tensor: 16 (over y, core), dp: 4 (over z_hi).
Axes of the slice: x: 8, y: 8, z: 8 (z_hi: 4, z_lo: 2; z = z_hi * 2 + z_lo), core: 2. Of those that a mesh axis runs over, the one named last changes fastest.
Arguments:
- weights: bfloat16 [16, 8192, 8192], P('section', 'tensor'), may hold values from -0.09375 to 0.09375
- contexts: bfloat16 [16, 4, 512, 8192], P('section', None, 'dp', 'tensor'), may hold values from -6 to 6
- residual: bfloat16 [16, 4, 512, 8192], P('section', None, 'dp', 'tensor'), may hold values from -6 to 6
- plan: int32 [16], P('section'), may hold values from 0 to 3, as said below
- upstream: bfloat16 [16, 512, 8192], P('section', 'dp', 'tensor'), may hold values from -6 to 6
Outputs:
- boundary: bfloat16 [16, 512, 8192], P('section', 'dp', 'tensor')
- ctx_grad: bfloat16 [16, 512, 8192], P('section', 'dp', 'tensor')
Inputs may be any that keep to these rules, and one draw needn't show every extreme that they name: `plan`: some section names micro-batch 0 and some other section names micro-batch 4 - 1.
All inputs are finite; a program needn't handle non-finite values.
Results may differ from a plain program's by a relative error of at most 0.001.
Values may be sent and summed in bfloat16 or wider, within the bound.
No kernel may reach another device: no remote copies, remote signals or barrier semaphores. Data moves between devices by JAX's collectives and lax.ppermute only.
A program may use at most 64 MiB of HBM per device.

v0:
```python
import jax
import jax.numpy as jnp
from jax import lax
from jax.sharding import PartitionSpec as P


def from_behind(value, axis, by):
    peers = lax.axis_size(axis)
    return lax.ppermute(value, axis, [(i, (i + by) % peers) for i in range(peers)])


def on_device(weights, contexts, residual, plan, upstream):
    w_local = weights[0]
    chosen = plan[0]
    context = lax.dynamic_index_in_dim(contexts[0], chosen, 0, keepdims=False)
    stream = lax.dynamic_index_in_dim(residual[0], chosen, 0, keepdims=False)
    summed = lax.psum_scatter(
        jnp.dot(context, w_local, preferred_element_type=jnp.float32),
        "tensor",
        scatter_dimension=0,
        tiled=True,
    )
    projected = lax.all_to_all(summed, "tensor", split_axis=1, concat_axis=0, tiled=True)
    hidden = (stream.astype(jnp.float32) + projected).astype(jnp.bfloat16)
    boundary = from_behind(hidden, "section", 1)
    incoming = from_behind(upstream[0], "section", -1)
    gradient = lax.dot_general(
        lax.all_gather(incoming, "tensor", axis=1, tiled=True),
        w_local,
        (((1,), (1,)), ((), ())),
        preferred_element_type=jnp.float32,
    )
    return (boundary[None], gradient.astype(jnp.bfloat16)[None])


def solution(mesh):
    return jax.shard_map(
        on_device,
        mesh=mesh,
        in_specs=(
            P("section", "tensor", None),
            P("section", None, "dp", "tensor"),
            P("section", None, "dp", "tensor"),
            P("section"),
            P("section", "dp", "tensor"),
        ),
        out_specs=(P("section", "dp", "tensor"), P("section", "dp", "tensor")),
        check_vma=False,
    )
```

profile of v0, /device:TPU:1, one launch (start us, length us, event | category | flops | bytes accessed | tf_op | source)
XLA Modules:
  0.0 157.9 jit_solution(1719446109919173950)
XLA Ops:
  7.2 0.0 copy-start
  7.2 0.0 reduce-scatter.2.cloned.1.call-start
  7.9 0.3 copy-done
  8.2 0.0 copy-start.2
  8.2 6.6 %fusion.2 = f32[128,8192]{1,0:T(8,128)} fusion(bf16[1,512,8192]{2,1,0:T(8,128)(2,1)} %param.5, bf16[1,4,128,512]{3,2,1,0:T(8,128)(2,1)S(1)} %copy-done, s32[]{:T(128)S(6)} %select_n.5), kind=kOutput, calls=%fused_computation.2 | convolution fusion | flops 1073741824 | bytes 12713988 | tf_op jit(solution)/shard_map/dot_general | solution.py:18
  14.8 0.0 reduce-scatter.2.cloned.1.call-update
  14.9 0.0 all-gather.2.cloned.1.call-start
  14.9 0.0 copy-done.2
  14.9 8.0 %collective-permute-start.1 = (bf16[128,512]{1,0:T(8,128)(2,1)S(1)}, bf16[128,512]{1,0:T(8,128)(2,1)S(1)}, u32[]{:S(2)}, u32[]{:S(2)}) collective-permute-start(bf16[128,512]{1,0:T(8,128)(2,1)S(1)} %bitcast.33), channel_id=1, source_target_pairs={{0,960},{64,0},{128,64},{192,128},{256,192},{320,256},{384,320},{4... | collective-permute-start | bytes 393224 | tf_op jit(solution)/shard_map/ppermute | solution.py:9
  23.0 1.9 %collective-permute-done.1 = bf16[128,512]{1,0:T(8,128)(2,1)S(1)} collective-permute-done((bf16[128,512]{1,0:T(8,128)(2,1)S(1)}, bf16[128,512]{1,0:T(8,128)(2,1)S(1)}, u32[]{:S(2)}, u32[]{:S(2)}) %collective-permute-start.1) | collective-permute-done | bytes 131104 | tf_op jit(solution)/shard_map/ppermute | solution.py:9
  24.9 0.0 copy-start.1
  24.9 0.7 copy-done.1
  25.6 0.0 all-gather.2.cloned.1.call-update
  25.6 68.7 %reduce-scatter.2.cloned.1.call-done = f32[8,8192]{1,0:T(8,128)} async-done(((f32[128,8192]{1,0:T(8,128)}), f32[8,8192]{1,0:T(8,128)}) %reduce-scatter.2.cloned.1.call-update) | async-done | bytes 262160 | tf_op jit(solution)/shard_map/reduce_scatter | solution.py:17
  94.3 17.6 %all_to_all.19 = f32[8,16,512]{2,0,1:T(8,128)S(1)} all-to-all(f32[8,16,512]{2,0,1:T(8,128)} %bitcast.31), channel_id=1, replica_groups=mesh['section'=16,'tensor'=16,'dp'=4] {'tensor'}, dimensions={1} | all-to-all | bytes 524288 | tf_op jit(solution)/shard_map/all_to_all | solution.py:23
  111.9 0.9 fusion.10
  112.8 3.0 %collective-permute-start = (bf16[128,512]{1,0:T(8,128)(2,1)S(1)}, bf16[128,512]{1,0:T(8,128)(2,1)S(1)}, u32[]{:S(2)}, u32[]{:S(2)}) collective-permute-start(bf16[128,512]{1,0:T(8,128)(2,1)S(1)} %fusion.10), channel_id=1, source_target_pairs={{0,64},{64,128},{128,192},{192,256},{256,320},{320,384},{384,448},... | collective-permute-start | bytes 393224 | tf_op jit(solution)/shard_map/ppermute | solution.py:9
  115.8 27.0 %all-gather.2.cloned.1.call-done = bf16[128,8192]{1,0:T(8,128)(2,1)} async-done(((bf16[128,512]{1,0:T(8,128)(2,1)}), bf16[128,8192]{1,0:T(8,128)(2,1)}) %all-gather.2.cloned.1.call-update) | async-done | bytes 2097168 | tf_op jit(solution)/shard_map/all_gather | solution.py:28
  142.8 7.6 %fusion.7 = bf16[1,128,512]{2,1,0:T(8,128)(2,1)} fusion(bf16[128,8192]{1,0:T(8,128)(2,1)} %all-gather.2.cloned.1.call-done, bf16[1,512,8192]{2,1,0:T(8,128)(2,1)} %param.5), kind=kOutput, calls=%fused_computation.5 | convolution fusion | flops 1073807360 | bytes 10616832 | tf_op jit(solution)/shard_map/dot_general | solution.py:27
  150.4 0.0 collective-permute-done
  150.4 0.7 copy.9
Async XLA Ops:
  7.2 1.1 copy-start
  7.2 87.1 %reduce-scatter.2.cloned.1.call-start = ((), (), s32[]{:S(2)}) async-start(), calls=%async_computation.2 | async-start | bytes 4456448 | tf_op jit(solution)/shard_map/reduce_scatter | solution.py:17
  8.2 6.7 %copy-start.2 = (bf16[1,128,512]{2,1,0:T(8,128)(2,1)S(1)}, bf16[1,128,512]{2,1,0:T(8,128)(2,1)}, u32[]{:S(2)}) copy-start(bf16[1,128,512]{2,1,0:T(8,128)(2,1)} %param.9) | copy-start | bytes 393220
  14.9 127.9 %all-gather.2.cloned.1.call-start = ((), (), s32[]{:S(2)}) async-start(), calls=%async_computation.3 | async-start | bytes 2228224 | tf_op jit(solution)/shard_map/all_gather | solution.py:28
  14.9 10.0 %collective-permute-start.1 = (bf16[128,512]{1,0:T(8,128)(2,1)S(1)}, bf16[128,512]{1,0:T(8,128)(2,1)S(1)}, u32[]{:S(2)}, u32[]{:S(2)}) collective-permute-start(bf16[128,512]{1,0:T(8,128)(2,1)S(1)} %bitcast.33), channel_id=1, source_target_pairs={{0,960},{64,0},{128,64},{192,128},{256,192},{320,256},{384,320},{4... | collective-permute-start | bytes 393224 | tf_op jit(solution)/shard_map/ppermute | solution.py:9
  24.9 0.7 copy-start.1
  112.8 37.5 %collective-permute-start = (bf16[128,512]{1,0:T(8,128)(2,1)S(1)}, bf16[128,512]{1,0:T(8,128)(2,1)S(1)}, u32[]{:S(2)}, u32[]{:S(2)}) collective-permute-start(bf16[128,512]{1,0:T(8,128)(2,1)S(1)} %fusion.10), channel_id=1, source_target_pairs={{0,64},{64,128},{128,192},{192,256},{256,320},{320,384},{384,448},... | collective-permute-start | bytes 393224 | tf_op jit(solution)/shard_map/ppermute | solution.py:9
Sparse Core Ops, SparseCore 0:
  15.0 79.2 reduce-scatter.1
  97.6 45.1 all-gather.1
where the time goes:
time: 158 us
  waiting for transfers between devices  97.6 us (62%)
  blocking collectives  17.6 us (11%)
  between operations  14.8 us (9%)
  matrix products  14.2 us (9%)
  starting transfers between devices  11.1 us (7%)
  local copies, waits for them, and re-layouts  1.62 us (1%)
    reduce_scatter x1, waiting for transfers between devices, on_device(): lax.psum_scatter(jnp.dot(context, w_local, preferred_element_type=jnp.flo...  68.7 us
    all_gather x1, waiting for transfers between devices, on_device(): lax.all_gather(incoming, 'tensor', axis=1, tiled=True)  27 us
    all_to_all x1, blocking collectives, on_device(): lax.all_to_all(summed, 'tensor', split_axis=1, concat_axis=0, tiled=True)  17.6 us
    ppermute x2, starting transfers between devices, from_behind(): lax.ppermute(value, axis, [(i, (i + by) % peers) for i in range(peers)])  11 us
    dot_general x1, matrix products, on_device(): lax.dot_general(lax.all_gather(incoming, 'tensor', axis=1, tiled=True), w...  7.6 us
    dot_general x1, matrix products, on_device(): jnp.dot(context, w_local, preferred_element_type=jnp.float32)  6.62 us
  transfers between devices with their start and end apart: 4, of which 3 were waited for; matrix products, arithmetic and copies ran while one was open for 5% of the time, Pallas kernels for 0%

commit v1 on v0

v1 whole, which is shorter than its diff:
```python
import functools

import jax
import jax.numpy as jnp
from jax import lax
from jax.experimental import pallas as pl
from jax.experimental.pallas import tpu as pltpu
from jax.sharding import PartitionSpec as P

ROWS = 128
WIDE = 1024
LEVELS = 32700.0


def split_shift(value, by):
    peers = lax.axis_size("tensor")
    chips = peers // 2
    pairs = []
    for chip in range(chips):
        pairs.append((2 * chip, 2 * ((chip + by) % chips)))
        pairs.append((2 * chip + 1, 2 * ((chip - by) % chips) + 1))
    return lax.ppermute(value, "tensor", pairs)


def core_swap(value):
    peers = lax.axis_size("tensor")
    return lax.ppermute(value, "tensor", [(i, i ^ 1) for i in range(peers)])


def next_section(value, by, flip=False):
    sections, peers = lax.axis_size("section"), lax.axis_size("tensor")
    pairs = [
        (s * peers + t, ((s + by) % sections) * peers + (t ^ 1 if flip else t))
        for s in range(sections)
        for t in range(peers)
    ]
    return lax.ppermute(value, ("section", "tensor"), pairs)


def project(order, context, weights, count):
    def body(order_ref, ctx_ref, w_ref, out_ref):
        out_ref[0] = jnp.dot(ctx_ref[...], w_ref[...], preferred_element_type=jnp.float32)

    heads = context.shape[1]
    return pl.pallas_call(
        body,
        grid_spec=pltpu.PrefetchScalarGridSpec(
            num_scalar_prefetch=1,
            grid=(count,),
            in_specs=[
                pl.BlockSpec((ROWS, heads), lambda k, o: (0, 0)),
                pl.BlockSpec((heads, WIDE), lambda k, o: (0, o[k])),
            ],
            out_specs=pl.BlockSpec((1, ROWS, WIDE), lambda k, o: (k, 0, 0)),
        ),
        out_shape=jax.ShapeDtypeStruct((count, ROWS, WIDE), jnp.float32),
        cost_estimate=pl.CostEstimate(
            flops=2 * count * ROWS * heads * WIDE,
            bytes_accessed=count * WIDE * (2 * heads + 4 * ROWS),
            transcendentals=0,
        ),
    )(order, context, weights)


def backproject(order, parts, start, weights):
    count = len(parts)
    heads = weights.shape[0]

    def body(order_ref, *refs):
        lhs, w_ref, out_ref = refs[:count], refs[-2], refs[-1]
        step = pl.program_id(0)

        @pl.when(step == 0)
        def _():
            if start is None:
                out_ref[...] = jnp.zeros_like(out_ref)
            else:
                out_ref[...] = refs[count][...]

        for k in range(count):

            @pl.when(step == k)
            def _(k=k):
                out_ref[...] += lax.dot_general(
                    lhs[k][...],
                    w_ref[...],
                    (((1,), (1,)), ((), ())),
                    preferred_element_type=jnp.float32,
                )

    whole = pl.BlockSpec((ROWS, WIDE), lambda k, o: (0, 0))
    total = pl.BlockSpec((ROWS, heads), lambda k, o: (0, 0))
    extra = [] if start is None else [start]
    return pl.pallas_call(
        body,
        grid_spec=pltpu.PrefetchScalarGridSpec(
            num_scalar_prefetch=1,
            grid=(count,),
            in_specs=[whole] * count
            + [total] * len(extra)
            + [pl.BlockSpec((heads, WIDE), lambda k, o: (0, o[k]))],
            out_specs=total,
        ),
        out_shape=jax.ShapeDtypeStruct((ROWS, heads), jnp.float32),
        cost_estimate=pl.CostEstimate(
            flops=2 * count * ROWS * heads * WIDE,
            bytes_accessed=count * WIDE * 2 * heads,
            transcendentals=0,
        ),
    )(order, *parts, *extra, weights)


def encode(value):
    top = jnp.maximum(jnp.max(jnp.abs(value), axis=0, keepdims=True), 1e-30)
    level = jnp.ceil(jnp.log2(top) * 256.0) + 1.0
    codes = jnp.round(value * (LEVELS * jnp.exp2(level * (-1.0 / 256.0))))
    both = jnp.concatenate([codes, jnp.broadcast_to(level, (16, value.shape[1]))], axis=0)
    return both.astype(jnp.int32).astype(jnp.int16)


def decode(coded):
    coded = coded.astype(jnp.int32).astype(jnp.float32)
    rows = coded.shape[0] - 16
    return coded[:rows] * (jnp.exp2(coded[rows : rows + 1] * (1.0 / 256.0)) * (1.0 / LEVELS))


def on_device(weights, contexts, residual, plan, upstream):
    w_local = weights[0]
    chosen = plan[0]
    context = lax.dynamic_index_in_dim(contexts[0], chosen, 0, keepdims=False)
    stream = lax.dynamic_index_in_dim(residual[0], chosen, 0, keepdims=False)

    place = lax.axis_index("tensor")
    chips = lax.axis_size("tensor") // 2
    chip, core = place // 2, place % 2
    way = 1 - 2 * core
    first = core == 0
    half = ROWS // 2

    def chunk(by):
        return (chip + way * by + 2 * chips) % chips

    def mine_half(x):
        return jnp.where(first, x[:half], x[half:])

    def other_half(x):
        return jnp.where(first, x[half:], x[:half])

    def at_half(x):
        zero = jnp.zeros_like(x)
        return jnp.where(first, jnp.concatenate([x, zero], 0), jnp.concatenate([zero, x], 0))

    same = next_section(upstream[0], -1)
    other = next_section(upstream[0], -1, flip=True)
    u0 = jnp.where(first, jnp.concatenate([same, other], 1), jnp.concatenate([other, same], 1))

    far = project(jnp.stack([chunk(-3), chunk(4), chunk(3)]).astype(jnp.int32), context, w_local, 3)
    near = project(
        jnp.stack([chunk(-2), chunk(-1), chunk(0), chunk(2), chunk(1)]).astype(jnp.int32), context, w_local, 5
    )
    far_in = core_swap(jnp.concatenate([far[0], other_half(far[1])], 0))
    own = near[2]
    own_mine = jnp.where(first, own[:, : WIDE // 2], own[:, WIDE // 2 :])
    own_other = jnp.where(first, own[:, WIDE // 2 :], own[:, : WIDE // 2])
    near_in = core_swap(jnp.concatenate([near[0], near[1]], 0))
    own_in = core_swap(own_other)

    q3 = split_shift(encode(far[2] + far_in[:ROWS]), 1)
    q4 = split_shift(encode(mine_half(far[1]) + far_in[ROWS:]), 2)
    q1 = split_shift(encode(near[4] + near_in[ROWS:]), 1)
    q2 = split_shift(encode(near[3] + near_in[:ROWS] + decode(q3) + at_half(decode(q4))), 2)

    g1 = split_shift(u0, 1)
    g2 = split_shift(u0, 2)
    g3 = split_shift(g2, 1)
    g4 = split_shift(mine_half(g2), 2)
    h12 = core_swap(jnp.concatenate([g1, g2], 0))
    h34 = core_swap(jnp.concatenate([g3, g4], 0))

    here = decode(q1) + decode(q2)
    here_mine = jnp.where(first, here[:, : WIDE // 2], here[:, WIDE // 2 :])
    here_other = jnp.where(first, here[:, WIDE // 2 :], here[:, : WIDE // 2])
    projected = own_mine + own_in + here_mine + core_swap(here_other)
    hidden = (stream.astype(jnp.float32) + projected).astype(jnp.bfloat16)
    boundary = next_section(hidden, 1)

    early = backproject(
        jnp.stack([chunk(0), chunk(-1), chunk(-2), chunk(1), chunk(2)]).astype(jnp.int32),
        [u0, g1, g2, h12[:ROWS], h12[ROWS:]],
        None,
        w_local,
    )
    facing = jnp.where(
        first, jnp.concatenate([g4, h34[ROWS:]], 0), jnp.concatenate([h34[ROWS:], g4], 0)
    )
    gradient = backproject(
        jnp.stack([chunk(-3), chunk(3), chunk(4)]).astype(jnp.int32),
        [g3, h34[:ROWS], facing],
        early,
        w_local,
    )
    return (boundary[None], gradient.astype(jnp.bfloat16)[None])


def solution(mesh):
    return jax.shard_map(
        on_device,
        mesh=mesh,
        in_specs=(
            P("section", "tensor", None),
            P("section", None, "dp", "tensor"),
            P("section", None, "dp", "tensor"),
            P("section"),
            P("section", "dp", "tensor"),
        ),
        out_specs=(P("section", "dp", "tensor"), P("section", "dp", "tensor")),
        check_vma=False,
    )
```

time: 158 us -> 131 us (0.83)
  waiting for transfers between devices: 97.6 us -> 18 us
  starting transfers between devices: 11.1 us -> 62.5 us
  Pallas kernels: 0 us -> 23.8 us
  blocking collectives: 17.6 us -> 0 us
  matrix products: 14.2 us -> 0 us
  other arithmetic: 0.93 us -> 14.7 us
  between operations: 14.8 us -> 2.03 us
  local copies, waits for them, and re-layouts: 1.62 us -> 8.65 us
    reduce_scatter x1 -> x0, waiting for transfers between devices: 68.7 us -> none  [on_device(): lax.psum_scatter(jnp.dot(context, w_local, preferred_element_type=jnp.flo...]
    ppermute x2 -> x17, starting transfers between devices: 11 us -> 62.5 us  [the longest x6 24.2 us: core_swap(): return lax.ppermute(value, 'tensor', [(i, i ^ 1) for i in range(peers)])]
    all_gather x1 -> x0, waiting for transfers between devices: 27 us -> none  [on_device(): lax.all_gather(incoming, 'tensor', axis=1, tiled=True)]
    pallas_call x0 -> x4, Pallas kernels: none -> 23.8 us  [the longest x2 12.1 us: backproject(): pl.pallas_call(body, grid_spec=pltpu.PrefetchScalarGridSpec(num_scalar_pr...]
    all_to_all x1 -> x0, blocking collectives: 17.6 us -> none  [on_device(): lax.all_to_all(summed, 'tensor', split_axis=1, concat_axis=0, tiled=True)]
    ppermute x2 -> x17, waiting for transfers between devices: 1.93 us -> 18 us  [the longest x8 12.2 us: split_shift(): return lax.ppermute(value, 'tensor', pairs)]
    dot_general x2 -> x0, matrix products: 14.2 us -> none  [the longest x1 7.6 us: on_device(): lax.dot_general(lax.all_gather(incoming, 'tensor', axis=1, tiled=True), w...]
    reduce_max x0 -> x4, other arithmetic: none -> 4.69 us  [encode(): top = jnp.maximum(jnp.max(jnp.abs(value), axis=0, keepdims=True), 1e-30)]
  transfers between devices with their start and end apart: 4 -> 17, of which waited for: 3 -> 4; matrix products, arithmetic and copies ran while one was open for 5% -> 17% of each run, Pallas kernels for 0% -> 18%
where the time goes in v1:
time: 131 us; the launch traced here: 130 us
  starting transfers between devices  62.5 us (48%)
  Pallas kernels  23.8 us (18%)
  waiting for transfers between devices  18 us (14%)
  other arithmetic  14.7 us (11%)
  local copies, waits for them, and re-layouts  8.65 us (7%)
  between operations  2.03 us (2%)
    ppermute x6, starting transfers between devices, core_swap(): return lax.ppermute(value, 'tensor', [(i, i ^ 1) for i in range(peers)])  24.2 us
    ppermute x8, starting transfers between devices, split_shift(): return lax.ppermute(value, 'tensor', pairs)  23.9 us
    ppermute x3, starting transfers between devices, next_section(): return lax.ppermute(value, ('section', 'tensor'), pairs)  14.4 us
    ppermute x8, waiting for transfers between devices, split_shift(): return lax.ppermute(value, 'tensor', pairs)  12.2 us
    pallas_call x2, Pallas kernels, backproject(): pl.pallas_call(body, grid_spec=pltpu.PrefetchScalarGridSpec(num_scalar_pr...  12.1 us
    pallas_call x2, Pallas kernels, project(): pl.pallas_call(body, grid_spec=pltpu.PrefetchScalarGridSpec(num_scalar_pr...  11.8 us
    ppermute x3, waiting for transfers between devices, next_section(): return lax.ppermute(value, ('section', 'tensor'), pairs)  5.86 us
    reduce_max x4, other arithmetic, encode(): top = jnp.maximum(jnp.max(jnp.abs(value), axis=0, keepdims=True), 1e-30)  4.69 us
  transfers between devices with their start and end apart: 17, of which 4 were waited for; matrix products, arithmetic and copies ran while one was open for 17% of the time, Pallas kernels for 18%

profile of v1, /device:TPU:1, one launch (start us, length us, event | category | flops | bytes accessed | tf_op | source)
XLA Modules:
  0.0 129.7 jit_solution(2377398416593416372)
XLA Ops:
  0.6 8.7 %collective-permute-start.10 = (bf16[128,512]{1,0:T(8,128)(2,1)}, bf16[128,512]{1,0:T(8,128)(2,1)S(1)}, u32[]{:S(2)}, u32[]{:S(2)}) collective-permute-start(bf16[128,512]{1,0:T(8,128)(2,1)} %bitcast.69), channel_id=1, source_target_pairs={{0,964},{4,960},{8,972},{12,968},{16,980},{20,976},{24,988},{28,98... | collective-permute-start | bytes 393224 | tf_op jit(solution)/shard_map/ppermute | solution.py:37
  9.4 3.1 %collective-permute-start.9 = (bf16[128,512]{1,0:T(8,128)(2,1)}, bf16[128,512]{1,0:T(8,128)(2,1)S(1)}, u32[]{:S(2)}, u32[]{:S(2)}) collective-permute-start(bf16[128,512]{1,0:T(8,128)(2,1)} %bitcast.70), channel_id=1, source_target_pairs={{0,960},{4,964},{8,968},{12,972},{16,976},{20,980},{24,984},{28,98... | collective-permute-start | bytes 393224 | tf_op jit(solution)/shard_map/ppermute | solution.py:37
  14.5 5.0 %shard_map.69 = f32[3,128,1024]{2,1,0:T(8,128)} custom-call(s32[3]{0:T(128)} %pad_add_fusion.order_ref, bf16[128,512]{1,0:T(8,128)(2,1)} %dynamic-slice_bitcast_fusion.ctx_ref, bf16[512,8192]{1,0:T(8,128)(2,1)} %bitcast.60), custom_call_target="tpu_custom_call" | custom-call | flops 402653184 | bytes 4718592 | tf_op jit(solution)/shard_map/pallas_call | solution.py:45
  22.5 8.2 %collective-permute-start.3 = (f32[192,1024]{1,0:T(8,128)}, f32[192,1024]{1,0:T(8,128)}, u32[]{:S(2)}, u32[]{:S(2)}) collective-permute-start(f32[192,1024]{1,0:T(8,128)} %pad_maximum_fusion.1), channel_id=1, source_target_pairs={{0,4},{4,0},{8,12},{12,8},{16,20},{20,16},{24,28},{28,24},{32,36},... | collective-permute-start | bytes 2359304 | tf_op jit(solution)/shard_map/ppermute | solution.py:27
  31.5 6.8 %shard_map.68 = f32[5,128,1024]{2,1,0:T(8,128)} custom-call(s32[5]{0:T(128)} %stack.49.order_ref, bf16[128,512]{1,0:T(8,128)(2,1)} %dynamic-slice_bitcast_fusion.ctx_ref, bf16[512,8192]{1,0:T(8,128)(2,1)} %bitcast.61), custom_call_target="tpu_custom_call" | custom-call | flops 671088640 | bytes 7864320 | tf_op jit(solution)/shard_map/pallas_call | solution.py:45
  38.3 1.5 %slice_bitcast_fusion.6 = (f32[128,1024]{1,0:T(8,128)S(1)}, f32[128,1024]{1,0:T(8,128)S(1)}, f32[128,1024]{1,0:T(8,128)S(1)}) fusion(f32[5,128,1024]{2,1,0:T(8,128)} %shard_map.68), kind=kLoop, calls=%fused_computation.26 | loop fusion | bytes 3145728 | tf_op jit(solution)/shard_map/squeeze | solution.py:162
  40.8 1.9 %collective-permute-start.1 = (f32[256,1024]{1,0:T(8,128)}, f32[256,1024]{1,0:T(8,128)}, u32[]{:S(2)}, u32[]{:S(2)}) collective-permute-start(f32[256,1024]{1,0:T(8,128)} %pad_maximum_fusion), channel_id=1, source_target_pairs={{0,4},{4,0},{8,12},{12,8},{16,20},{20,16},{24,28},{28,24},{32,36},... | collective-permute-start | bytes 3145736 | tf_op jit(solution)/shard_map/ppermute | solution.py:27
  42.9 1.9 %collective-permute-start.11 = (bf16[128,1024]{1,0:T(8,128)(2,1)S(1)}, bf16[128,1024]{1,0:T(8,128)(2,1)S(1)}, u32[]{:S(2)}, u32[]{:S(2)}) collective-permute-start(bf16[128,1024]{1,0:T(8,128)(2,1)S(1)} %maximum_select_fusion.refs_0_), channel_id=1, source_target_pairs={{0,16},{4,52},{8,24},{12,60},{16,32},{20,4},{24,40},{28,12},{32,48... | collective-permute-start | bytes 786440 | tf_op jit(solution)/shard_map/ppermute | solution.py:22
  45.6 2.4 %collective-permute-start = (f32[128,512]{1,0:T(8,128)}, f32[128,512]{1,0:T(8,128)}, u32[]{:S(2)}, u32[]{:S(2)}) collective-permute-start(f32[128,512]{1,0:T(8,128)} %slice_select_fusion.1), channel_id=1, source_target_pairs={{0,4},{4,0},{8,12},{12,8},{16,20},{20,16},{24,28},{28,24},{32,36},... | collective-permute-start | bytes 786440 | tf_op jit(solution)/shard_map/ppermute | solution.py:27
  49.2 1.9 %collective-permute-start.15 = (bf16[128,1024]{1,0:T(8,128)(2,1)S(1)}, bf16[128,1024]{1,0:T(8,128)(2,1)S(1)}, u32[]{:S(2)}, u32[]{:S(2)}) collective-permute-start(bf16[128,1024]{1,0:T(8,128)(2,1)S(1)} %maximum_select_fusion.refs_0_), channel_id=1, source_target_pairs={{0,8},{4,60},{8,16},{12,4},{16,24},{20,12},{24,32},{28,20},{32,40}... | collective-permute-start | bytes 786440 | tf_op jit(solution)/shard_map/ppermute | solution.py:22
  51.2 5.8 %collective-permute-start.13 = (bf16[64,1024]{1,0:T(8,128)(2,1)S(1)}, bf16[64,1024]{1,0:T(8,128)(2,1)S(1)}, u32[]{:S(2)}, u32[]{:S(2)}) collective-permute-start(bf16[64,1024]{1,0:T(8,128)(2,1)S(1)} %slice_select_fusion.2), channel_id=1, source_target_pairs={{0,16},{4,52},{8,24},{12,60},{16,32},{20,4},{24,40},{28,12},{32,48... | collective-permute-start | bytes 393224 | tf_op jit(solution)/shard_map/ppermute | solution.py:22
  58.1 1.9 %collective-permute-start.5 = (s16[80,1024]{1,0:T(8,128)(2,1)S(1)}, s16[80,1024]{1,0:T(8,128)(2,1)S(1)}, u32[]{:S(2)}, u32[]{:S(2)}) collective-permute-start(s16[80,1024]{1,0:T(8,128)(2,1)S(1)} %fusion.6), channel_id=1, source_target_pairs={{0,16},{4,52},{8,24},{12,60},{16,32},{20,4},{24,40},{28,12},{32,48... | collective-permute-start | bytes 491528 | tf_op jit(solution)/shard_map/ppermute | solution.py:22
  60.0 1.1 abs_reduce_fusion.1
  61.2 1.3 multiply_round-nearest-even_fusion.1
  62.5 3.0 %collective-permute-done.5 = s16[80,1024]{1,0:T(8,128)(2,1)S(1)} collective-permute-done((s16[80,1024]{1,0:T(8,128)(2,1)S(1)}, s16[80,1024]{1,0:T(8,128)(2,1)S(1)}, u32[]{:S(2)}, u32[]{:S(2)}) %collective-permute-start.5) | collective-permute-done | bytes 163872 | tf_op jit(solution)/shard_map/ppermute | solution.py:22
  65.5 4.7 %collective-permute-start.12 = (bf16[128,1024]{1,0:T(8,128)(2,1)S(1)}, bf16[128,1024]{1,0:T(8,128)(2,1)S(1)}, u32[]{:S(2)}, u32[]{:S(2)}) collective-permute-start(bf16[128,1024]{1,0:T(8,128)(2,1)S(1)} %collective-permute-done.11.refs_2_), channel_id=1, source_target_pairs={{0,8},{4,60},{8,16},{12,4},{16,24},{20,12},{24,32},{28,20},{32,40}... | collective-permute-start | bytes 786440 | tf_op jit(solution)/shard_map/ppermute | solution.py:22
  70.3 1.9 %collective-permute-start.4 = (s16[144,1024]{1,0:T(8,128)(2,1)S(1)}, s16[144,1024]{1,0:T(8,128)(2,1)S(1)}, u32[]{:S(2)}, u32[]{:S(2)}) collective-permute-start(s16[144,1024]{1,0:T(8,128)(2,1)S(1)} %fusion.1), channel_id=1, source_target_pairs={{0,8},{4,60},{8,16},{12,4},{16,24},{20,12},{24,32},{28,20},{32,40}... | collective-permute-start | bytes 884744 | tf_op jit(solution)/shard_map/ppermute | solution.py:22
  72.3 1.1 abs_reduce_fusion.2
  73.4 4.7 %collective-permute-done.4 = s16[144,1024]{1,0:T(8,128)(2,1)S(1)} collective-permute-done((s16[144,1024]{1,0:T(8,128)(2,1)S(1)}, s16[144,1024]{1,0:T(8,128)(2,1)S(1)}, u32[]{:S(2)}, u32[]{:S(2)}) %collective-permute-start.4) | collective-permute-done | bytes 294944 | tf_op jit(solution)/shard_map/ppermute | solution.py:22
  78.2 1.4 %abs_reduce_fusion = (f32[1024]{0:T(1024)S(1)}, f32[128,1024]{1,0:T(8,128)S(1)}, f32[128,1024]{1,0:T(8,128)S(1)}) fusion(f32[64,1024]{1,0:T(8,128)S(1)} %slice_multiply_fusion.3, pred[]{:T(512)S(6)} %eq.21, f32[1024]{0:T(1024)S(1)} %bitcast.65, f32[144,1024]{1,0:T(8,128)S(1)} %convert_convert_fusion.1, f32[256,1024]{1,0:T(8,128)} %collective-permute-done.1, ...), kind=kLoop, calls=%fused_computation.29 | loop fusion | flops 1309696 | bytes 3944449 | tf_op jit(solution)/shard_map/reduce_max | solution.py:114
  79.8 2.7 %collective-permute-start.6 = (s16[144,1024]{1,0:T(8,128)(2,1)S(1)}, s16[144,1024]{1,0:T(8,128)(2,1)S(1)}, u32[]{:S(2)}, u32[]{:S(2)}) collective-permute-start(s16[144,1024]{1,0:T(8,128)(2,1)S(1)} %fusion.2), channel_id=1, source_target_pairs={{0,16},{4,52},{8,24},{12,60},{16,32},{20,4},{24,40},{28,12},{32,48... | collective-permute-start | bytes 884744 | tf_op jit(solution)/shard_map/ppermute | solution.py:22
  82.6 4.6 %collective-permute-start.16 = (bf16[256,1024]{1,0:T(8,128)(2,1)S(1)}, bf16[256,1024]{1,0:T(8,128)(2,1)S(1)}, u32[]{:S(2)}, u32[]{:S(2)}) collective-permute-start(bf16[256,1024]{1,0:T(8,128)(2,1)S(1)} %pad_maximum_fusion.2), channel_id=1, source_target_pairs={{0,4},{4,0},{8,12},{12,8},{16,20},{20,16},{24,28},{28,24},{32,36},... | collective-permute-start | bytes 1572872 | tf_op jit(solution)/shard_map/ppermute | solution.py:27
  87.2 1.9 %collective-permute-start.14 = (bf16[192,1024]{1,0:T(8,128)(2,1)S(1)}, bf16[192,1024]{1,0:T(8,128)(2,1)}, u32[]{:S(2)}, u32[]{:S(2)}) collective-permute-start(bf16[192,1024]{1,0:T(8,128)(2,1)S(1)} %pad_maximum_fusion.3), channel_id=1, source_target_pairs={{0,4},{4,0},{8,12},{12,8},{16,20},{20,16},{24,28},{28,24},{32,36},... | collective-permute-start | bytes 1179656 | tf_op jit(solution)/shard_map/ppermute | solution.py:27
  89.3 3.1 %collective-permute-start.2 = (s16[144,1024]{1,0:T(8,128)(2,1)S(1)}, s16[144,1024]{1,0:T(8,128)(2,1)S(1)}, u32[]{:S(2)}, u32[]{:S(2)}) collective-permute-start(s16[144,1024]{1,0:T(8,128)(2,1)S(1)} %fusion), channel_id=1, source_target_pairs={{0,8},{4,60},{8,16},{12,4},{16,24},{20,12},{24,32},{28,20},{32,40}... | collective-permute-start | bytes 884744 | tf_op jit(solution)/shard_map/ppermute | solution.py:22
  92.5 4.5 %collective-permute-done.2 = s16[144,1024]{1,0:T(8,128)(2,1)S(1)} collective-permute-done((s16[144,1024]{1,0:T(8,128)(2,1)S(1)}, s16[144,1024]{1,0:T(8,128)(2,1)S(1)}, u32[]{:S(2)}, u32[]{:S(2)}) %collective-permute-start.2) | collective-permute-done | bytes 294944 | tf_op jit(solution)/shard_map/ppermute | solution.py:22
  97.3 5.1 %collective-permute-start.7 = (f32[128,512]{1,0:T(8,128)S(1)}, f32[128,512]{1,0:T(8,128)S(1)}, u32[]{:S(2)}, u32[]{:S(2)}) collective-permute-start(f32[128,512]{1,0:T(8,128)S(1)} %slice_select_fusion), channel_id=1, source_target_pairs={{0,4},{4,0},{8,12},{12,8},{16,20},{20,16},{24,28},{28,24},{32,36},... | collective-permute-start | bytes 786440 | tf_op jit(solution)/shard_map/ppermute | solution.py:27
  103.3 7.0 %shard_map.70.refs_3_ = f32[128,512]{1,0:T(8,128)} custom-call(s32[5]{0:T(128)} %stack.55.order_ref, bf16[128,1024]{1,0:T(8,128)(2,1)} %copy-done.5, bf16[128,1024]{1,0:T(8,128)(2,1)} %copy-done.7, bf16[128,1024]{1,0:T(8,128)(2,1)} %copy-done.3, bf16[128,1024]{1,0:T(8,128)(2,1)} %get-tuple-element.11.refs_3_, bf16[128,1024]{1,0:T(8,128)(2,1)} %get-tuple-element.10.refs_4_, ...), custom_call_target="tpu_custom_call" | custom-call | flops 671088640 | bytes 5242880 | tf_op jit(solution)/shard_map/pallas_call | solution.py:94
  110.3 1.7 %slice.164.refs_1_ = bf16[128,1024]{1,0:T(8,128)(2,1)} slice(bf16[192,1024]{1,0:T(8,128)(2,1)} %collective-permute-done.14), slice={[0:128], [0:1024]} | slice | bytes 524288 | tf_op jit(solution)/shard_map/slice | solution.py:198
  113.6 5.1 %shard_map.71 = f32[128,512]{1,0:T(8,128)} custom-call(s32[3]{0:T(128)} %pad_add_fusion.1.order_ref, bf16[128,1024]{1,0:T(8,128)(2,1)} %copy-done.4, bf16[128,1024]{1,0:T(8,128)(2,1)} %slice.164.refs_1_, bf16[128,1024]{1,0:T(8,128)(2,1)} %maximum_select_fusion.1.refs_2_, f32[128,512]{1,0:T(8,128)} %shard_map.70.refs_3_, bf16[512,8192]{1,0:T(8,128)(2,1)} %bitcast.63), custom_call_target="tpu_custom_call" | custom-call | flops 402653184 | bytes 3145728 | tf_op jit(solution)/shard_map/pallas_call | solution.py:94
  118.7 1.2 fusion.7
  119.9 2.6 %collective-permute-start.8 = (bf16[128,512]{1,0:T(8,128)(2,1)S(1)}, bf16[128,512]{1,0:T(8,128)(2,1)S(1)}, u32[]{:S(2)}, u32[]{:S(2)}) collective-permute-start(bf16[128,512]{1,0:T(8,128)(2,1)S(1)} %fusion.7), channel_id=1, source_target_pairs={{0,64},{4,68},{8,72},{12,76},{16,80},{20,84},{24,88},{28,92},{32,9... | collective-permute-start | bytes 393224 | tf_op jit(solution)/shard_map/ppermute | solution.py:37
  123.2 5.9 %collective-permute-done.8 = bf16[128,512]{1,0:T(8,128)(2,1)S(1)} collective-permute-done((bf16[128,512]{1,0:T(8,128)(2,1)S(1)}, bf16[128,512]{1,0:T(8,128)(2,1)S(1)}, u32[]{:S(2)}, u32[]{:S(2)}) %collective-permute-start.8) | collective-permute-done | bytes 131104 | tf_op jit(solution)/shard_map/ppermute | solution.py:37
  (74 shorter events, 14.0 us)
Async XLA Ops:
  0.6 12.6 %copy-start = (bf16[1,4,128,512]{3,2,1,0:T(8,128)(2,1)S(1)}, bf16[1,4,128,512]{3,2,1,0:T(8,128)(2,1)}, u32[]{:S(2)}) copy-start(bf16[1,4,128,512]{3,2,1,0:T(8,128)(2,1)} %param.6) | copy-start | bytes 1572868
  0.6 42.1 %collective-permute-start.10 = (bf16[128,512]{1,0:T(8,128)(2,1)}, bf16[128,512]{1,0:T(8,128)(2,1)S(1)}, u32[]{:S(2)}, u32[]{:S(2)}) collective-permute-start(bf16[128,512]{1,0:T(8,128)(2,1)} %bitcast.69), channel_id=1, source_target_pairs={{0,964},{4,960},{8,972},{12,968},{16,980},{20,976},{24,988},{28,98... | collective-permute-start | bytes 393224 | tf_op jit(solution)/shard_map/ppermute | solution.py:37
  9.4 33.4 %collective-permute-start.9 = (bf16[128,512]{1,0:T(8,128)(2,1)}, bf16[128,512]{1,0:T(8,128)(2,1)S(1)}, u32[]{:S(2)}, u32[]{:S(2)}) collective-permute-start(bf16[128,512]{1,0:T(8,128)(2,1)} %bitcast.70), channel_id=1, source_target_pairs={{0,960},{4,964},{8,968},{12,972},{16,976},{20,980},{24,984},{28,98... | collective-permute-start | bytes 393224 | tf_op jit(solution)/shard_map/ppermute | solution.py:37
  22.5 34.4 %collective-permute-start.3 = (f32[192,1024]{1,0:T(8,128)}, f32[192,1024]{1,0:T(8,128)}, u32[]{:S(2)}, u32[]{:S(2)}) collective-permute-start(f32[192,1024]{1,0:T(8,128)} %pad_maximum_fusion.1), channel_id=1, source_target_pairs={{0,4},{4,0},{8,12},{12,8},{16,20},{20,16},{24,28},{28,24},{32,36},... | collective-permute-start | bytes 2359304 | tf_op jit(solution)/shard_map/ppermute | solution.py:27
  39.7 17.2 %copy-start.2 = (f32[3,128,1024]{2,1,0:T(8,128)S(1)}, f32[3,128,1024]{2,1,0:T(8,128)}, u32[]{:S(2)}) copy-start(f32[3,128,1024]{2,1,0:T(8,128)} %shard_map.69) | copy-start | bytes 4718596
  40.8 29.5 %collective-permute-start.1 = (f32[256,1024]{1,0:T(8,128)}, f32[256,1024]{1,0:T(8,128)}, u32[]{:S(2)}, u32[]{:S(2)}) collective-permute-start(f32[256,1024]{1,0:T(8,128)} %pad_maximum_fusion), channel_id=1, source_target_pairs={{0,4},{4,0},{8,12},{12,8},{16,20},{20,16},{24,28},{28,24},{32,36},... | collective-permute-start | bytes 3145736 | tf_op jit(solution)/shard_map/ppermute | solution.py:27
  42.8 15.3 %copy-start.5 = (bf16[128,1024]{1,0:T(8,128)(2,1)}, bf16[128,1024]{1,0:T(8,128)(2,1)S(1)}, u32[]{:S(2)}) copy-start(bf16[128,1024]{1,0:T(8,128)(2,1)S(1)} %maximum_select_fusion.refs_0_) | copy-start | bytes 786436
  42.9 8.3 %collective-permute-start.11 = (bf16[128,1024]{1,0:T(8,128)(2,1)S(1)}, bf16[128,1024]{1,0:T(8,128)(2,1)S(1)}, u32[]{:S(2)}, u32[]{:S(2)}) collective-permute-start(bf16[128,1024]{1,0:T(8,128)(2,1)S(1)} %maximum_select_fusion.refs_0_), channel_id=1, source_target_pairs={{0,16},{4,52},{8,24},{12,60},{16,32},{20,4},{24,40},{28,12},{32,48... | collective-permute-start | bytes 786440 | tf_op jit(solution)/shard_map/ppermute | solution.py:22
  45.6 73.2 %collective-permute-start = (f32[128,512]{1,0:T(8,128)}, f32[128,512]{1,0:T(8,128)}, u32[]{:S(2)}, u32[]{:S(2)}) collective-permute-start(f32[128,512]{1,0:T(8,128)} %slice_select_fusion.1), channel_id=1, source_target_pairs={{0,4},{4,0},{8,12},{12,8},{16,20},{20,16},{24,28},{28,24},{32,36},... | collective-permute-start | bytes 786440 | tf_op jit(solution)/shard_map/ppermute | solution.py:27
  49.2 33.3 %collective-permute-start.15 = (bf16[128,1024]{1,0:T(8,128)(2,1)S(1)}, bf16[128,1024]{1,0:T(8,128)(2,1)S(1)}, u32[]{:S(2)}, u32[]{:S(2)}) collective-permute-start(bf16[128,1024]{1,0:T(8,128)(2,1)S(1)} %maximum_select_fusion.refs_0_), channel_id=1, source_target_pairs={{0,8},{4,60},{8,16},{12,4},{16,24},{20,12},{24,32},{28,20},{32,40}... | collective-permute-start | bytes 786440 | tf_op jit(solution)/shard_map/ppermute | solution.py:22
  51.2 31.3 %copy-start.3 = (bf16[128,1024]{1,0:T(8,128)(2,1)}, bf16[128,1024]{1,0:T(8,128)(2,1)S(1)}, u32[]{:S(2)}) copy-start(bf16[128,1024]{1,0:T(8,128)(2,1)S(1)} %collective-permute-done.11.refs_2_) | copy-start | bytes 786436
  51.2 36.0 %collective-permute-start.13 = (bf16[64,1024]{1,0:T(8,128)(2,1)S(1)}, bf16[64,1024]{1,0:T(8,128)(2,1)S(1)}, u32[]{:S(2)}, u32[]{:S(2)}) collective-permute-start(bf16[64,1024]{1,0:T(8,128)(2,1)S(1)} %slice_select_fusion.2), channel_id=1, source_target_pairs={{0,16},{4,52},{8,24},{12,60},{16,32},{20,4},{24,40},{28,12},{32,48... | collective-permute-start | bytes 393224 | tf_op jit(solution)/shard_map/ppermute | solution.py:22
  58.1 7.4 %collective-permute-start.5 = (s16[80,1024]{1,0:T(8,128)(2,1)S(1)}, s16[80,1024]{1,0:T(8,128)(2,1)S(1)}, u32[]{:S(2)}, u32[]{:S(2)}) collective-permute-start(s16[80,1024]{1,0:T(8,128)(2,1)S(1)} %fusion.6), channel_id=1, source_target_pairs={{0,16},{4,52},{8,24},{12,60},{16,32},{20,4},{24,40},{28,12},{32,48... | collective-permute-start | bytes 491528 | tf_op jit(solution)/shard_map/ppermute | solution.py:22
  61.2 11.1 %copy-start.1 = (f32[5,128,1024]{2,1,0:T(8,128)S(1)}, f32[5,128,1024]{2,1,0:T(8,128)}, u32[]{:S(2)}) copy-start(f32[5,128,1024]{2,1,0:T(8,128)} %shard_map.68) | copy-start | bytes 7864324
  65.5 21.7 %collective-permute-start.12 = (bf16[128,1024]{1,0:T(8,128)(2,1)S(1)}, bf16[128,1024]{1,0:T(8,128)(2,1)S(1)}, u32[]{:S(2)}, u32[]{:S(2)}) collective-permute-start(bf16[128,1024]{1,0:T(8,128)(2,1)S(1)} %collective-permute-done.11.refs_2_), channel_id=1, source_target_pairs={{0,8},{4,60},{8,16},{12,4},{16,24},{20,12},{24,32},{28,20},{32,40}... | collective-permute-start | bytes 786440 | tf_op jit(solution)/shard_map/ppermute | solution.py:22
  70.3 7.8 %collective-permute-start.4 = (s16[144,1024]{1,0:T(8,128)(2,1)S(1)}, s16[144,1024]{1,0:T(8,128)(2,1)S(1)}, u32[]{:S(2)}, u32[]{:S(2)}) collective-permute-start(s16[144,1024]{1,0:T(8,128)(2,1)S(1)} %fusion.1), channel_id=1, source_target_pairs={{0,8},{4,60},{8,16},{12,4},{16,24},{20,12},{24,32},{28,20},{32,40}... | collective-permute-start | bytes 884744 | tf_op jit(solution)/shard_map/ppermute | solution.py:22
  79.8 12.5 %collective-permute-start.6 = (s16[144,1024]{1,0:T(8,128)(2,1)S(1)}, s16[144,1024]{1,0:T(8,128)(2,1)S(1)}, u32[]{:S(2)}, u32[]{:S(2)}) collective-permute-start(s16[144,1024]{1,0:T(8,128)(2,1)S(1)} %fusion.2), channel_id=1, source_target_pairs={{0,16},{4,52},{8,24},{12,60},{16,32},{20,4},{24,40},{28,12},{32,48... | collective-permute-start | bytes 884744 | tf_op jit(solution)/shard_map/ppermute | solution.py:22
  82.5 9.9 %copy-start.7 = (bf16[128,1024]{1,0:T(8,128)(2,1)}, bf16[128,1024]{1,0:T(8,128)(2,1)S(1)}, u32[]{:S(2)}) copy-start(bf16[128,1024]{1,0:T(8,128)(2,1)S(1)} %collective-permute-done.15.refs_1_) | copy-start | bytes 786436
  82.6 19.9 %collective-permute-start.16 = (bf16[256,1024]{1,0:T(8,128)(2,1)S(1)}, bf16[256,1024]{1,0:T(8,128)(2,1)S(1)}, u32[]{:S(2)}, u32[]{:S(2)}) collective-permute-start(bf16[256,1024]{1,0:T(8,128)(2,1)S(1)} %pad_maximum_fusion.2), channel_id=1, source_target_pairs={{0,4},{4,0},{8,12},{12,8},{16,20},{20,16},{24,28},{28,24},{32,36},... | collective-permute-start | bytes 1572872 | tf_op jit(solution)/shard_map/ppermute | solution.py:27
  87.2 9.9 %copy-start.4 = (bf16[128,1024]{1,0:T(8,128)(2,1)}, bf16[128,1024]{1,0:T(8,128)(2,1)S(1)}, u32[]{:S(2)}) copy-start(bf16[128,1024]{1,0:T(8,128)(2,1)S(1)} %collective-permute-done.12.refs_0_) | copy-start | bytes 786436
  87.2 23.0 %collective-permute-start.14 = (bf16[192,1024]{1,0:T(8,128)(2,1)S(1)}, bf16[192,1024]{1,0:T(8,128)(2,1)}, u32[]{:S(2)}, u32[]{:S(2)}) collective-permute-start(bf16[192,1024]{1,0:T(8,128)(2,1)S(1)} %pad_maximum_fusion.3), channel_id=1, source_target_pairs={{0,4},{4,0},{8,12},{12,8},{16,20},{20,16},{24,28},{28,24},{32,36},... | collective-permute-start | bytes 1179656 | tf_op jit(solution)/shard_map/ppermute | solution.py:27
  89.3 7.8 %collective-permute-start.2 = (s16[144,1024]{1,0:T(8,128)(2,1)S(1)}, s16[144,1024]{1,0:T(8,128)(2,1)S(1)}, u32[]{:S(2)}, u32[]{:S(2)}) collective-permute-start(s16[144,1024]{1,0:T(8,128)(2,1)S(1)} %fusion), channel_id=1, source_target_pairs={{0,8},{4,60},{8,16},{12,4},{16,24},{20,12},{24,32},{28,20},{32,40}... | collective-permute-start | bytes 884744 | tf_op jit(solution)/shard_map/ppermute | solution.py:22
  97.3 21.5 %collective-permute-start.7 = (f32[128,512]{1,0:T(8,128)S(1)}, f32[128,512]{1,0:T(8,128)S(1)}, u32[]{:S(2)}, u32[]{:S(2)}) collective-permute-start(f32[128,512]{1,0:T(8,128)S(1)} %slice_select_fusion), channel_id=1, source_target_pairs={{0,4},{4,0},{8,12},{12,8},{16,20},{20,16},{24,28},{28,24},{32,36},... | collective-permute-start | bytes 786440 | tf_op jit(solution)/shard_map/ppermute | solution.py:27
  118.7 3.8 %copy-start.6 = (f32[128,512]{1,0:T(8,128)S(1)}, f32[128,512]{1,0:T(8,128)}, u32[]{:S(2)}) copy-start(f32[128,512]{1,0:T(8,128)} %shard_map.71) | copy-start | bytes 786436
  119.9 9.1 %collective-permute-start.8 = (bf16[128,512]{1,0:T(8,128)(2,1)S(1)}, bf16[128,512]{1,0:T(8,128)(2,1)S(1)}, u32[]{:S(2)}, u32[]{:S(2)}) collective-permute-start(bf16[128,512]{1,0:T(8,128)(2,1)S(1)} %fusion.7), channel_id=1, source_target_pairs={{0,64},{4,68},{8,72},{12,76},{16,80},{20,84},{24,88},{28,92},{32,9... | collective-permute-start | bytes 393224 | tf_op jit(solution)/shard_map/ppermute | solution.py:37

commit v2 on v0

v2 whole, which is shorter than its diff:
```python
import jax
import jax.numpy as jnp
from jax import lax
from jax.experimental import pallas as pl
from jax.experimental.pallas import tpu as pltpu
from jax.sharding import PartitionSpec as P

ROWS = 128
HALF = 64
BLOCK = 512
WIDE = 1024
LEVELS = 32700.0
F32, BF16, CODE = jnp.float32, jnp.bfloat16, jnp.int16

SMEM = pl.BlockSpec(memory_space=pltpu.SMEM)
VMEM = pl.BlockSpec(memory_space=pltpu.VMEM)
ANY = pl.BlockSpec(memory_space=pl.ANY)


def split_shift(value, by):
    peers = lax.axis_size("tensor")
    chips = peers // 2
    pairs = []
    for chip in range(chips):
        pairs.append((2 * chip, 2 * ((chip + by) % chips)))
        pairs.append((2 * chip + 1, 2 * ((chip - by) % chips) + 1))
    return lax.ppermute(value, "tensor", pairs)


def core_swap(value):
    peers = lax.axis_size("tensor")
    return lax.ppermute(value, "tensor", [(i, i ^ 1) for i in range(peers)])


def next_section(value, by, shift=0):
    sections, peers = lax.axis_size("section"), lax.axis_size("tensor")
    pairs = []
    for s in range(sections):
        for t in range(peers):
            chip = (t // 2 + (1 - 2 * (t % 2)) * shift) % (peers // 2)
            pairs.append((s * peers + t, ((s + by) % sections) * peers + 2 * chip + t % 2))
    return lax.ppermute(value, ("section", "tensor"), pairs)


def call(body, outs, ins, specs, scratch=(), flops=0, moved=0, vmem=24):
    return pl.pallas_call(
        body,
        grid=(1,),
        in_specs=specs,
        out_specs=[VMEM] * len(outs),
        out_shape=[jax.ShapeDtypeStruct(s, d) for s, d in outs],
        scratch_shapes=list(scratch),
        compiler_params=pltpu.CompilerParams(vmem_limit_bytes=vmem * 2**20),
        cost_estimate=pl.CostEstimate(flops=flops, bytes_accessed=moved, transcendentals=0),
    )(*ins)


def rows_of(count, index, width=WIDE):
    return pl.BlockSpec((count, width), lambda i: (index, 0))


def chunk_of(place, by, chips):
    core = place % 2
    return (place // 2 + (1 - 2 * core) * by + 2 * chips) % chips


def chunk_of_weights(w_ref, place, by, chips):
    return w_ref[:, pl.ds(pl.multiple_of(chunk_of(place, by, chips) * WIDE, WIDE), WIDE)]


def encode(value, out_ref):
    rows = value.shape[0]
    top = jnp.maximum(jnp.max(jnp.abs(value), axis=0, keepdims=True), 1e-30)
    level = jnp.ceil(jnp.log2(top) * 256.0) + 1.0
    codes = jnp.round(value * (LEVELS * jnp.exp2(level * (-1.0 / 256.0))))
    out_ref[:rows] = codes.astype(jnp.int32).astype(CODE)
    out_ref[rows:] = jnp.broadcast_to(level, (16, value.shape[1])).astype(jnp.int32).astype(CODE)


def decode(ref):
    rows = ref.shape[0] - 16
    level = ref[rows:].astype(jnp.int32).astype(F32)[:1]
    return ref[:rows].astype(jnp.int32).astype(F32) * (jnp.exp2(level * (1.0 / 256.0)) * (1.0 / LEVELS))


def project(place, plan, contexts, weights, chips):

    order = (-3, 3, -2, 2, -1, 1, 4, 0)

    def body(place_ref, plan_ref, ctx_ref, w_ref, send_ref, keep_ref, own_ref, held, ctx, full, sems, ctx_sem):
        here = place_ref[0]
        core = here % 2
        mine, theirs = core, 1 - core
        fetch = pltpu.make_async_copy(ctx_ref.at[plan_ref[0]], ctx, ctx_sem)
        fetch.start()
        copies = []
        for slot, by in enumerate(order):
            at = pl.multiple_of(chunk_of(here, by, chips) * WIDE, WIDE)
            copies.append(pltpu.make_async_copy(w_ref.at[:, pl.ds(at, WIDE)], held.at[slot], sems.at[slot]))
        for copy in copies:
            copy.start()
        fetch.wait()

        def product(by):
            slot = order.index(by)
            copies[slot].wait()
            return jnp.dot(ctx[...], held[slot], preferred_element_type=F32)

        for slot, by in enumerate((3, 2, 1)):
            rows = slice(slot * ROWS, (slot + 1) * ROWS)
            send_ref[rows] = product(-by)
            keep_ref[rows] = product(by)
        full[...] = product(4)
        send_ref[3 * ROWS : 3 * ROWS + HALF] = full[pl.ds(pl.multiple_of(theirs * HALF, HALF), HALF)]
        keep_ref[3 * ROWS :] = full[pl.ds(pl.multiple_of(mine * HALF, HALF), HALF)]
        full[...] = product(0)
        for part, at in ((0, 0), (1, HALF)):
            lanes = slice(part * BLOCK, (part + 1) * BLOCK)
            rows = slice(at, at + HALF)
            send_ref[3 * ROWS + HALF :, lanes] = full[rows, pl.ds(pl.multiple_of(theirs * BLOCK, BLOCK), BLOCK)]
            own_ref[:, lanes] = full[rows, pl.ds(pl.multiple_of(mine * BLOCK, BLOCK), BLOCK)]

    heads = weights.shape[0]
    return call(
        body,
        [((4 * ROWS, WIDE), F32), ((3 * ROWS + HALF, WIDE), F32), ((HALF, WIDE), F32)],
        (place, plan, contexts, weights),
        [SMEM, SMEM, ANY, ANY],
        [
            pltpu.VMEM((8, heads, WIDE), BF16),
            pltpu.VMEM((ROWS, heads), BF16),
            pltpu.VMEM((ROWS, WIDE), F32),
            pltpu.SemaphoreType.DMA((8,)),
            pltpu.SemaphoreType.DMA,
        ],
        flops=16 * ROWS * heads * WIDE,
        moved=16 * heads * WIDE,
        vmem=58,
    )


def encode_far(place, keep, arrived):
    def body(place_ref, keep_ref, in_ref, q3_ref, q4_ref, q1_ref):
        encode(keep_ref[:ROWS] + in_ref[:ROWS], q3_ref)
        encode(keep_ref[3 * ROWS :] + in_ref[3 * ROWS : 3 * ROWS + HALF], q4_ref)
        encode(keep_ref[2 * ROWS : 3 * ROWS] + in_ref[2 * ROWS : 3 * ROWS], q1_ref)

    return call(
        body,
        [((ROWS + 16, WIDE), CODE), ((HALF + 16, WIDE), CODE), ((ROWS + 16, WIDE), CODE)],
        (place, keep, arrived),
        [SMEM, VMEM, VMEM],
        flops=2**21,
        moved=2**21,
    )


def encode_two(place, keep, arrived, q3, q4):
    def body(place_ref, keep_ref, in_ref, q3_ref, q4_ref, q_ref, total):
        mine = pl.multiple_of((place_ref[0] % 2) * HALF, HALF)
        total[...] = keep_ref[...] + in_ref[...] + decode(q3_ref)
        total[pl.ds(mine, HALF)] += decode(q4_ref)
        encode(total[...], q_ref)

    return call(
        body,
        [((ROWS + 16, WIDE), CODE)],
        (place, keep, arrived, q3, q4),
        [SMEM, rows_of(ROWS, 1), rows_of(ROWS, 1), VMEM, VMEM],
        [pltpu.VMEM((ROWS, WIDE), F32)],
        flops=2**20,
        moved=2**21,
    )[0]


def gather_home(place, plan, q1, q2, own, arrived, residual):
    def body(place_ref, plan_ref, q1_ref, q2_ref, own_ref, in_ref, res_ref, send_ref, part_ref, full, stream, sem):
        fetch = pltpu.make_async_copy(res_ref.at[plan_ref[0]], stream, sem)
        fetch.start()
        core = place_ref[0] % 2
        mine = pl.multiple_of(core * BLOCK, BLOCK)
        theirs = pl.multiple_of((1 - core) * BLOCK, BLOCK)
        full[...] = decode(q1_ref) + decode(q2_ref)
        send_ref[...] = full[:, pl.ds(theirs, BLOCK)]
        fetch.wait()
        for part, at in ((0, 0), (1, HALF)):
            lanes = slice(part * BLOCK, (part + 1) * BLOCK)
            rows = slice(at, at + HALF)
            part_ref[rows] = (
                full[rows, pl.ds(mine, BLOCK)]
                + own_ref[:, lanes]
                + in_ref[:, lanes]
                + stream[rows].astype(F32)
            )

    return call(
        body,
        [((ROWS, BLOCK), F32)] * 2,
        (place, plan, q1, q2, own, arrived, residual),
        [SMEM, SMEM, VMEM, VMEM, VMEM, rows_of(HALF, 7), ANY],
        [pltpu.VMEM((ROWS, WIDE), F32), pltpu.VMEM((ROWS, BLOCK), BF16), pltpu.SemaphoreType.DMA],
        flops=2**20,
        moved=2**21,
    )


def times_transposed(x, w):
    return lax.dot_general(x, w, (((1,), (1,)), ((), ())), preferred_element_type=F32)


def backproject_first(place, parts, weights, chips):
    offsets = (0, -1, -2, -3)

    def body(place_ref, u_ref, g1_ref, g2_ref, g3_ref, w_ref, out_ref):
        for slot, x in enumerate((u_ref, g1_ref, g2_ref, g3_ref)):
            term = times_transposed(x[...], chunk_of_weights(w_ref, place_ref[0], offsets[slot], chips))
            out_ref[...] = term if slot == 0 else out_ref[...] + term

    heads = weights.shape[0]
    return call(
        body,
        [((ROWS, heads), F32)],
        (place, *parts, weights),
        [SMEM] + [VMEM] * 5,
        flops=8 * ROWS * heads * WIDE,
        moved=8 * heads * WIDE,
    )[0]


def backproject_rest(place, swapped, g4, start, weights, chips):
    offsets = (1, 2, 3, 4)

    def body(place_ref, h_ref, g4_ref, start_ref, w_ref, out_ref, facing, total):
        core = place_ref[0] % 2
        facing[pl.ds(pl.multiple_of(core * HALF, HALF), HALF)] = g4_ref[...]
        facing[pl.ds(pl.multiple_of((1 - core) * HALF, HALF), HALF)] = h_ref[3 * ROWS :]
        total[...] = start_ref[...]
        for slot in range(3):
            total[...] += times_transposed(
                h_ref[slot * ROWS : (slot + 1) * ROWS],
                chunk_of_weights(w_ref, place_ref[0], offsets[slot], chips),
            )
        last = times_transposed(facing[...], chunk_of_weights(w_ref, place_ref[0], offsets[3], chips))
        out_ref[...] = (total[...] + last).astype(BF16)

    heads = weights.shape[0]
    return call(
        body,
        [((ROWS, heads), BF16)],
        (place, swapped, g4, start, weights),
        [SMEM] + [VMEM] * 4,
        [
            pltpu.VMEM((ROWS, WIDE), BF16),
            pltpu.VMEM((ROWS, heads), F32),
        ],
        flops=8 * ROWS * heads * WIDE,
        moved=8 * heads * WIDE,
    )[0]


def on_device(weights, contexts, residual, plan, upstream):
    w_local, contexts, residual = weights[0], contexts[0], residual[0]
    at = lax.axis_index("tensor")
    place = at.astype(jnp.int32)[None]
    chips = lax.axis_size("tensor") // 2
    first = at % 2 == 0

    mate = core_swap(upstream[0])
    pair = jnp.where(
        first, jnp.concatenate([upstream[0], mate], 1), jnp.concatenate([mate, upstream[0]], 1)
    )
    g1 = next_section(pair, -1, 1)
    g2 = next_section(pair, -1, 2)
    g0 = next_section(pair, -1)

    send, keep, own = project(place, plan, contexts, w_local, chips)
    arrived = core_swap(send)
    q3, q4, q1 = encode_far(place, keep, arrived)
    g2, _ = lax.optimization_barrier((g2, q3))
    q3, q4 = split_shift(q3, 1), split_shift(q4, 2)
    q1 = split_shift(q1, 1)
    q2 = split_shift(encode_two(place, keep, arrived, q3, q4), 2)

    g3 = split_shift(g2, 1)
    g4 = split_shift(jnp.where(first, g2[:HALF], g2[HALF:]), 2)
    g1, g0 = lax.optimization_barrier((g1, g0))
    early = backproject_first(place, (g0, g1, g2, g3), w_local, chips)
    swapped = core_swap(jnp.concatenate([g1, g2, g3, g4], 0))

    after, _ = lax.optimization_barrier((place, early))
    send, part = gather_home(after, plan, q1, q2, own, arrived, residual)
    hidden = (part + core_swap(send)).astype(BF16)
    boundary = next_section(hidden, 1)
    gradient = backproject_rest(place, swapped, g4, early, w_local, chips)
    boundary, gradient = lax.optimization_barrier((boundary, gradient))
    return (boundary[None], gradient[None])


def solution(mesh):
    return jax.shard_map(
        on_device,
        mesh=mesh,
        in_specs=(
            P("section", "tensor", None),
            P("section", None, "dp", "tensor"),
            P("section", None, "dp", "tensor"),
            P("section"),
            P("section", "dp", "tensor"),
        ),
        out_specs=(P("section", "dp", "tensor"), P("section", "dp", "tensor")),
        check_vma=False,
    )
```

time: 158 us -> 90.6 us (0.57)
  waiting for transfers between devices: 97.6 us -> 25.9 us
  starting transfers between devices: 11.1 us -> 47.8 us
  blocking collectives: 17.6 us -> 0 us
  matrix products: 14.2 us -> 0 us
  between operations: 14.8 us -> 1.56 us
  Pallas kernels: 0 us -> 12.4 us
    reduce_scatter x1 -> x0, waiting for transfers between devices: 68.7 us -> none  [on_device(): lax.psum_scatter(jnp.dot(context, w_local, preferred_element_type=jnp.flo...]
    ppermute x2 -> x14, starting transfers between devices: 11 us -> 47.8 us  [the longest x4 26.2 us: core_swap(): return lax.ppermute(value, 'tensor', [(i, i ^ 1) for i in range(peers)])]
    all_gather x1 -> x0, waiting for transfers between devices: 27 us -> none  [on_device(): lax.all_gather(incoming, 'tensor', axis=1, tiled=True)]
    ppermute x2 -> x14, waiting for transfers between devices: 1.93 us -> 25.9 us  [the longest x4 12.4 us: next_section(): return lax.ppermute(value, ('section', 'tensor'), pairs)]
    all_to_all x1 -> x0, blocking collectives: 17.6 us -> none  [on_device(): lax.all_to_all(summed, 'tensor', split_axis=1, concat_axis=0, tiled=True)]
    dot_general x2 -> x0, matrix products: 14.2 us -> none  [the longest x1 7.6 us: on_device(): lax.dot_general(lax.all_gather(incoming, 'tensor', axis=1, tiled=True), w...]
    pallas_call x0 -> x6, Pallas kernels: none -> 12.4 us  [call(): pl.pallas_call(body, grid=(1,), in_specs=specs, out_specs=[VMEM] * len(ou...]
  transfers between devices with their start and end apart: 4 -> 14, of which waited for: 3 -> 8; matrix products, arithmetic and copies ran while one was open for 5% -> 0% of each run, Pallas kernels for 0% -> 5%
where the time goes in v2:
time: 90.6 us; the launch traced here: 90 us
  starting transfers between devices  47.8 us (53%)
  waiting for transfers between devices  25.9 us (29%)
  Pallas kernels  12.4 us (14%)
  local copies, waits for them, and re-layouts  2.17 us (2%)
  between operations  1.56 us (2%)
    ppermute x4, starting transfers between devices, core_swap(): return lax.ppermute(value, 'tensor', [(i, i ^ 1) for i in range(peers)])  26.2 us
    ppermute x6, starting transfers between devices, split_shift(): return lax.ppermute(value, 'tensor', pairs)  13.9 us
    ppermute x4, waiting for transfers between devices, next_section(): return lax.ppermute(value, ('section', 'tensor'), pairs)  12.4 us
    pallas_call x6, Pallas kernels, call(): pl.pallas_call(body, grid=(1,), in_specs=specs, out_specs=[VMEM] * len(ou...  12.4 us
    ppermute x6, waiting for transfers between devices, split_shift(): return lax.ppermute(value, 'tensor', pairs)  10.3 us
    ppermute x4, starting transfers between devices, next_section(): return lax.ppermute(value, ('section', 'tensor'), pairs)  7.68 us
    ppermute x4, waiting for transfers between devices, core_swap(): return lax.ppermute(value, 'tensor', [(i, i ^ 1) for i in range(peers)])  3.15 us
    unnamed x11, local copies, waits for them, and re-layouts  2.17 us
  transfers between devices with their start and end apart: 14, of which 8 were waited for; matrix products, arithmetic and copies ran while one was open for 0% of the time, Pallas kernels for 5%

profile of v2, /device:TPU:1, one launch (start us, length us, event | category | flops | bytes accessed | tf_op | source)
XLA Modules:
  0.0 90.0 jit_solution(1732367615880134914)
XLA Ops:
  1.3 7.5 %shard_map.68 = (f32[512,1024]{1,0:T(8,128)}, f32[448,1024]{1,0:T(8,128)}, f32[64,1024]{1,0:T(8,128)}) custom-call(s32[1]{0:T(128)} %bitcast.place_ref, s32[1]{0:T(128)S(6)} %copy.8.plan_ref, bf16[4,128,512]{2,1,0:T(8,128)(2,1)} %bitcast.11, bf16[512,8192]{1,0:T(8,128)(2,1)} %bitcast.7), custom_call_target="tpu_custom_call" | custom-call | flops 1073741824 | bytes 8388608 | tf_op jit(solution)/shard_map/pallas_call | solution.py:46
  8.8 16.1 %collective-permute-start.4 = (f32[512,1024]{1,0:T(8,128)}, f32[512,1024]{1,0:T(8,128)S(1)}, u32[]{:S(2)}, u32[]{:S(2)}) collective-permute-start(f32[512,1024]{1,0:T(8,128)} %get-tuple-element.19), channel_id=1, source_target_pairs={{0,4},{4,0},{8,12},{12,8},{16,20},{20,16},{24,28},{28,24},{32,36},... | collective-permute-start | bytes 6291464 | tf_op jit(solution)/shard_map/ppermute | solution.py:32
  24.8 1.9 %collective-permute-start = (bf16[128,512]{1,0:T(8,128)(2,1)S(1)}, bf16[128,512]{1,0:T(8,128)(2,1)S(1)}, u32[]{:S(2)}, u32[]{:S(2)}) collective-permute-start(bf16[128,512]{1,0:T(8,128)(2,1)S(1)} %bitcast.13), channel_id=1, source_target_pairs={{0,4},{4,0},{8,12},{12,8},{16,20},{20,16},{24,28},{28,24},{32,36},... | collective-permute-start | bytes 393224 | tf_op jit(solution)/shard_map/ppermute | solution.py:32
  26.8 2.0 %collective-permute-done = bf16[128,512]{1,0:T(8,128)(2,1)S(1)} collective-permute-done((bf16[128,512]{1,0:T(8,128)(2,1)S(1)}, bf16[128,512]{1,0:T(8,128)(2,1)S(1)}, u32[]{:S(2)}, u32[]{:S(2)}) %collective-permute-start) | collective-permute-done | bytes 131104 | tf_op jit(solution)/shard_map/ppermute | solution.py:32
  28.8 0.1 maximum_select_fusion
  28.9 1.9 %collective-permute-start.3 = (bf16[128,1024]{1,0:T(8,128)(2,1)S(1)}, bf16[128,1024]{1,0:T(8,128)(2,1)S(1)}, u32[]{:S(2)}, u32[]{:S(2)}) collective-permute-start(bf16[128,1024]{1,0:T(8,128)(2,1)S(1)} %maximum_select_fusion), channel_id=1, source_target_pairs={{0,976},{4,1012},{8,984},{12,1020},{16,992},{20,964},{24,1000},{28... | collective-permute-start | bytes 786440 | tf_op jit(solution)/shard_map/ppermute | solution.py:42
  30.8 1.9 %collective-permute-start.2 = (bf16[128,1024]{1,0:T(8,128)(2,1)S(1)}, bf16[128,1024]{1,0:T(8,128)(2,1)S(1)}, u32[]{:S(2)}, u32[]{:S(2)}) collective-permute-start(bf16[128,1024]{1,0:T(8,128)(2,1)S(1)} %maximum_select_fusion), channel_id=1, source_target_pairs={{0,960},{4,964},{8,968},{12,972},{16,976},{20,980},{24,984},{28,98... | collective-permute-start | bytes 786440 | tf_op jit(solution)/shard_map/ppermute | solution.py:42
  32.7 1.9 %collective-permute-start.1 = (bf16[128,1024]{1,0:T(8,128)(2,1)S(1)}, bf16[128,1024]{1,0:T(8,128)(2,1)S(1)}, u32[]{:S(2)}, u32[]{:S(2)}) collective-permute-start(bf16[128,1024]{1,0:T(8,128)(2,1)S(1)} %maximum_select_fusion), channel_id=1, source_target_pairs={{0,968},{4,1020},{8,976},{12,964},{16,984},{20,972},{24,992},{28,9... | collective-permute-start | bytes 786440 | tf_op jit(solution)/shard_map/ppermute | solution.py:42
  34.7 1.5 %copy-done.1 = f32[448,1024]{1,0:T(8,128)S(1)} copy-done((f32[448,1024]{1,0:T(8,128)S(1)}, f32[448,1024]{1,0:T(8,128)}, u32[]{:S(2)}) %copy-start.1) | copy-done | bytes 1835032
  36.2 0.3 shard_map.69
  36.5 4.3 %collective-permute-done.3.g2_ref = bf16[128,1024]{1,0:T(8,128)(2,1)S(1)} collective-permute-done((bf16[128,1024]{1,0:T(8,128)(2,1)S(1)}, bf16[128,1024]{1,0:T(8,128)(2,1)S(1)}, u32[]{:S(2)}, u32[]{:S(2)}) %collective-permute-start.3) | collective-permute-done | bytes 262176 | tf_op jit(solution)/shard_map/ppermute | solution.py:42
  40.8 1.9 %collective-permute-start.5 = (bf16[128,1024]{1,0:T(8,128)(2,1)S(1)}, bf16[128,1024]{1,0:T(8,128)(2,1)S(1)}, u32[]{:S(2)}, u32[]{:S(2)}) collective-permute-start(bf16[128,1024]{1,0:T(8,128)(2,1)S(1)} %collective-permute-done.3.g2_ref), channel_id=1, source_target_pairs={{0,8},{4,60},{8,16},{12,4},{16,24},{20,12},{24,32},{28,20},{32,40}... | collective-permute-start | bytes 786440 | tf_op jit(solution)/shard_map/ppermute | solution.py:27
  42.7 1.9 %collective-permute-start.12 = (bf16[64,1024]{1,0:T(8,128)(2,1)S(1)}, bf16[64,1024]{1,0:T(8,128)(2,1)S(1)}, u32[]{:S(2)}, u32[]{:S(2)}) collective-permute-start(bf16[64,1024]{1,0:T(8,128)(2,1)S(1)} %slice_select_fusion), channel_id=1, source_target_pairs={{0,16},{4,52},{8,24},{12,60},{16,32},{20,4},{24,40},{28,12},{32,48... | collective-permute-start | bytes 393224 | tf_op jit(solution)/shard_map/ppermute | solution.py:27
  44.7 1.9 %collective-permute-start.7 = (s16[144,1024]{1,0:T(8,128)(2,1)S(1)}, s16[144,1024]{1,0:T(8,128)(2,1)S(1)}, u32[]{:S(2)}, u32[]{:S(2)}) collective-permute-start(s16[144,1024]{1,0:T(8,128)(2,1)S(1)} %get-tuple-element.20), channel_id=1, source_target_pairs={{0,8},{4,60},{8,16},{12,4},{16,24},{20,12},{24,32},{28,20},{32,40}... | collective-permute-start | bytes 884744 | tf_op jit(solution)/shard_map/ppermute | solution.py:27
  46.6 1.0 %collective-permute-done.1.g1_ref = bf16[128,1024]{1,0:T(8,128)(2,1)S(1)} collective-permute-done((bf16[128,1024]{1,0:T(8,128)(2,1)S(1)}, bf16[128,1024]{1,0:T(8,128)(2,1)S(1)}, u32[]{:S(2)}, u32[]{:S(2)}) %collective-permute-start.1) | collective-permute-done | bytes 262176 | tf_op jit(solution)/shard_map/ppermute | solution.py:42
  47.7 1.9 %collective-permute-start.8 = (s16[80,1024]{1,0:T(8,128)(2,1)S(1)}, s16[80,1024]{1,0:T(8,128)(2,1)S(1)}, u32[]{:S(2)}, u32[]{:S(2)}) collective-permute-start(s16[80,1024]{1,0:T(8,128)(2,1)S(1)} %get-tuple-element.24), channel_id=1, source_target_pairs={{0,16},{4,52},{8,24},{12,60},{16,32},{20,4},{24,40},{28,12},{32,48... | collective-permute-start | bytes 491528 | tf_op jit(solution)/shard_map/ppermute | solution.py:27
  49.6 2.2 %collective-permute-done.12.g4_ref = bf16[64,1024]{1,0:T(8,128)(2,1)S(1)} collective-permute-done((bf16[64,1024]{1,0:T(8,128)(2,1)S(1)}, bf16[64,1024]{1,0:T(8,128)(2,1)S(1)}, u32[]{:S(2)}, u32[]{:S(2)}) %collective-permute-start.12) | collective-permute-done | bytes 131104 | tf_op jit(solution)/shard_map/ppermute | solution.py:27
  51.7 0.1 pad_maximum_fusion
  51.8 4.6 %collective-permute-start.13 = (bf16[448,1024]{1,0:T(8,128)(2,1)S(1)}, bf16[448,1024]{1,0:T(8,128)(2,1)S(1)}, u32[]{:S(2)}, u32[]{:S(2)}) collective-permute-start(bf16[448,1024]{1,0:T(8,128)(2,1)S(1)} %pad_maximum_fusion), channel_id=1, source_target_pairs={{0,4},{4,0},{8,12},{12,8},{16,20},{20,16},{24,28},{28,24},{32,36},... | collective-permute-start | bytes 2752520 | tf_op jit(solution)/shard_map/ppermute | solution.py:32
  56.4 3.6 %collective-permute-start.6 = (s16[144,1024]{1,0:T(8,128)(2,1)S(1)}, s16[144,1024]{1,0:T(8,128)(2,1)S(1)}, u32[]{:S(2)}, u32[]{:S(2)}) collective-permute-start(s16[144,1024]{1,0:T(8,128)(2,1)S(1)} %get-tuple-element.23), channel_id=1, source_target_pairs={{0,8},{4,60},{8,16},{12,4},{16,24},{20,12},{24,32},{28,20},{32,40}... | collective-permute-start | bytes 884744 | tf_op jit(solution)/shard_map/ppermute | solution.py:27
  60.0 0.4 shard_map.71
  60.4 2.7 %collective-permute-start.9 = (s16[144,1024]{1,0:T(8,128)(2,1)S(1)}, s16[144,1024]{1,0:T(8,128)(2,1)S(1)}, u32[]{:S(2)}, u32[]{:S(2)}) collective-permute-start(s16[144,1024]{1,0:T(8,128)(2,1)S(1)} %shard_map.71), channel_id=1, source_target_pairs={{0,16},{4,52},{8,24},{12,60},{16,32},{20,4},{24,40},{28,12},{32,48... | collective-permute-start | bytes 884744 | tf_op jit(solution)/shard_map/ppermute | solution.py:27
  63.2 1.5 %shard_map.70.start_ref = f32[128,512]{1,0:T(8,128)S(1)} custom-call(s32[1]{0:T(128)} %bitcast.place_ref, bf16[128,1024]{1,0:T(8,128)(2,1)S(1)} %collective-permute-done.2.u_ref, bf16[128,1024]{1,0:T(8,128)(2,1)S(1)} %collective-permute-done.1.g1_ref, bf16[128,1024]{1,0:T(8,128)(2,1)S(1)} %collective-permute-done.3.g2_ref, ...), custom_call_target="tpu_custom_call" | custom-call | flops 536870912 | bytes 4194304 | tf_op jit(solution)/shard_map/pallas_call | solution.py:46
  64.7 0.6 collective-permute-done.6.q1_ref
  65.3 7.6 %collective-permute-done.9.q2_ref = s16[144,1024]{1,0:T(8,128)(2,1)S(1)} collective-permute-done((s16[144,1024]{1,0:T(8,128)(2,1)S(1)}, s16[144,1024]{1,0:T(8,128)(2,1)S(1)}, u32[]{:S(2)}, u32[]{:S(2)}) %collective-permute-start.9) | collective-permute-done | bytes 294944 | tf_op jit(solution)/shard_map/ppermute | solution.py:27
  72.9 0.5 shard_map.72
  73.4 3.6 %collective-permute-start.10 = (f32[128,512]{1,0:T(8,128)S(1)}, f32[128,512]{1,0:T(8,128)S(1)}, u32[]{:S(2)}, u32[]{:S(2)}) collective-permute-start(f32[128,512]{1,0:T(8,128)S(1)} %get-tuple-element.27), channel_id=1, source_target_pairs={{0,4},{4,0},{8,12},{12,8},{16,20},{20,16},{24,28},{28,24},{32,36},... | collective-permute-start | bytes 786440 | tf_op jit(solution)/shard_map/ppermute | solution.py:32
  77.0 1.1 %collective-permute-done.10 = f32[128,512]{1,0:T(8,128)S(1)} collective-permute-done((f32[128,512]{1,0:T(8,128)S(1)}, f32[128,512]{1,0:T(8,128)S(1)}, u32[]{:S(2)}, u32[]{:S(2)}) %collective-permute-start.10) | collective-permute-done | bytes 262176 | tf_op jit(solution)/shard_map/ppermute | solution.py:32
  78.2 1.9 %collective-permute-start.11 = (bf16[128,512]{1,0:T(8,128)(2,1)S(1)}, bf16[128,512]{1,0:T(8,128)(2,1)S(1)}, u32[]{:S(2)}, u32[]{:S(2)}) collective-permute-start(bf16[128,512]{1,0:T(8,128)(2,1)S(1)} %add_convert_fusion), channel_id=1, source_target_pairs={{0,64},{4,68},{8,72},{12,76},{16,80},{20,84},{24,88},{28,92},{32,9... | collective-permute-start | bytes 393224 | tf_op jit(solution)/shard_map/ppermute | solution.py:42
  80.1 2.2 %shard_map.73 = bf16[128,512]{1,0:T(8,128)(2,1)} custom-call(s32[1]{0:T(128)} %bitcast.place_ref, bf16[448,1024]{1,0:T(8,128)(2,1)S(1)} %collective-permute-done.13.h_ref, bf16[64,1024]{1,0:T(8,128)(2,1)S(1)} %collective-permute-done.12.g4_ref, f32[128,512]{1,0:T(8,128)S(1)} %shard_map.70.start_ref, bf16[512,8192]{1,0:T(8,128)(2,1)S(1)} %bitcast.9), custom_call_target="tpu_custom_call" | custom-call | flops 536870912 | bytes 4194304 | tf_op jit(solution)/shard_map/pallas_call | solution.py:46
  82.3 7.0 %collective-permute-done.11 = bf16[128,512]{1,0:T(8,128)(2,1)S(1)} collective-permute-done((bf16[128,512]{1,0:T(8,128)(2,1)S(1)}, bf16[128,512]{1,0:T(8,128)(2,1)S(1)}, u32[]{:S(2)}, u32[]{:S(2)}) %collective-permute-start.11) | collective-permute-done | bytes 131104 | tf_op jit(solution)/shard_map/ppermute | solution.py:42
  89.4 0.7 copy.9
  (17 shorter events, 0.1 us)
Async XLA Ops:
  1.3 23.6 %copy-start.4 = (bf16[1,128,512]{2,1,0:T(8,128)(2,1)S(1)}, bf16[1,128,512]{2,1,0:T(8,128)(2,1)}, u32[]{:S(2)}) copy-start(bf16[1,128,512]{2,1,0:T(8,128)(2,1)} %param.9) | copy-start | bytes 393220
  8.8 25.9 %collective-permute-start.4 = (f32[512,1024]{1,0:T(8,128)}, f32[512,1024]{1,0:T(8,128)S(1)}, u32[]{:S(2)}, u32[]{:S(2)}) collective-permute-start(f32[512,1024]{1,0:T(8,128)} %get-tuple-element.19), channel_id=1, source_target_pairs={{0,4},{4,0},{8,12},{12,8},{16,20},{20,16},{24,28},{28,24},{32,36},... | collective-permute-start | bytes 6291464 | tf_op jit(solution)/shard_map/ppermute | solution.py:32
  24.8 3.9 %collective-permute-start = (bf16[128,512]{1,0:T(8,128)(2,1)S(1)}, bf16[128,512]{1,0:T(8,128)(2,1)S(1)}, u32[]{:S(2)}, u32[]{:S(2)}) collective-permute-start(bf16[128,512]{1,0:T(8,128)(2,1)S(1)} %bitcast.13), channel_id=1, source_target_pairs={{0,4},{4,0},{8,12},{12,8},{16,20},{20,16},{24,28},{28,24},{32,36},... | collective-permute-start | bytes 393224 | tf_op jit(solution)/shard_map/ppermute | solution.py:32
  28.9 11.9 %collective-permute-start.3 = (bf16[128,1024]{1,0:T(8,128)(2,1)S(1)}, bf16[128,1024]{1,0:T(8,128)(2,1)S(1)}, u32[]{:S(2)}, u32[]{:S(2)}) collective-permute-start(bf16[128,1024]{1,0:T(8,128)(2,1)S(1)} %maximum_select_fusion), channel_id=1, source_target_pairs={{0,976},{4,1012},{8,984},{12,1020},{16,992},{20,964},{24,1000},{28... | collective-permute-start | bytes 786440 | tf_op jit(solution)/shard_map/ppermute | solution.py:42
  30.8 15.8 %collective-permute-start.2 = (bf16[128,1024]{1,0:T(8,128)(2,1)S(1)}, bf16[128,1024]{1,0:T(8,128)(2,1)S(1)}, u32[]{:S(2)}, u32[]{:S(2)}) collective-permute-start(bf16[128,1024]{1,0:T(8,128)(2,1)S(1)} %maximum_select_fusion), channel_id=1, source_target_pairs={{0,960},{4,964},{8,968},{12,972},{16,976},{20,980},{24,984},{28,98... | collective-permute-start | bytes 786440 | tf_op jit(solution)/shard_map/ppermute | solution.py:42
  32.7 14.9 %collective-permute-start.1 = (bf16[128,1024]{1,0:T(8,128)(2,1)S(1)}, bf16[128,1024]{1,0:T(8,128)(2,1)S(1)}, u32[]{:S(2)}, u32[]{:S(2)}) collective-permute-start(bf16[128,1024]{1,0:T(8,128)(2,1)S(1)} %maximum_select_fusion), channel_id=1, source_target_pairs={{0,968},{4,1020},{8,976},{12,964},{16,984},{20,972},{24,992},{28,9... | collective-permute-start | bytes 786440 | tf_op jit(solution)/shard_map/ppermute | solution.py:42
  34.7 1.5 %copy-start.1 = (f32[448,1024]{1,0:T(8,128)S(1)}, f32[448,1024]{1,0:T(8,128)}, u32[]{:S(2)}) copy-start(f32[448,1024]{1,0:T(8,128)} %get-tuple-element.18.keep_ref) | copy-start | bytes 5505028
  36.2 27.0 %copy-start = (bf16[1,512,8192]{2,1,0:T(8,128)(2,1)S(1)}, bf16[1,512,8192]{2,1,0:T(8,128)(2,1)}, u32[]{:S(2)}) copy-start(bf16[1,512,8192]{2,1,0:T(8,128)(2,1)} %param.5) | copy-start | bytes 25165828
  40.8 10.9 %collective-permute-start.5 = (bf16[128,1024]{1,0:T(8,128)(2,1)S(1)}, bf16[128,1024]{1,0:T(8,128)(2,1)S(1)}, u32[]{:S(2)}, u32[]{:S(2)}) collective-permute-start(bf16[128,1024]{1,0:T(8,128)(2,1)S(1)} %collective-permute-done.3.g2_ref), channel_id=1, source_target_pairs={{0,8},{4,60},{8,16},{12,4},{16,24},{20,12},{24,32},{28,20},{32,40}... | collective-permute-start | bytes 786440 | tf_op jit(solution)/shard_map/ppermute | solution.py:27
  42.7 9.0 %collective-permute-start.12 = (bf16[64,1024]{1,0:T(8,128)(2,1)S(1)}, bf16[64,1024]{1,0:T(8,128)(2,1)S(1)}, u32[]{:S(2)}, u32[]{:S(2)}) collective-permute-start(bf16[64,1024]{1,0:T(8,128)(2,1)S(1)} %slice_select_fusion), channel_id=1, source_target_pairs={{0,16},{4,52},{8,24},{12,60},{16,32},{20,4},{24,40},{28,12},{32,48... | collective-permute-start | bytes 393224 | tf_op jit(solution)/shard_map/ppermute | solution.py:27
  44.7 15.3 %collective-permute-start.7 = (s16[144,1024]{1,0:T(8,128)(2,1)S(1)}, s16[144,1024]{1,0:T(8,128)(2,1)S(1)}, u32[]{:S(2)}, u32[]{:S(2)}) collective-permute-start(s16[144,1024]{1,0:T(8,128)(2,1)S(1)} %get-tuple-element.20), channel_id=1, source_target_pairs={{0,8},{4,60},{8,16},{12,4},{16,24},{20,12},{24,32},{28,20},{32,40}... | collective-permute-start | bytes 884744 | tf_op jit(solution)/shard_map/ppermute | solution.py:27
  47.7 12.4 %collective-permute-start.8 = (s16[80,1024]{1,0:T(8,128)(2,1)S(1)}, s16[80,1024]{1,0:T(8,128)(2,1)S(1)}, u32[]{:S(2)}, u32[]{:S(2)}) collective-permute-start(s16[80,1024]{1,0:T(8,128)(2,1)S(1)} %get-tuple-element.24), channel_id=1, source_target_pairs={{0,16},{4,52},{8,24},{12,60},{16,32},{20,4},{24,40},{28,12},{32,48... | collective-permute-start | bytes 491528 | tf_op jit(solution)/shard_map/ppermute | solution.py:27
  51.8 28.3 %collective-permute-start.13 = (bf16[448,1024]{1,0:T(8,128)(2,1)S(1)}, bf16[448,1024]{1,0:T(8,128)(2,1)S(1)}, u32[]{:S(2)}, u32[]{:S(2)}) collective-permute-start(bf16[448,1024]{1,0:T(8,128)(2,1)S(1)} %pad_maximum_fusion), channel_id=1, source_target_pairs={{0,4},{4,0},{8,12},{12,8},{16,20},{20,16},{24,28},{28,24},{32,36},... | collective-permute-start | bytes 2752520 | tf_op jit(solution)/shard_map/ppermute | solution.py:32
  56.4 8.9 %collective-permute-start.6 = (s16[144,1024]{1,0:T(8,128)(2,1)S(1)}, s16[144,1024]{1,0:T(8,128)(2,1)S(1)}, u32[]{:S(2)}, u32[]{:S(2)}) collective-permute-start(s16[144,1024]{1,0:T(8,128)(2,1)S(1)} %get-tuple-element.23), channel_id=1, source_target_pairs={{0,8},{4,60},{8,16},{12,4},{16,24},{20,12},{24,32},{28,20},{32,40}... | collective-permute-start | bytes 884744 | tf_op jit(solution)/shard_map/ppermute | solution.py:27
  60.4 12.5 %copy-start.2 = (bf16[1,4,128,512]{3,2,1,0:T(8,128)(2,1)S(1)}, bf16[1,4,128,512]{3,2,1,0:T(8,128)(2,1)}, u32[]{:S(2)}) copy-start(bf16[1,4,128,512]{3,2,1,0:T(8,128)(2,1)} %param.7) | copy-start | bytes 1572868
  60.4 12.4 %copy-start.3 = (f32[64,1024]{1,0:T(8,128)S(1)}, f32[64,1024]{1,0:T(8,128)}, u32[]{:S(2)}) copy-start(f32[64,1024]{1,0:T(8,128)} %get-tuple-element.25.own_ref) | copy-start | bytes 786436
  60.4 12.4 %collective-permute-start.9 = (s16[144,1024]{1,0:T(8,128)(2,1)S(1)}, s16[144,1024]{1,0:T(8,128)(2,1)S(1)}, u32[]{:S(2)}, u32[]{:S(2)}) collective-permute-start(s16[144,1024]{1,0:T(8,128)(2,1)S(1)} %shard_map.71), channel_id=1, source_target_pairs={{0,16},{4,52},{8,24},{12,60},{16,32},{20,4},{24,40},{28,12},{32,48... | collective-permute-start | bytes 884744 | tf_op jit(solution)/shard_map/ppermute | solution.py:27
  73.4 4.8 %collective-permute-start.10 = (f32[128,512]{1,0:T(8,128)S(1)}, f32[128,512]{1,0:T(8,128)S(1)}, u32[]{:S(2)}, u32[]{:S(2)}) collective-permute-start(f32[128,512]{1,0:T(8,128)S(1)} %get-tuple-element.27), channel_id=1, source_target_pairs={{0,4},{4,0},{8,12},{12,8},{16,20},{20,16},{24,28},{28,24},{32,36},... | collective-permute-start | bytes 786440 | tf_op jit(solution)/shard_map/ppermute | solution.py:32
  78.2 11.2 %collective-permute-start.11 = (bf16[128,512]{1,0:T(8,128)(2,1)S(1)}, bf16[128,512]{1,0:T(8,128)(2,1)S(1)}, u32[]{:S(2)}, u32[]{:S(2)}) collective-permute-start(bf16[128,512]{1,0:T(8,128)(2,1)S(1)} %add_convert_fusion), channel_id=1, source_target_pairs={{0,64},{4,68},{8,72},{12,76},{16,80},{20,84},{24,88},{28,92},{32,9... | collective-permute-start | bytes 393224 | tf_op jit(solution)/shard_map/ppermute | solution.py:42

commit v3 on v2

--- a/solution.py
+++ b/solution.py
@@ -42,7 +42,7 @@
     return lax.ppermute(value, ("section", "tensor"), pairs)
 
 
-def call(body, outs, ins, specs, scratch=(), flops=0, moved=0, vmem=24):
+def call(body, outs, ins, specs, scratch=(), vmem=24):
     return pl.pallas_call(
         body,
         grid=(1,),
@@ -51,7 +51,7 @@
         out_shape=[jax.ShapeDtypeStruct(s, d) for s, d in outs],
         scratch_shapes=list(scratch),
         compiler_params=pltpu.CompilerParams(vmem_limit_bytes=vmem * 2**20),
-        cost_estimate=pl.CostEstimate(flops=flops, bytes_accessed=moved, transcendentals=0),
+        cost_estimate=pl.CostEstimate(flops=1, bytes_accessed=1, transcendentals=0),
     )(*ins)
 
 
@@ -133,54 +133,46 @@
             pltpu.SemaphoreType.DMA((8,)),
             pltpu.SemaphoreType.DMA,
         ],
-        flops=16 * ROWS * heads * WIDE,
-        moved=16 * heads * WIDE,
-        vmem=58,
-    )
-
-
-def encode_far(place, keep, arrived):
-    def body(place_ref, keep_ref, in_ref, q3_ref, q4_ref, q1_ref):
-        encode(keep_ref[:ROWS] + in_ref[:ROWS], q3_ref)
+        vmem=46,
+    )
+
+
+def encode_first(place, keep, arrived):
+    def body(place_ref, keep_ref, in_ref, q31_ref, q4_ref):
+        coded = ROWS + 16
+        encode(keep_ref[:ROWS] + in_ref[:ROWS], q31_ref.at[:coded])
+        encode(keep_ref[2 * ROWS : 3 * ROWS] + in_ref[2 * ROWS : 3 * ROWS], q31_ref.at[coded:])
         encode(keep_ref[3 * ROWS :] + in_ref[3 * ROWS : 3 * ROWS + HALF], q4_ref)
-        encode(keep_ref[2 * ROWS : 3 * ROWS] + in_ref[2 * ROWS : 3 * ROWS], q1_ref)
-
-    return call(
-        body,
-        [((ROWS + 16, WIDE), CODE), ((HALF + 16, WIDE), CODE), ((ROWS + 16, WIDE), CODE)],
+
+    return call(
+        body,
+        [((2 * ROWS + 32, WIDE), CODE), ((HALF + 16, WIDE), CODE)],
         (place, keep, arrived),
         [SMEM, VMEM, VMEM],
-        flops=2**21,
-        moved=2**21,
-    )
-
-
-def encode_two(place, keep, arrived, q3, q4):
-    def body(place_ref, keep_ref, in_ref, q3_ref, q4_ref, q_ref, total):
-        mine = pl.multiple_of((place_ref[0] % 2) * HALF, HALF)
-        total[...] = keep_ref[...] + in_ref[...] + decode(q3_ref)
-        total[pl.ds(mine, HALF)] += decode(q4_ref)
-        encode(total[...], q_ref)
+    )
+
+
+def encode_two(keep, arrived, q31):
+    def body(keep_ref, in_ref, q3_ref, q_ref):
+        encode(keep_ref[...] + in_ref[...] + decode(q3_ref), q_ref)
 
     return call(
         body,
         [((ROWS + 16, WIDE), CODE)],
-        (place, keep, arrived, q3, q4),
-        [SMEM, rows_of(ROWS, 1), rows_of(ROWS, 1), VMEM, VMEM],
-        [pltpu.VMEM((ROWS, WIDE), F32)],
-        flops=2**20,
-        moved=2**21,
+        (keep, arrived, q31),
+        [rows_of(ROWS, 1), rows_of(ROWS, 1), rows_of(ROWS + 16, 0)],
     )[0]
 
 
-def gather_home(place, plan, q1, q2, own, arrived, residual):
-    def body(place_ref, plan_ref, q1_ref, q2_ref, own_ref, in_ref, res_ref, send_ref, part_ref, full, stream, sem):
+def gather_home(place, plan, q31, q2, q4, own, arrived, residual):
+    def body(place_ref, plan_ref, q1_ref, q2_ref, q4_ref, own_ref, in_ref, res_ref, send_ref, part_ref, full, stream, sem):
         fetch = pltpu.make_async_copy(res_ref.at[plan_ref[0]], stream, sem)
         fetch.start()
         core = place_ref[0] % 2
         mine = pl.multiple_of(core * BLOCK, BLOCK)
         theirs = pl.multiple_of((1 - core) * BLOCK, BLOCK)
         full[...] = decode(q1_ref) + decode(q2_ref)
+        full[pl.ds(pl.multiple_of(core * HALF, HALF), HALF)] += decode(q4_ref)
         send_ref[...] = full[:, pl.ds(theirs, BLOCK)]
         fetch.wait()
         for part, at in ((0, 0), (1, HALF)):
@@ -196,11 +188,9 @@
     return call(
         body,
         [((ROWS, BLOCK), F32)] * 2,
-        (place, plan, q1, q2, own, arrived, residual),
-        [SMEM, SMEM, VMEM, VMEM, VMEM, rows_of(HALF, 7), ANY],
+        (place, plan, q31, q2, q4, own, arrived, residual),
+        [SMEM, SMEM, rows_of(ROWS + 16, 1), VMEM, VMEM, VMEM, rows_of(HALF, 7), ANY],
         [pltpu.VMEM((ROWS, WIDE), F32), pltpu.VMEM((ROWS, BLOCK), BF16), pltpu.SemaphoreType.DMA],
-        flops=2**20,
-        moved=2**21,
     )
 
 
@@ -209,10 +199,10 @@
 
 
 def backproject_first(place, parts, weights, chips):
-    offsets = (0, -1, -2, -3)
-
-    def body(place_ref, u_ref, g1_ref, g2_ref, g3_ref, w_ref, out_ref):
-        for slot, x in enumerate((u_ref, g1_ref, g2_ref, g3_ref)):
+    offsets = (0, -1, -2)
+
+    def body(place_ref, u_ref, g1_ref, g2_ref, w_ref, out_ref):
+        for slot, x in enumerate((u_ref, g1_ref, g2_ref)):
             term = times_transposed(x[...], chunk_of_weights(w_ref, place_ref[0], offsets[slot], chips))
             out_ref[...] = term if slot == 0 else out_ref[...] + term
 
@@ -221,40 +211,33 @@
         body,
         [((ROWS, heads), F32)],
         (place, *parts, weights),
-        [SMEM] + [VMEM] * 5,
-        flops=8 * ROWS * heads * WIDE,
-        moved=8 * heads * WIDE,
+        [SMEM] + [VMEM] * 4,
     )[0]
 
 
-def backproject_rest(place, swapped, g4, start, weights, chips):
-    offsets = (1, 2, 3, 4)
-
-    def body(place_ref, h_ref, g4_ref, start_ref, w_ref, out_ref, facing, total):
+def backproject_rest(place, h1, h2, h34, g3, g4, start, weights, chips):
+    offsets = (1, 2, 3, -3, 4)
+
+    def body(place_ref, h1_ref, h2_ref, h34_ref, g3_ref, g4_ref, start_ref, w_ref, out_ref, facing, total):
         core = place_ref[0] % 2
         facing[pl.ds(pl.multiple_of(core * HALF, HALF), HALF)] = g4_ref[...]
-        facing[pl.ds(pl.multiple_of((1 - core) * HALF, HALF), HALF)] = h_ref[3 * ROWS :]
+        facing[pl.ds(pl.multiple_of((1 - core) * HALF, HALF), HALF)] = h34_ref[ROWS:]
         total[...] = start_ref[...]
-        for slot in range(3):
-            total[...] += times_transposed(
-                h_ref[slot * ROWS : (slot + 1) * ROWS],
-                chunk_of_weights(w_ref, place_ref[0], offsets[slot], chips),
-            )
-        last = times_transposed(facing[...], chunk_of_weights(w_ref, place_ref[0], offsets[3], chips))
+        for slot, x in enumerate((h1_ref, h2_ref, h34_ref.at[:ROWS], g3_ref)):
+            total[...] += times_transposed(x[...], chunk_of_weights(w_ref, place_ref[0], offsets[slot], chips))
+        last = times_transposed(facing[...], chunk_of_weights(w_ref, place_ref[0], offsets[4], chips))
         out_ref[...] = (total[...] + last).astype(BF16)
 
     heads = weights.shape[0]
     return call(
         body,
         [((ROWS, heads), BF16)],
-        (place, swapped, g4, start, weights),
-        [SMEM] + [VMEM] * 4,
+        (place, h1, h2, h34, g3, g4, start, weights),
+        [SMEM] + [VMEM] * 7,
         [
             pltpu.VMEM((ROWS, WIDE), BF16),
             pltpu.VMEM((ROWS, heads), F32),
         ],
-        flops=8 * ROWS * heads * WIDE,
-        moved=8 * heads * WIDE,
     )[0]
 
 
@@ -265,33 +248,34 @@
     chips = lax.axis_size("tensor") // 2
     first = at % 2 == 0
 
+    send, keep, own = project(place, plan, contexts, w_local, chips)
+    arrived = core_swap(send)
     mate = core_swap(upstream[0])
     pair = jnp.where(
         first, jnp.concatenate([upstream[0], mate], 1), jnp.concatenate([mate, upstream[0]], 1)
     )
+    after, pair = lax.optimization_barrier((place, pair))
+    q31, q4 = encode_first(after, keep, arrived)
+    q31, q4 = split_shift(q31, 1), split_shift(q4, 4)
+    q2 = split_shift(encode_two(keep, arrived, q31), 2)
+
     g1 = next_section(pair, -1, 1)
     g2 = next_section(pair, -1, 2)
-    g0 = next_section(pair, -1)
-
-    send, keep, own = project(place, plan, contexts, w_local, chips)
-    arrived = core_swap(send)
-    q3, q4, q1 = encode_far(place, keep, arrived)
-    g2, _ = lax.optimization_barrier((g2, q3))
-    q3, q4 = split_shift(q3, 1), split_shift(q4, 2)
-    q1 = split_shift(q1, 1)
-    q2 = split_shift(encode_two(place, keep, arrived, q3, q4), 2)
-
     g3 = split_shift(g2, 1)
     g4 = split_shift(jnp.where(first, g2[:HALF], g2[HALF:]), 2)
-    g1, g0 = lax.optimization_barrier((g1, g0))
-    early = backproject_first(place, (g0, g1, g2, g3), w_local, chips)
-    swapped = core_swap(jnp.concatenate([g1, g2, g3, g4], 0))
-
-    after, _ = lax.optimization_barrier((place, early))
-    send, part = gather_home(after, plan, q1, q2, own, arrived, residual)
+    g0 = next_section(pair, -1)
+    to_mate, q4 = lax.optimization_barrier((g1, q4))
+    h1 = core_swap(to_mate)
+    to_mate, g0 = lax.optimization_barrier((g2, g0))
+    h2 = core_swap(to_mate)
+    h34 = core_swap(jnp.concatenate([g3, g4], 0))
+    early = backproject_first(place, (g0, g1, g2), w_local, chips)
+
+    after, _, _, _ = lax.optimization_barrier((place, early, h1, h2))
+    send, part = gather_home(after, plan, q31, q2, q4, own, arrived, residual)
     hidden = (part + core_swap(send)).astype(BF16)
     boundary = next_section(hidden, 1)
-    gradient = backproject_rest(place, swapped, g4, early, w_local, chips)
+    gradient = backproject_rest(place, h1, h2, h34, g3, g4, early, w_local, chips)
     boundary, gradient = lax.optimization_barrier((boundary, gradient))
     return (boundary[None], gradient[None])
 

time: 90.6 us -> 86.1 us (0.950)
  waiting for transfers between devices: 25.9 us -> 12.3 us
  starting transfers between devices: 47.8 us -> 56.1 us
  local copies, waits for them, and re-layouts: 2.17 us -> 4.41 us
  Pallas kernels: 12.4 us -> 10.2 us
    ppermute x4, waiting for transfers between devices: 12.4 us -> 3.38 us  [next_section(): return lax.ppermute(value, ('section', 'tensor'), pairs)]
    ppermute x4 -> x6, starting transfers between devices: 26.2 us -> 33.3 us  [core_swap(): return lax.ppermute(value, 'tensor', [(i, i ^ 1) for i in range(peers)])]
    ppermute x6 -> x5, waiting for transfers between devices: 10.3 us -> 6.93 us  [split_shift(): return lax.ppermute(value, 'tensor', pairs)]
    ppermute x4, starting transfers between devices: 7.68 us -> 10.5 us  [next_section(): return lax.ppermute(value, ('section', 'tensor'), pairs)]
    unnamed x11 -> x13, local copies, waits for them, and re-layouts: 2.17 us -> 4.41 us
    pallas_call x6, Pallas kernels: 12.4 us -> 10.2 us  [call(): pl.pallas_call(body, grid=(1,), in_specs=specs, out_specs=[VMEM] * len(ou...]
    ppermute x6 -> x5, starting transfers between devices: 13.9 us -> 12.2 us  [split_shift(): return lax.ppermute(value, 'tensor', pairs)]
    ppermute x4 -> x6, waiting for transfers between devices: 3.15 us -> 2.01 us  [core_swap(): return lax.ppermute(value, 'tensor', [(i, i ^ 1) for i in range(peers)])]
  transfers between devices with their start and end apart: 14 -> 15, of which waited for: 8 -> 6; matrix products, arithmetic and copies ran while one was open for 0% -> 0% of each run, Pallas kernels for 5% -> 5%
where the time goes in v3:
time: 86.1 us; the launch traced here: 84.8 us
  starting transfers between devices  56.1 us (65%)
  waiting for transfers between devices  12.3 us (14%)
  Pallas kernels  10.2 us (12%)
  local copies, waits for them, and re-layouts  4.41 us (5%)
  between operations  1.6 us (2%)
    ppermute x6, starting transfers between devices, core_swap(): return lax.ppermute(value, 'tensor', [(i, i ^ 1) for i in range(peers)])  33.3 us
    ppermute x5, starting transfers between devices, split_shift(): return lax.ppermute(value, 'tensor', pairs)  12.2 us
    ppermute x4, starting transfers between devices, next_section(): return lax.ppermute(value, ('section', 'tensor'), pairs)  10.5 us
    pallas_call x6, Pallas kernels, call(): pl.pallas_call(body, grid=(1,), in_specs=specs, out_specs=[VMEM] * len(ou...  10.2 us
    ppermute x5, waiting for transfers between devices, split_shift(): return lax.ppermute(value, 'tensor', pairs)  6.93 us
    unnamed x13, local copies, waits for them, and re-layouts  4.41 us
    ppermute x4, waiting for transfers between devices, next_section(): return lax.ppermute(value, ('section', 'tensor'), pairs)  3.38 us
    ppermute x6, waiting for transfers between devices, core_swap(): return lax.ppermute(value, 'tensor', [(i, i ^ 1) for i in range(peers)])  2.01 us
  transfers between devices with their start and end apart: 15, of which 6 were waited for; matrix products, arithmetic and copies ran while one was open for 0% of the time, Pallas kernels for 5%

profile of v3, /device:TPU:1, one launch (start us, length us, event | category | flops | bytes accessed | tf_op | source)
XLA Modules:
  0.0 84.8 jit_solution(15037176532029915085)
XLA Ops:
  1.3 1.0 %copy-done.3 = bf16[1,4,128,512]{3,2,1,0:T(8,128)(2,1)S(1)} copy-done((bf16[1,4,128,512]{3,2,1,0:T(8,128)(2,1)S(1)}, bf16[1,4,128,512]{3,2,1,0:T(8,128)(2,1)}, u32[]{:S(2)}) %copy-start.3) | copy-done | bytes 524312
  2.3 5.4 %shard_map.69 = (f32[512,1024]{1,0:T(8,128)}, f32[448,1024]{1,0:T(8,128)S(1)}, f32[64,1024]{1,0:T(8,128)S(1)}) custom-call(s32[1]{0:T(128)} %bitcast.place_ref, s32[1]{0:T(128)S(6)} %copy.8.plan_ref, bf16[4,128,512]{2,1,0:T(8,128)(2,1)S(1)} %bitcast.10, bf16[512,8192]{1,0:T(8,128)(2,1)} %bitcast.7), custom_call_target="tpu_custom_call" | custom-call | flops 1 | bytes 1 | tf_op jit(solution)/shard_map/pallas_call | solution.py:46
  7.8 1.2 %copy-done.1 = f32[448,1024]{1,0:T(8,128)} copy-done((f32[448,1024]{1,0:T(8,128)}, f32[448,1024]{1,0:T(8,128)S(1)}, u32[]{:S(2)}) %copy-start.1) | copy-done | bytes 1835032
  9.0 16.0 %collective-permute-start.4 = (f32[512,1024]{1,0:T(8,128)}, f32[512,1024]{1,0:T(8,128)S(1)}, u32[]{:S(2)}, u32[]{:S(2)}) collective-permute-start(f32[512,1024]{1,0:T(8,128)} %get-tuple-element.22), channel_id=1, source_target_pairs={{0,4},{4,0},{8,12},{12,8},{16,20},{20,16},{24,28},{28,24},{32,36},... | collective-permute-start | bytes 6291464 | tf_op jit(solution)/shard_map/ppermute | solution.py:32
  25.1 1.9 %collective-permute-start = (bf16[128,512]{1,0:T(8,128)(2,1)S(1)}, bf16[128,512]{1,0:T(8,128)(2,1)S(1)}, u32[]{:S(2)}, u32[]{:S(2)}) collective-permute-start(bf16[128,512]{1,0:T(8,128)(2,1)S(1)} %bitcast.13), channel_id=1, source_target_pairs={{0,4},{4,0},{8,12},{12,8},{16,20},{20,16},{24,28},{28,24},{32,36},... | collective-permute-start | bytes 393224 | tf_op jit(solution)/shard_map/ppermute | solution.py:32
  27.0 2.0 %collective-permute-done = bf16[128,512]{1,0:T(8,128)(2,1)S(1)} collective-permute-done((bf16[128,512]{1,0:T(8,128)(2,1)S(1)}, bf16[128,512]{1,0:T(8,128)(2,1)S(1)}, u32[]{:S(2)}, u32[]{:S(2)}) %collective-permute-start) | collective-permute-done | bytes 131104 | tf_op jit(solution)/shard_map/ppermute | solution.py:32
  29.0 0.1 maximum_select_fusion
  29.1 1.5 %copy-done.2 = f32[448,1024]{1,0:T(8,128)S(1)} copy-done((f32[448,1024]{1,0:T(8,128)S(1)}, f32[448,1024]{1,0:T(8,128)}, u32[]{:S(2)}) %copy-start.2) | copy-done | bytes 1835032
  30.6 0.3 shard_map.70
  30.9 2.3 %collective-permute-start.8 = (s16[288,1024]{1,0:T(8,128)(2,1)S(1)}, s16[288,1024]{1,0:T(8,128)(2,1)S(1)}, u32[]{:S(2)}, u32[]{:S(2)}) collective-permute-start(s16[288,1024]{1,0:T(8,128)(2,1)S(1)} %get-tuple-element.27), channel_id=1, source_target_pairs={{0,8},{4,60},{8,16},{12,4},{16,24},{20,12},{24,32},{28,20},{32,40}... | collective-permute-start | bytes 1769480 | tf_op jit(solution)/shard_map/ppermute | solution.py:27
  33.2 1.9 %collective-permute-start.1 = (bf16[128,1024]{1,0:T(8,128)(2,1)S(1)}, bf16[128,1024]{1,0:T(8,128)(2,1)S(1)}, u32[]{:S(2)}, u32[]{:S(2)}) collective-permute-start(bf16[128,1024]{1,0:T(8,128)(2,1)S(1)} %maximum_select_fusion), channel_id=1, source_target_pairs={{0,976},{4,1012},{8,984},{12,1020},{16,992},{20,964},{24,1000},{28... | collective-permute-start | bytes 786440 | tf_op jit(solution)/shard_map/ppermute | solution.py:42
  35.2 1.9 %collective-permute-start.2 = (bf16[128,1024]{1,0:T(8,128)(2,1)S(1)}, bf16[128,1024]{1,0:T(8,128)(2,1)S(1)}, u32[]{:S(2)}, u32[]{:S(2)}) collective-permute-start(bf16[128,1024]{1,0:T(8,128)(2,1)S(1)} %maximum_select_fusion), channel_id=1, source_target_pairs={{0,960},{4,964},{8,968},{12,972},{16,976},{20,980},{24,984},{28,98... | collective-permute-start | bytes 786440 | tf_op jit(solution)/shard_map/ppermute | solution.py:42
  37.1 2.7 %collective-permute-start.3 = (bf16[128,1024]{1,0:T(8,128)(2,1)S(1)}, bf16[128,1024]{1,0:T(8,128)(2,1)S(1)}, u32[]{:S(2)}, u32[]{:S(2)}) collective-permute-start(bf16[128,1024]{1,0:T(8,128)(2,1)S(1)} %maximum_select_fusion), channel_id=1, source_target_pairs={{0,968},{4,1020},{8,976},{12,964},{16,984},{20,972},{24,992},{28,9... | collective-permute-start | bytes 786440 | tf_op jit(solution)/shard_map/ppermute | solution.py:42
  39.8 1.9 %collective-permute-start.5 = (s16[80,1024]{1,0:T(8,128)(2,1)S(1)}, s16[80,1024]{1,0:T(8,128)(2,1)S(1)}, u32[]{:S(2)}, u32[]{:S(2)}) collective-permute-start(s16[80,1024]{1,0:T(8,128)(2,1)S(1)} %get-tuple-element.23), channel_id=1, source_target_pairs={{0,32},{4,36},{8,40},{12,44},{16,48},{20,52},{24,56},{28,60},{32,0... | collective-permute-start | bytes 491528 | tf_op jit(solution)/shard_map/ppermute | solution.py:27
  41.7 3.0 %collective-permute-done.8.q3_ref.q1_ref = s16[288,1024]{1,0:T(8,128)(2,1)S(1)} collective-permute-done((s16[288,1024]{1,0:T(8,128)(2,1)S(1)}, s16[288,1024]{1,0:T(8,128)(2,1)S(1)}, u32[]{:S(2)}, u32[]{:S(2)}) %collective-permute-start.8) | collective-permute-done | bytes 589856 | tf_op jit(solution)/shard_map/ppermute | solution.py:27
  44.8 0.2 shard_map.71
  45.0 2.9 %collective-permute-start.9 = (s16[144,1024]{1,0:T(8,128)(2,1)S(1)}, s16[144,1024]{1,0:T(8,128)(2,1)S(1)}, u32[]{:S(2)}, u32[]{:S(2)}) collective-permute-start(s16[144,1024]{1,0:T(8,128)(2,1)S(1)} %shard_map.71), channel_id=1, source_target_pairs={{0,16},{4,52},{8,24},{12,60},{16,32},{20,4},{24,40},{28,12},{32,48... | collective-permute-start | bytes 884744 | tf_op jit(solution)/shard_map/ppermute | solution.py:27
  47.9 3.0 %collective-permute-start.7 = (bf16[128,1024]{1,0:T(8,128)(2,1)S(1)}, bf16[128,1024]{1,0:T(8,128)(2,1)S(1)}, u32[]{:S(2)}, u32[]{:S(2)}) collective-permute-start(bf16[128,1024]{1,0:T(8,128)(2,1)S(1)} %collective-permute-done.1.g2_ref), channel_id=1, source_target_pairs={{0,4},{4,0},{8,12},{12,8},{16,20},{20,16},{24,28},{28,24},{32,36},... | collective-permute-start | bytes 786440 | tf_op jit(solution)/shard_map/ppermute | solution.py:32
  50.9 1.1 %collective-permute-done.3.g1_ref = bf16[128,1024]{1,0:T(8,128)(2,1)S(1)} collective-permute-done((bf16[128,1024]{1,0:T(8,128)(2,1)S(1)}, bf16[128,1024]{1,0:T(8,128)(2,1)S(1)}, u32[]{:S(2)}, u32[]{:S(2)}) %collective-permute-start.3) | collective-permute-done | bytes 262176 | tf_op jit(solution)/shard_map/ppermute | solution.py:42
  52.0 2.2 %collective-permute-done.5.q4_ref = s16[80,1024]{1,0:T(8,128)(2,1)S(1)} collective-permute-done((s16[80,1024]{1,0:T(8,128)(2,1)S(1)}, s16[80,1024]{1,0:T(8,128)(2,1)S(1)}, u32[]{:S(2)}, u32[]{:S(2)}) %collective-permute-start.5) | collective-permute-done | bytes 163872 | tf_op jit(solution)/shard_map/ppermute | solution.py:27
  54.2 7.9 %collective-permute-start.6 = (bf16[128,1024]{1,0:T(8,128)(2,1)S(1)}, bf16[128,1024]{1,0:T(8,128)(2,1)S(1)}, u32[]{:S(2)}, u32[]{:S(2)}) collective-permute-start(bf16[128,1024]{1,0:T(8,128)(2,1)S(1)} %collective-permute-done.3.g1_ref), channel_id=1, source_target_pairs={{0,4},{4,0},{8,12},{12,8},{16,20},{20,16},{24,28},{28,24},{32,36},... | collective-permute-start | bytes 786440 | tf_op jit(solution)/shard_map/ppermute | solution.py:32
  62.2 3.0 %collective-permute-start.12 = (bf16[128,1024]{1,0:T(8,128)(2,1)S(1)}, bf16[128,1024]{1,0:T(8,128)(2,1)S(1)}, u32[]{:S(2)}, u32[]{:S(2)}) collective-permute-start(bf16[128,1024]{1,0:T(8,128)(2,1)S(1)} %collective-permute-done.1.g2_ref), channel_id=1, source_target_pairs={{0,8},{4,60},{8,16},{12,4},{16,24},{20,12},{24,32},{28,20},{32,40}... | collective-permute-start | bytes 786440 | tf_op jit(solution)/shard_map/ppermute | solution.py:27
  65.3 2.1 %collective-permute-start.13 = (bf16[64,1024]{1,0:T(8,128)(2,1)S(1)}, bf16[64,1024]{1,0:T(8,128)(2,1)S(1)}, u32[]{:S(2)}, u32[]{:S(2)}) collective-permute-start(bf16[64,1024]{1,0:T(8,128)(2,1)S(1)} %slice_select_fusion), channel_id=1, source_target_pairs={{0,16},{4,52},{8,24},{12,60},{16,32},{20,4},{24,40},{28,12},{32,48... | collective-permute-start | bytes 393224 | tf_op jit(solution)/shard_map/ppermute | solution.py:27
  67.3 1.2 %shard_map.68.start_ref = f32[128,512]{1,0:T(8,128)S(1)} custom-call(s32[1]{0:T(128)} %bitcast.place_ref, bf16[128,1024]{1,0:T(8,128)(2,1)S(1)} %collective-permute-done.2.u_ref, bf16[128,1024]{1,0:T(8,128)(2,1)S(1)} %collective-permute-done.3.g1_ref, bf16[128,1024]{1,0:T(8,128)(2,1)S(1)} %collective-permute-done.1.g2_ref, bf16[512,8192]{1,0:T(8,128)(2,1)S(1)} %bitcast.8), custom_call_target="tpu_custom_call" | custom-call | flops 1 | bytes 1 | tf_op jit(solution)/shard_map/pallas_call | solution.py:46
  68.6 0.5 shard_map.72
  69.1 2.3 %collective-permute-start.10 = (f32[128,512]{1,0:T(8,128)S(1)}, f32[128,512]{1,0:T(8,128)S(1)}, u32[]{:S(2)}, u32[]{:S(2)}) collective-permute-start(f32[128,512]{1,0:T(8,128)S(1)} %get-tuple-element.31), channel_id=1, source_target_pairs={{0,4},{4,0},{8,12},{12,8},{16,20},{20,16},{24,28},{28,24},{32,36},... | collective-permute-start | bytes 786440 | tf_op jit(solution)/shard_map/ppermute | solution.py:32
  71.4 1.7 %collective-permute-done.13.g4_ref = bf16[64,1024]{1,0:T(8,128)(2,1)S(1)} collective-permute-done((bf16[64,1024]{1,0:T(8,128)(2,1)S(1)}, bf16[64,1024]{1,0:T(8,128)(2,1)S(1)}, u32[]{:S(2)}, u32[]{:S(2)}) %collective-permute-start.13) | collective-permute-done | bytes 131104 | tf_op jit(solution)/shard_map/ppermute | solution.py:27
  73.1 2.2 %collective-permute-start.14 = (bf16[192,1024]{1,0:T(8,128)(2,1)S(1)}, bf16[192,1024]{1,0:T(8,128)(2,1)S(1)}, u32[]{:S(2)}, u32[]{:S(2)}) collective-permute-start(bf16[192,1024]{1,0:T(8,128)(2,1)S(1)} %pad_maximum_fusion), channel_id=1, source_target_pairs={{0,4},{4,0},{8,12},{12,8},{16,20},{20,16},{24,28},{28,24},{32,36},... | collective-permute-start | bytes 1179656 | tf_op jit(solution)/shard_map/ppermute | solution.py:32
  75.3 4.0 %collective-permute-start.11 = (bf16[128,512]{1,0:T(8,128)(2,1)S(1)}, bf16[128,512]{1,0:T(8,128)(2,1)S(1)}, u32[]{:S(2)}, u32[]{:S(2)}) collective-permute-start(bf16[128,512]{1,0:T(8,128)(2,1)S(1)} %add_convert_fusion), channel_id=1, source_target_pairs={{0,64},{4,68},{8,72},{12,76},{16,80},{20,84},{24,88},{28,92},{32,9... | collective-permute-start | bytes 393224 | tf_op jit(solution)/shard_map/ppermute | solution.py:42
  79.4 2.5 %shard_map.73 = bf16[128,512]{1,0:T(8,128)(2,1)} custom-call(s32[1]{0:T(128)} %bitcast.place_ref, bf16[128,1024]{1,0:T(8,128)(2,1)S(1)} %collective-permute-done.6.h1_ref, bf16[128,1024]{1,0:T(8,128)(2,1)S(1)} %collective-permute-done.7.h2_ref, bf16[192,1024]{1,0:T(8,128)(2,1)S(1)} %collective-permute-done.14.h34_ref, ...), custom_call_target="tpu_custom_call" | custom-call | flops 1 | bytes 1 | tf_op jit(solution)/shard_map/pallas_call | solution.py:46
  81.9 2.3 %collective-permute-done.11 = bf16[128,512]{1,0:T(8,128)(2,1)S(1)} collective-permute-done((bf16[128,512]{1,0:T(8,128)(2,1)S(1)}, bf16[128,512]{1,0:T(8,128)(2,1)S(1)}, u32[]{:S(2)}, u32[]{:S(2)}) %collective-permute-start.11) | collective-permute-done | bytes 131104 | tf_op jit(solution)/shard_map/ppermute | solution.py:42
  84.2 0.7 copy.9
  (21 shorter events, 0.1 us)
Async XLA Ops:
  1.3 1.0 %copy-start.3 = (bf16[1,4,128,512]{3,2,1,0:T(8,128)(2,1)S(1)}, bf16[1,4,128,512]{3,2,1,0:T(8,128)(2,1)}, u32[]{:S(2)}) copy-start(bf16[1,4,128,512]{3,2,1,0:T(8,128)(2,1)} %param.6) | copy-start | bytes 1572868
  2.3 22.7 %copy-start.5 = (bf16[1,128,512]{2,1,0:T(8,128)(2,1)S(1)}, bf16[1,128,512]{2,1,0:T(8,128)(2,1)}, u32[]{:S(2)}) copy-start(bf16[1,128,512]{2,1,0:T(8,128)(2,1)} %param.9) | copy-start | bytes 393220
  7.8 1.2 %copy-start.1 = (f32[448,1024]{1,0:T(8,128)}, f32[448,1024]{1,0:T(8,128)S(1)}, u32[]{:S(2)}) copy-start(f32[448,1024]{1,0:T(8,128)S(1)} %get-tuple-element.21.keep_ref) | copy-start | bytes 5505028
  9.0 20.1 %collective-permute-start.4 = (f32[512,1024]{1,0:T(8,128)}, f32[512,1024]{1,0:T(8,128)S(1)}, u32[]{:S(2)}, u32[]{:S(2)}) collective-permute-start(f32[512,1024]{1,0:T(8,128)} %get-tuple-element.22), channel_id=1, source_target_pairs={{0,4},{4,0},{8,12},{12,8},{16,20},{20,16},{24,28},{28,24},{32,36},... | collective-permute-start | bytes 6291464 | tf_op jit(solution)/shard_map/ppermute | solution.py:32
  25.1 3.9 %collective-permute-start = (bf16[128,512]{1,0:T(8,128)(2,1)S(1)}, bf16[128,512]{1,0:T(8,128)(2,1)S(1)}, u32[]{:S(2)}, u32[]{:S(2)}) collective-permute-start(bf16[128,512]{1,0:T(8,128)(2,1)S(1)} %bitcast.13), channel_id=1, source_target_pairs={{0,4},{4,0},{8,12},{12,8},{16,20},{20,16},{24,28},{28,24},{32,36},... | collective-permute-start | bytes 393224 | tf_op jit(solution)/shard_map/ppermute | solution.py:32
  29.1 1.5 %copy-start.2 = (f32[448,1024]{1,0:T(8,128)S(1)}, f32[448,1024]{1,0:T(8,128)}, u32[]{:S(2)}) copy-start(f32[448,1024]{1,0:T(8,128)} %copy-done.1) | copy-start | bytes 5505028
  30.6 36.7 %copy-start = (bf16[1,512,8192]{2,1,0:T(8,128)(2,1)S(1)}, bf16[1,512,8192]{2,1,0:T(8,128)(2,1)}, u32[]{:S(2)}) copy-start(bf16[1,512,8192]{2,1,0:T(8,128)(2,1)} %param.5) | copy-start | bytes 25165828
  30.9 13.9 %collective-permute-start.8 = (s16[288,1024]{1,0:T(8,128)(2,1)S(1)}, s16[288,1024]{1,0:T(8,128)(2,1)S(1)}, u32[]{:S(2)}, u32[]{:S(2)}) collective-permute-start(s16[288,1024]{1,0:T(8,128)(2,1)S(1)} %get-tuple-element.27), channel_id=1, source_target_pairs={{0,8},{4,60},{8,16},{12,4},{16,24},{20,12},{24,32},{28,20},{32,40}... | collective-permute-start | bytes 1769480 | tf_op jit(solution)/shard_map/ppermute | solution.py:27
  33.2 14.7 %collective-permute-start.1 = (bf16[128,1024]{1,0:T(8,128)(2,1)S(1)}, bf16[128,1024]{1,0:T(8,128)(2,1)S(1)}, u32[]{:S(2)}, u32[]{:S(2)}) collective-permute-start(bf16[128,1024]{1,0:T(8,128)(2,1)S(1)} %maximum_select_fusion), channel_id=1, source_target_pairs={{0,976},{4,1012},{8,984},{12,1020},{16,992},{20,964},{24,1000},{28... | collective-permute-start | bytes 786440 | tf_op jit(solution)/shard_map/ppermute | solution.py:42
  35.2 12.7 %collective-permute-start.2 = (bf16[128,1024]{1,0:T(8,128)(2,1)S(1)}, bf16[128,1024]{1,0:T(8,128)(2,1)S(1)}, u32[]{:S(2)}, u32[]{:S(2)}) collective-permute-start(bf16[128,1024]{1,0:T(8,128)(2,1)S(1)} %maximum_select_fusion), channel_id=1, source_target_pairs={{0,960},{4,964},{8,968},{12,972},{16,976},{20,980},{24,984},{28,98... | collective-permute-start | bytes 786440 | tf_op jit(solution)/shard_map/ppermute | solution.py:42
  37.1 14.9 %collective-permute-start.3 = (bf16[128,1024]{1,0:T(8,128)(2,1)S(1)}, bf16[128,1024]{1,0:T(8,128)(2,1)S(1)}, u32[]{:S(2)}, u32[]{:S(2)}) collective-permute-start(bf16[128,1024]{1,0:T(8,128)(2,1)S(1)} %maximum_select_fusion), channel_id=1, source_target_pairs={{0,968},{4,1020},{8,976},{12,964},{16,984},{20,972},{24,992},{28,9... | collective-permute-start | bytes 786440 | tf_op jit(solution)/shard_map/ppermute | solution.py:42
  39.8 14.4 %collective-permute-start.5 = (s16[80,1024]{1,0:T(8,128)(2,1)S(1)}, s16[80,1024]{1,0:T(8,128)(2,1)S(1)}, u32[]{:S(2)}, u32[]{:S(2)}) collective-permute-start(s16[80,1024]{1,0:T(8,128)(2,1)S(1)} %get-tuple-element.23), channel_id=1, source_target_pairs={{0,32},{4,36},{8,40},{12,44},{16,48},{20,52},{24,56},{28,60},{32,0... | collective-permute-start | bytes 491528 | tf_op jit(solution)/shard_map/ppermute | solution.py:27
  45.0 23.6 %collective-permute-start.9 = (s16[144,1024]{1,0:T(8,128)(2,1)S(1)}, s16[144,1024]{1,0:T(8,128)(2,1)S(1)}, u32[]{:S(2)}, u32[]{:S(2)}) collective-permute-start(s16[144,1024]{1,0:T(8,128)(2,1)S(1)} %shard_map.71), channel_id=1, source_target_pairs={{0,16},{4,52},{8,24},{12,60},{16,32},{20,4},{24,40},{28,12},{32,48... | collective-permute-start | bytes 884744 | tf_op jit(solution)/shard_map/ppermute | solution.py:27
  47.9 20.6 %collective-permute-start.7 = (bf16[128,1024]{1,0:T(8,128)(2,1)S(1)}, bf16[128,1024]{1,0:T(8,128)(2,1)S(1)}, u32[]{:S(2)}, u32[]{:S(2)}) collective-permute-start(bf16[128,1024]{1,0:T(8,128)(2,1)S(1)} %collective-permute-done.1.g2_ref), channel_id=1, source_target_pairs={{0,4},{4,0},{8,12},{12,8},{16,20},{20,16},{24,28},{28,24},{32,36},... | collective-permute-start | bytes 786440 | tf_op jit(solution)/shard_map/ppermute | solution.py:32
  54.2 14.3 %collective-permute-start.6 = (bf16[128,1024]{1,0:T(8,128)(2,1)S(1)}, bf16[128,1024]{1,0:T(8,128)(2,1)S(1)}, u32[]{:S(2)}, u32[]{:S(2)}) collective-permute-start(bf16[128,1024]{1,0:T(8,128)(2,1)S(1)} %collective-permute-done.3.g1_ref), channel_id=1, source_target_pairs={{0,4},{4,0},{8,12},{12,8},{16,20},{20,16},{24,28},{28,24},{32,36},... | collective-permute-start | bytes 786440 | tf_op jit(solution)/shard_map/ppermute | solution.py:32
  62.2 10.9 %collective-permute-start.12 = (bf16[128,1024]{1,0:T(8,128)(2,1)S(1)}, bf16[128,1024]{1,0:T(8,128)(2,1)S(1)}, u32[]{:S(2)}, u32[]{:S(2)}) collective-permute-start(bf16[128,1024]{1,0:T(8,128)(2,1)S(1)} %collective-permute-done.1.g2_ref), channel_id=1, source_target_pairs={{0,8},{4,60},{8,16},{12,4},{16,24},{20,12},{24,32},{28,20},{32,40}... | collective-permute-start | bytes 786440 | tf_op jit(solution)/shard_map/ppermute | solution.py:27
  65.3 3.3 %copy-start.4 = (bf16[1,4,128,512]{3,2,1,0:T(8,128)(2,1)S(1)}, bf16[1,4,128,512]{3,2,1,0:T(8,128)(2,1)}, u32[]{:S(2)}) copy-start(bf16[1,4,128,512]{3,2,1,0:T(8,128)(2,1)} %param.7) | copy-start | bytes 1572868
  65.3 7.8 %collective-permute-start.13 = (bf16[64,1024]{1,0:T(8,128)(2,1)S(1)}, bf16[64,1024]{1,0:T(8,128)(2,1)S(1)}, u32[]{:S(2)}, u32[]{:S(2)}) collective-permute-start(bf16[64,1024]{1,0:T(8,128)(2,1)S(1)} %slice_select_fusion), channel_id=1, source_target_pairs={{0,16},{4,52},{8,24},{12,60},{16,32},{20,4},{24,40},{28,12},{32,48... | collective-permute-start | bytes 393224 | tf_op jit(solution)/shard_map/ppermute | solution.py:27
  69.1 6.2 %collective-permute-start.10 = (f32[128,512]{1,0:T(8,128)S(1)}, f32[128,512]{1,0:T(8,128)S(1)}, u32[]{:S(2)}, u32[]{:S(2)}) collective-permute-start(f32[128,512]{1,0:T(8,128)S(1)} %get-tuple-element.31), channel_id=1, source_target_pairs={{0,4},{4,0},{8,12},{12,8},{16,20},{20,16},{24,28},{28,24},{32,36},... | collective-permute-start | bytes 786440 | tf_op jit(solution)/shard_map/ppermute | solution.py:32
  73.1 6.2 %collective-permute-start.14 = (bf16[192,1024]{1,0:T(8,128)(2,1)S(1)}, bf16[192,1024]{1,0:T(8,128)(2,1)S(1)}, u32[]{:S(2)}, u32[]{:S(2)}) collective-permute-start(bf16[192,1024]{1,0:T(8,128)(2,1)S(1)} %pad_maximum_fusion), channel_id=1, source_target_pairs={{0,4},{4,0},{8,12},{12,8},{16,20},{20,16},{24,28},{28,24},{32,36},... | collective-permute-start | bytes 1179656 | tf_op jit(solution)/shard_map/ppermute | solution.py:32
  75.3 8.8 %collective-permute-start.11 = (bf16[128,512]{1,0:T(8,128)(2,1)S(1)}, bf16[128,512]{1,0:T(8,128)(2,1)S(1)}, u32[]{:S(2)}, u32[]{:S(2)}) collective-permute-start(bf16[128,512]{1,0:T(8,128)(2,1)S(1)} %add_convert_fusion), channel_id=1, source_target_pairs={{0,64},{4,68},{8,72},{12,76},{16,80},{20,84},{24,88},{28,92},{32,9... | collective-permute-start | bytes 393224 | tf_op jit(solution)/shard_map/ppermute | solution.py:42

commit v4 on v3

--- a/solution.py
+++ b/solution.py
@@ -87,7 +87,7 @@
 
     order = (-3, 3, -2, 2, -1, 1, 4, 0)
 
-    def body(place_ref, plan_ref, ctx_ref, w_ref, send_ref, keep_ref, own_ref, held, ctx, full, sems, ctx_sem):
+    def body(place_ref, plan_ref, ctx_ref, w_ref, send_ref, keep3_ref, keep2_ref, keep1_ref, keep4_ref, own_ref, held, ctx, full, sems, ctx_sem):
         here = place_ref[0]
         core = here % 2
         mine, theirs = core, 1 - core
@@ -106,13 +106,12 @@
             copies[slot].wait()
             return jnp.dot(ctx[...], held[slot], preferred_element_type=F32)
 
-        for slot, by in enumerate((3, 2, 1)):
-            rows = slice(slot * ROWS, (slot + 1) * ROWS)
-            send_ref[rows] = product(-by)
-            keep_ref[rows] = product(by)
+        for slot, (by, keep_ref) in enumerate(((3, keep3_ref), (2, keep2_ref), (1, keep1_ref))):
+            send_ref[slot * ROWS : (slot + 1) * ROWS] = product(-by)
+            keep_ref[...] = product(by)
         full[...] = product(4)
         send_ref[3 * ROWS : 3 * ROWS + HALF] = full[pl.ds(pl.multiple_of(theirs * HALF, HALF), HALF)]
-        keep_ref[3 * ROWS :] = full[pl.ds(pl.multiple_of(mine * HALF, HALF), HALF)]
+        keep4_ref[...] = full[pl.ds(pl.multiple_of(mine * HALF, HALF), HALF)]
         full[...] = product(0)
         for part, at in ((0, 0), (1, HALF)):
             lanes = slice(part * BLOCK, (part + 1) * BLOCK)
@@ -123,7 +122,7 @@
     heads = weights.shape[0]
     return call(
         body,
-        [((4 * ROWS, WIDE), F32), ((3 * ROWS + HALF, WIDE), F32), ((HALF, WIDE), F32)],
+        [((4 * ROWS, WIDE), F32)] + [((ROWS, WIDE), F32)] * 3 + [((HALF, WIDE), F32)] * 2,
         (place, plan, contexts, weights),
         [SMEM, SMEM, ANY, ANY],
         [
@@ -137,42 +136,44 @@
     )
 
 
-def encode_first(place, keep, arrived):
-    def body(place_ref, keep_ref, in_ref, q31_ref, q4_ref):
-        coded = ROWS + 16
-        encode(keep_ref[:ROWS] + in_ref[:ROWS], q31_ref.at[:coded])
-        encode(keep_ref[2 * ROWS : 3 * ROWS] + in_ref[2 * ROWS : 3 * ROWS], q31_ref.at[coded:])
-        encode(keep_ref[3 * ROWS :] + in_ref[3 * ROWS : 3 * ROWS + HALF], q4_ref)
-
-    return call(
-        body,
-        [((2 * ROWS + 32, WIDE), CODE), ((HALF + 16, WIDE), CODE)],
-        (place, keep, arrived),
-        [SMEM, VMEM, VMEM],
-    )
-
-
-def encode_two(keep, arrived, q31):
-    def body(keep_ref, in_ref, q3_ref, q_ref):
-        encode(keep_ref[...] + in_ref[...] + decode(q3_ref), q_ref)
-
-    return call(
-        body,
-        [((ROWS + 16, WIDE), CODE)],
-        (keep, arrived, q31),
-        [rows_of(ROWS, 1), rows_of(ROWS, 1), rows_of(ROWS + 16, 0)],
+def encode_first(place, keep3, keep4, arrived):
+    def body(place_ref, keep3_ref, keep4_ref, in3_ref, in4_ref, q_ref):
+        encode(keep3_ref[...] + in3_ref[...], q_ref.at[: ROWS + 16])
+        encode(keep4_ref[...] + in4_ref[...], q_ref.at[ROWS + 16 :])
+
+    return call(
+        body,
+        [((ROWS + HALF + 32, WIDE), CODE)],
+        (place, keep3, keep4, arrived, arrived),
+        [SMEM, VMEM, VMEM, rows_of(ROWS, 0), rows_of(HALF, 6)],
     )[0]
 
 
-def gather_home(place, plan, q31, q2, q4, own, arrived, residual):
-    def body(place_ref, plan_ref, q1_ref, q2_ref, q4_ref, own_ref, in_ref, res_ref, send_ref, part_ref, full, stream, sem):
+def encode_two(place, keep2, keep1, arrived, q34):
+    def body(place_ref, keep2_ref, keep1_ref, in2_ref, in1_ref, q34_ref, q2_ref, q1_ref, total):
+        mine = pl.multiple_of((place_ref[0] % 2) * HALF, HALF)
+        total[...] = keep2_ref[...] + in2_ref[...]
+        total[pl.ds(mine, HALF)] += decode(q34_ref.at[ROWS + 16 :])
+        encode(total[...], q2_ref)
+        encode(keep1_ref[...] + in1_ref[...] + decode(q34_ref.at[: ROWS + 16]), q1_ref)
+
+    return call(
+        body,
+        [((ROWS + 16, WIDE), CODE)] * 2,
+        (place, keep2, keep1, arrived, arrived, q34),
+        [SMEM, VMEM, VMEM, rows_of(ROWS, 1), rows_of(ROWS, 2), VMEM],
+        [pltpu.VMEM((ROWS, WIDE), F32)],
+    )
+
+
+def gather_home(place, plan, q1, q2, own, arrived, residual):
+    def body(place_ref, plan_ref, q1_ref, q2_ref, own_ref, in_ref, res_ref, send_ref, part_ref, full, stream, sem):
         fetch = pltpu.make_async_copy(res_ref.at[plan_ref[0]], stream, sem)
         fetch.start()
         core = place_ref[0] % 2
         mine = pl.multiple_of(core * BLOCK, BLOCK)
         theirs = pl.multiple_of((1 - core) * BLOCK, BLOCK)
         full[...] = decode(q1_ref) + decode(q2_ref)
-        full[pl.ds(pl.multiple_of(core * HALF, HALF), HALF)] += decode(q4_ref)
         send_ref[...] = full[:, pl.ds(theirs, BLOCK)]
         fetch.wait()
         for part, at in ((0, 0), (1, HALF)):
@@ -188,8 +189,8 @@
     return call(
         body,
         [((ROWS, BLOCK), F32)] * 2,
-        (place, plan, q31, q2, q4, own, arrived, residual),
-        [SMEM, SMEM, rows_of(ROWS + 16, 1), VMEM, VMEM, VMEM, rows_of(HALF, 7), ANY],
+        (place, plan, q1, q2, own, arrived, residual),
+        [SMEM, SMEM, VMEM, VMEM, VMEM, rows_of(HALF, 7), ANY],
         [pltpu.VMEM((ROWS, WIDE), F32), pltpu.VMEM((ROWS, BLOCK), BF16), pltpu.SemaphoreType.DMA],
     )
 
@@ -248,31 +249,30 @@
     chips = lax.axis_size("tensor") // 2
     first = at % 2 == 0
 
-    send, keep, own = project(place, plan, contexts, w_local, chips)
+    send, keep3, keep2, keep1, keep4, own = project(place, plan, contexts, w_local, chips)
     arrived = core_swap(send)
     mate = core_swap(upstream[0])
     pair = jnp.where(
         first, jnp.concatenate([upstream[0], mate], 1), jnp.concatenate([mate, upstream[0]], 1)
     )
     after, pair = lax.optimization_barrier((place, pair))
-    q31, q4 = encode_first(after, keep, arrived)
-    q31, q4 = split_shift(q31, 1), split_shift(q4, 4)
-    q2 = split_shift(encode_two(keep, arrived, q31), 2)
+    q34 = split_shift(encode_first(after, keep3, keep4, arrived), 2)
+    q2, q1 = encode_two(place, keep2, keep1, arrived, q34)
+    q2, q1 = split_shift(q2, 2), split_shift(q1, 1)
 
     g1 = next_section(pair, -1, 1)
     g2 = next_section(pair, -1, 2)
     g3 = split_shift(g2, 1)
     g4 = split_shift(jnp.where(first, g2[:HALF], g2[HALF:]), 2)
     g0 = next_section(pair, -1)
-    to_mate, q4 = lax.optimization_barrier((g1, q4))
+    h2 = core_swap(g2)
+    to_mate, g0 = lax.optimization_barrier((g1, g0))
     h1 = core_swap(to_mate)
-    to_mate, g0 = lax.optimization_barrier((g2, g0))
-    h2 = core_swap(to_mate)
     h34 = core_swap(jnp.concatenate([g3, g4], 0))
     early = backproject_first(place, (g0, g1, g2), w_local, chips)
 
     after, _, _, _ = lax.optimization_barrier((place, early, h1, h2))
-    send, part = gather_home(after, plan, q31, q2, q4, own, arrived, residual)
+    send, part = gather_home(after, plan, q1, q2, own, arrived, residual)
     hidden = (part + core_swap(send)).astype(BF16)
     boundary = next_section(hidden, 1)
     gradient = backproject_rest(place, h1, h2, h34, g3, g4, early, w_local, chips)

time: 86.1 us -> 87 us (1.010)
  other arithmetic: 0.16 us -> 1.13 us
    ppermute x5, starting transfers between devices: 12.2 us -> 18.9 us  [split_shift(): return lax.ppermute(value, 'tensor', pairs)]
    ppermute x6, starting transfers between devices: 33.3 us -> 28.5 us  [core_swap(): return lax.ppermute(value, 'tensor', [(i, i ^ 1) for i in range(peers)])]
    ppermute x4, starting transfers between devices: 10.5 us -> 8.24 us  [next_section(): return lax.ppermute(value, ('section', 'tensor'), pairs)]
    ppermute x4, waiting for transfers between devices: 3.38 us -> 4.64 us  [next_section(): return lax.ppermute(value, ('section', 'tensor'), pairs)]
    ppermute x5, waiting for transfers between devices: 6.93 us -> 5.73 us  [split_shift(): return lax.ppermute(value, 'tensor', pairs)]
    select_n x1, other arithmetic: 0.08 us -> 1.05 us  [on_device(): jnp.where(first, jnp.concatenate([upstream[0], mate], 1), jnp.concatenate...]
    unnamed x13 -> x17, local copies, waits for them, and re-layouts: 4.41 us -> 5.19 us
  transfers between devices with their start and end apart: 15 -> 15, of which waited for: 6 -> 3; matrix products, arithmetic and copies ran while one was open for 0% -> 1% of each run, Pallas kernels for 5% -> 5%
where the time goes in v4:
time: 87 us; the launch traced here: 86.4 us
  starting transfers between devices  55.6 us (64%)
  waiting for transfers between devices  12.5 us (14%)
  Pallas kernels  10.3 us (12%)
  local copies, waits for them, and re-layouts  5.19 us (6%)
  between operations  1.64 us (2%)
  other arithmetic  1.13 us (1%)
    ppermute x6, starting transfers between devices, core_swap(): return lax.ppermute(value, 'tensor', [(i, i ^ 1) for i in range(peers)])  28.5 us
    ppermute x5, starting transfers between devices, split_shift(): return lax.ppermute(value, 'tensor', pairs)  18.9 us
    pallas_call x6, Pallas kernels, call(): pl.pallas_call(body, grid=(1,), in_specs=specs, out_specs=[VMEM] * len(ou...  10.3 us
    ppermute x4, starting transfers between devices, next_section(): return lax.ppermute(value, ('section', 'tensor'), pairs)  8.24 us
    ppermute x5, waiting for transfers between devices, split_shift(): return lax.ppermute(value, 'tensor', pairs)  5.73 us
    unnamed x17, local copies, waits for them, and re-layouts  5.19 us
    ppermute x4, waiting for transfers between devices, next_section(): return lax.ppermute(value, ('section', 'tensor'), pairs)  4.64 us
    ppermute x6, waiting for transfers between devices, core_swap(): return lax.ppermute(value, 'tensor', [(i, i ^ 1) for i in range(peers)])  2.15 us
  transfers between devices with their start and end apart: 15, of which 3 were waited for; matrix products, arithmetic and copies ran while one was open for 1% of the time, Pallas kernels for 5%

profile of v4, /device:TPU:1, one launch (start us, length us, event | category | flops | bytes accessed | tf_op | source)
XLA Modules:
  0.0 86.4 jit_solution(7811238923204623635)
XLA Ops:
  1.3 1.0 %copy-done.1 = bf16[1,4,128,512]{3,2,1,0:T(8,128)(2,1)S(1)} copy-done((bf16[1,4,128,512]{3,2,1,0:T(8,128)(2,1)S(1)}, bf16[1,4,128,512]{3,2,1,0:T(8,128)(2,1)}, u32[]{:S(2)}) %copy-start.1) | copy-done | bytes 524312
  2.3 5.4 %shard_map.69 = (f32[512,1024]{1,0:T(8,128)}, f32[128,1024]{1,0:T(8,128)S(1)}, f32[128,1024]{1,0:T(8,128)S(1)}, f32[128,1024]{1,0:T(8,128)S(1)}, f32[64,1024]{1,0:T(8,128)S(1)}, /*index=5*/f32[64,1024]{1,0:T(8,128)S(1)}) custom-call(s32[1]{0:T(128)} %bitcast.place_ref, s32[1]{0:T(128)S(6)} %copy.8.plan_ref, bf16[4,128,512]{2,1,0:T(8,128)(2,1)S(1)} %bitcast.10, ...), custom_call_target="tpu_custom_call" | custom-call | flops 1 | bytes 1 | tf_op jit(solution)/shard_map/pallas_call | solution.py:46
  7.8 0.8 copy-done.3
  8.6 0.7 copy-done.5
  9.3 16.0 %collective-permute-start.6 = (f32[512,1024]{1,0:T(8,128)}, f32[512,1024]{1,0:T(8,128)S(1)}, u32[]{:S(2)}, u32[]{:S(2)}) collective-permute-start(f32[512,1024]{1,0:T(8,128)} %get-tuple-element.25), channel_id=1, source_target_pairs={{0,4},{4,0},{8,12},{12,8},{16,20},{20,16},{24,28},{28,24},{32,36},... | collective-permute-start | bytes 6291464 | tf_op jit(solution)/shard_map/ppermute | solution.py:32
  25.4 1.9 %collective-permute-start = (bf16[128,512]{1,0:T(8,128)(2,1)S(1)}, bf16[128,512]{1,0:T(8,128)(2,1)}, u32[]{:S(2)}, u32[]{:S(2)}) collective-permute-start(bf16[128,512]{1,0:T(8,128)(2,1)S(1)} %bitcast.13), channel_id=1, source_target_pairs={{0,4},{4,0},{8,12},{12,8},{16,20},{20,16},{24,28},{28,24},{32,36},... | collective-permute-start | bytes 393224 | tf_op jit(solution)/shard_map/ppermute | solution.py:32
  27.3 2.1 %collective-permute-done = bf16[128,512]{1,0:T(8,128)(2,1)} collective-permute-done((bf16[128,512]{1,0:T(8,128)(2,1)S(1)}, bf16[128,512]{1,0:T(8,128)(2,1)}, u32[]{:S(2)}, u32[]{:S(2)}) %collective-permute-start) | collective-permute-done | bytes 131104 | tf_op jit(solution)/shard_map/ppermute | solution.py:32
  29.4 1.0 %maximum_select_fusion = bf16[128,1024]{1,0:T(8,128)(2,1)S(1)} fusion(bf16[128,512]{1,0:T(8,128)(2,1)} %collective-permute-done, bf16[128,512]{1,0:T(8,128)(2,1)S(1)} %bitcast.14, pred[]{:T(512)S(6)} %eq.5), kind=kLoop, calls=%fused_computation.1 | loop fusion | flops 1179648 | bytes 524289 | tf_op jit(solution)/shard_map/jit(_where)/select_n | solution.py:255
  30.5 1.0 %copy-done.4 = f32[128,1024]{1,0:T(8,128)S(1)} copy-done((f32[128,1024]{1,0:T(8,128)S(1)}, f32[128,1024]{1,0:T(8,128)}, u32[]{:S(2)}) %copy-start.4) | copy-done | bytes 524312
  31.5 0.9 %copy-done.6 = f32[64,1024]{1,0:T(8,128)S(1)} copy-done((f32[64,1024]{1,0:T(8,128)S(1)}, f32[64,1024]{1,0:T(8,128)}, u32[]{:S(2)}) %copy-start.6) | copy-done | bytes 262168
  32.5 0.2 shard_map.70
  32.7 2.3 %collective-permute-start.7 = (s16[224,1024]{1,0:T(8,128)(2,1)S(1)}, s16[224,1024]{1,0:T(8,128)(2,1)S(1)}, u32[]{:S(2)}, u32[]{:S(2)}) collective-permute-start(s16[224,1024]{1,0:T(8,128)(2,1)S(1)} %shard_map.70), channel_id=1, source_target_pairs={{0,16},{4,52},{8,24},{12,60},{16,32},{20,4},{24,40},{28,12},{32,48... | collective-permute-start | bytes 1376264 | tf_op jit(solution)/shard_map/ppermute | solution.py:27
  35.0 1.9 %collective-permute-start.3 = (bf16[128,1024]{1,0:T(8,128)(2,1)S(1)}, bf16[128,1024]{1,0:T(8,128)(2,1)S(1)}, u32[]{:S(2)}, u32[]{:S(2)}) collective-permute-start(bf16[128,1024]{1,0:T(8,128)(2,1)S(1)} %maximum_select_fusion), channel_id=1, source_target_pairs={{0,976},{4,1012},{8,984},{12,1020},{16,992},{20,964},{24,1000},{28... | collective-permute-start | bytes 786440 | tf_op jit(solution)/shard_map/ppermute | solution.py:42
  36.9 1.9 %collective-permute-start.2 = (bf16[128,1024]{1,0:T(8,128)(2,1)S(1)}, bf16[128,1024]{1,0:T(8,128)(2,1)S(1)}, u32[]{:S(2)}, u32[]{:S(2)}) collective-permute-start(bf16[128,1024]{1,0:T(8,128)(2,1)S(1)} %maximum_select_fusion), channel_id=1, source_target_pairs={{0,960},{4,964},{8,968},{12,972},{16,976},{20,980},{24,984},{28,98... | collective-permute-start | bytes 786440 | tf_op jit(solution)/shard_map/ppermute | solution.py:42
  38.9 2.5 %collective-permute-start.1 = (bf16[128,1024]{1,0:T(8,128)(2,1)S(1)}, bf16[128,1024]{1,0:T(8,128)(2,1)S(1)}, u32[]{:S(2)}, u32[]{:S(2)}) collective-permute-start(bf16[128,1024]{1,0:T(8,128)(2,1)S(1)} %maximum_select_fusion), channel_id=1, source_target_pairs={{0,968},{4,1020},{8,976},{12,964},{16,984},{20,972},{24,992},{28,9... | collective-permute-start | bytes 786440 | tf_op jit(solution)/shard_map/ppermute | solution.py:42
  41.4 5.7 %collective-permute-done.7.q34_ref = s16[224,1024]{1,0:T(8,128)(2,1)S(1)} collective-permute-done((s16[224,1024]{1,0:T(8,128)(2,1)S(1)}, s16[224,1024]{1,0:T(8,128)(2,1)S(1)}, u32[]{:S(2)}, u32[]{:S(2)}) %collective-permute-start.7) | collective-permute-done | bytes 458784 | tf_op jit(solution)/shard_map/ppermute | solution.py:27
  47.1 0.5 shard_map.71
  47.6 5.1 %collective-permute-start.8 = (s16[144,1024]{1,0:T(8,128)(2,1)S(1)}, s16[144,1024]{1,0:T(8,128)(2,1)S(1)}, u32[]{:S(2)}, u32[]{:S(2)}) collective-permute-start(s16[144,1024]{1,0:T(8,128)(2,1)S(1)} %get-tuple-element.29), channel_id=1, source_target_pairs={{0,8},{4,60},{8,16},{12,4},{16,24},{20,12},{24,32},{28,20},{32,40}... | collective-permute-start | bytes 884744 | tf_op jit(solution)/shard_map/ppermute | solution.py:27
  52.7 1.9 %collective-permute-start.9 = (s16[144,1024]{1,0:T(8,128)(2,1)S(1)}, s16[144,1024]{1,0:T(8,128)(2,1)S(1)}, u32[]{:S(2)}, u32[]{:S(2)}) collective-permute-start(s16[144,1024]{1,0:T(8,128)(2,1)S(1)} %get-tuple-element.30), channel_id=1, source_target_pairs={{0,16},{4,52},{8,24},{12,60},{16,32},{20,4},{24,40},{28,12},{32,48... | collective-permute-start | bytes 884744 | tf_op jit(solution)/shard_map/ppermute | solution.py:27
  54.6 3.8 %collective-permute-start.5 = (bf16[128,1024]{1,0:T(8,128)(2,1)S(1)}, bf16[128,1024]{1,0:T(8,128)(2,1)S(1)}, u32[]{:S(2)}, u32[]{:S(2)}) collective-permute-start(bf16[128,1024]{1,0:T(8,128)(2,1)S(1)} %collective-permute-done.3.g2_ref), channel_id=1, source_target_pairs={{0,4},{4,0},{8,12},{12,8},{16,20},{20,16},{24,28},{28,24},{32,36},... | collective-permute-start | bytes 786440 | tf_op jit(solution)/shard_map/ppermute | solution.py:32
  58.4 1.9 %collective-permute-start.4 = (bf16[128,1024]{1,0:T(8,128)(2,1)S(1)}, bf16[128,1024]{1,0:T(8,128)(2,1)S(1)}, u32[]{:S(2)}, u32[]{:S(2)}) collective-permute-start(bf16[128,1024]{1,0:T(8,128)(2,1)S(1)} %collective-permute-done.1.g1_ref), channel_id=1, source_target_pairs={{0,4},{4,0},{8,12},{12,8},{16,20},{20,16},{24,28},{28,24},{32,36},... | collective-permute-start | bytes 786440 | tf_op jit(solution)/shard_map/ppermute | solution.py:32
  60.4 4.9 %collective-permute-start.12 = (bf16[128,1024]{1,0:T(8,128)(2,1)S(1)}, bf16[128,1024]{1,0:T(8,128)(2,1)S(1)}, u32[]{:S(2)}, u32[]{:S(2)}) collective-permute-start(bf16[128,1024]{1,0:T(8,128)(2,1)S(1)} %collective-permute-done.3.g2_ref), channel_id=1, source_target_pairs={{0,8},{4,60},{8,16},{12,4},{16,24},{20,12},{24,32},{28,20},{32,40}... | collective-permute-start | bytes 786440 | tf_op jit(solution)/shard_map/ppermute | solution.py:27
  65.2 0.0 copy-start.2
  65.3 4.7 %collective-permute-start.13 = (bf16[64,1024]{1,0:T(8,128)(2,1)S(1)}, bf16[64,1024]{1,0:T(8,128)(2,1)S(1)}, u32[]{:S(2)}, u32[]{:S(2)}) collective-permute-start(bf16[64,1024]{1,0:T(8,128)(2,1)S(1)} %slice_select_fusion), channel_id=1, source_target_pairs={{0,16},{4,52},{8,24},{12,60},{16,32},{20,4},{24,40},{28,12},{32,48... | collective-permute-start | bytes 393224 | tf_op jit(solution)/shard_map/ppermute | solution.py:27
  70.0 1.2 %shard_map.68.start_ref = f32[128,512]{1,0:T(8,128)S(1)} custom-call(s32[1]{0:T(128)} %bitcast.place_ref, bf16[128,1024]{1,0:T(8,128)(2,1)S(1)} %collective-permute-done.2.u_ref, bf16[128,1024]{1,0:T(8,128)(2,1)S(1)} %collective-permute-done.1.g1_ref, bf16[128,1024]{1,0:T(8,128)(2,1)S(1)} %collective-permute-done.3.g2_ref, bf16[512,8192]{1,0:T(8,128)(2,1)S(1)} %bitcast.8), custom_call_target="tpu_custom_call" | custom-call | flops 1 | bytes 1 | tf_op jit(solution)/shard_map/pallas_call | solution.py:46
  71.2 0.5 shard_map.72
  71.7 1.9 %collective-permute-start.10 = (f32[128,512]{1,0:T(8,128)S(1)}, f32[128,512]{1,0:T(8,128)S(1)}, u32[]{:S(2)}, u32[]{:S(2)}) collective-permute-start(f32[128,512]{1,0:T(8,128)S(1)} %get-tuple-element.33), channel_id=1, source_target_pairs={{0,4},{4,0},{8,12},{12,8},{16,20},{20,16},{24,28},{28,24},{32,36},... | collective-permute-start | bytes 786440 | tf_op jit(solution)/shard_map/ppermute | solution.py:32
  73.7 2.9 %collective-permute-start.14 = (bf16[192,1024]{1,0:T(8,128)(2,1)S(1)}, bf16[192,1024]{1,0:T(8,128)(2,1)S(1)}, u32[]{:S(2)}, u32[]{:S(2)}) collective-permute-start(bf16[192,1024]{1,0:T(8,128)(2,1)S(1)} %pad_maximum_fusion), channel_id=1, source_target_pairs={{0,4},{4,0},{8,12},{12,8},{16,20},{20,16},{24,28},{28,24},{32,36},... | collective-permute-start | bytes 1179656 | tf_op jit(solution)/shard_map/ppermute | solution.py:32
  76.6 1.9 %collective-permute-start.11 = (bf16[128,512]{1,0:T(8,128)(2,1)S(1)}, bf16[128,512]{1,0:T(8,128)(2,1)S(1)}, u32[]{:S(2)}, u32[]{:S(2)}) collective-permute-start(bf16[128,512]{1,0:T(8,128)(2,1)S(1)} %add_convert_fusion), channel_id=1, source_target_pairs={{0,64},{4,68},{8,72},{12,76},{16,80},{20,84},{24,88},{28,92},{32,9... | collective-permute-start | bytes 393224 | tf_op jit(solution)/shard_map/ppermute | solution.py:42
  78.5 2.5 %shard_map.73 = bf16[128,512]{1,0:T(8,128)(2,1)} custom-call(s32[1]{0:T(128)} %bitcast.place_ref, bf16[128,1024]{1,0:T(8,128)(2,1)S(1)} %collective-permute-done.4.h1_ref, bf16[128,1024]{1,0:T(8,128)(2,1)S(1)} %collective-permute-done.5.h2_ref, bf16[192,1024]{1,0:T(8,128)(2,1)S(1)} %collective-permute-done.14.h34_ref, ...), custom_call_target="tpu_custom_call" | custom-call | flops 1 | bytes 1 | tf_op jit(solution)/shard_map/pallas_call | solution.py:46
  81.1 4.6 %collective-permute-done.11 = bf16[128,512]{1,0:T(8,128)(2,1)S(1)} collective-permute-done((bf16[128,512]{1,0:T(8,128)(2,1)S(1)}, bf16[128,512]{1,0:T(8,128)(2,1)S(1)}, u32[]{:S(2)}, u32[]{:S(2)}) %collective-permute-start.11) | collective-permute-done | bytes 131104 | tf_op jit(solution)/shard_map/ppermute | solution.py:42
  85.7 0.7 copy.9
  (25 shorter events, 0.1 us)
Async XLA Ops:
  1.3 1.0 %copy-start.1 = (bf16[1,4,128,512]{3,2,1,0:T(8,128)(2,1)S(1)}, bf16[1,4,128,512]{3,2,1,0:T(8,128)(2,1)}, u32[]{:S(2)}) copy-start(bf16[1,4,128,512]{3,2,1,0:T(8,128)(2,1)} %param.6) | copy-start | bytes 1572868
  2.3 23.0 %copy-start.7 = (bf16[1,128,512]{2,1,0:T(8,128)(2,1)S(1)}, bf16[1,128,512]{2,1,0:T(8,128)(2,1)}, u32[]{:S(2)}) copy-start(bf16[1,128,512]{2,1,0:T(8,128)(2,1)} %param.9) | copy-start | bytes 393220
  7.8 0.8 copy-start.3
  8.6 0.7 copy-start.5
  9.3 21.2 %collective-permute-start.6 = (f32[512,1024]{1,0:T(8,128)}, f32[512,1024]{1,0:T(8,128)S(1)}, u32[]{:S(2)}, u32[]{:S(2)}) collective-permute-start(f32[512,1024]{1,0:T(8,128)} %get-tuple-element.25), channel_id=1, source_target_pairs={{0,4},{4,0},{8,12},{12,8},{16,20},{20,16},{24,28},{28,24},{32,36},... | collective-permute-start | bytes 6291464 | tf_op jit(solution)/shard_map/ppermute | solution.py:32
  25.4 4.1 %collective-permute-start = (bf16[128,512]{1,0:T(8,128)(2,1)S(1)}, bf16[128,512]{1,0:T(8,128)(2,1)}, u32[]{:S(2)}, u32[]{:S(2)}) collective-permute-start(bf16[128,512]{1,0:T(8,128)(2,1)S(1)} %bitcast.13), channel_id=1, source_target_pairs={{0,4},{4,0},{8,12},{12,8},{16,20},{20,16},{24,28},{28,24},{32,36},... | collective-permute-start | bytes 393224 | tf_op jit(solution)/shard_map/ppermute | solution.py:32
  30.5 1.0 %copy-start.4 = (f32[128,1024]{1,0:T(8,128)S(1)}, f32[128,1024]{1,0:T(8,128)}, u32[]{:S(2)}) copy-start(f32[128,1024]{1,0:T(8,128)} %copy-done.3) | copy-start | bytes 1572868
  31.5 0.9 %copy-start.6 = (f32[64,1024]{1,0:T(8,128)S(1)}, f32[64,1024]{1,0:T(8,128)}, u32[]{:S(2)}) copy-start(f32[64,1024]{1,0:T(8,128)} %copy-done.5) | copy-start | bytes 786436
  32.5 37.5 %copy-start = (bf16[1,512,8192]{2,1,0:T(8,128)(2,1)S(1)}, bf16[1,512,8192]{2,1,0:T(8,128)(2,1)}, u32[]{:S(2)}) copy-start(bf16[1,512,8192]{2,1,0:T(8,128)(2,1)} %param.5) | copy-start | bytes 25165828
  32.7 14.4 %collective-permute-start.7 = (s16[224,1024]{1,0:T(8,128)(2,1)S(1)}, s16[224,1024]{1,0:T(8,128)(2,1)S(1)}, u32[]{:S(2)}, u32[]{:S(2)}) collective-permute-start(s16[224,1024]{1,0:T(8,128)(2,1)S(1)} %shard_map.70), channel_id=1, source_target_pairs={{0,16},{4,52},{8,24},{12,60},{16,32},{20,4},{24,40},{28,12},{32,48... | collective-permute-start | bytes 1376264 | tf_op jit(solution)/shard_map/ppermute | solution.py:27
  35.0 19.6 %collective-permute-start.3 = (bf16[128,1024]{1,0:T(8,128)(2,1)S(1)}, bf16[128,1024]{1,0:T(8,128)(2,1)S(1)}, u32[]{:S(2)}, u32[]{:S(2)}) collective-permute-start(bf16[128,1024]{1,0:T(8,128)(2,1)S(1)} %maximum_select_fusion), channel_id=1, source_target_pairs={{0,976},{4,1012},{8,984},{12,1020},{16,992},{20,964},{24,1000},{28... | collective-permute-start | bytes 786440 | tf_op jit(solution)/shard_map/ppermute | solution.py:42
  36.9 21.5 %collective-permute-start.2 = (bf16[128,1024]{1,0:T(8,128)(2,1)S(1)}, bf16[128,1024]{1,0:T(8,128)(2,1)S(1)}, u32[]{:S(2)}, u32[]{:S(2)}) collective-permute-start(bf16[128,1024]{1,0:T(8,128)(2,1)S(1)} %maximum_select_fusion), channel_id=1, source_target_pairs={{0,960},{4,964},{8,968},{12,972},{16,976},{20,980},{24,984},{28,98... | collective-permute-start | bytes 786440 | tf_op jit(solution)/shard_map/ppermute | solution.py:42
  38.9 19.6 %collective-permute-start.1 = (bf16[128,1024]{1,0:T(8,128)(2,1)S(1)}, bf16[128,1024]{1,0:T(8,128)(2,1)S(1)}, u32[]{:S(2)}, u32[]{:S(2)}) collective-permute-start(bf16[128,1024]{1,0:T(8,128)(2,1)S(1)} %maximum_select_fusion), channel_id=1, source_target_pairs={{0,968},{4,1020},{8,976},{12,964},{16,984},{20,972},{24,992},{28,9... | collective-permute-start | bytes 786440 | tf_op jit(solution)/shard_map/ppermute | solution.py:42
  47.6 23.6 %collective-permute-start.8 = (s16[144,1024]{1,0:T(8,128)(2,1)S(1)}, s16[144,1024]{1,0:T(8,128)(2,1)S(1)}, u32[]{:S(2)}, u32[]{:S(2)}) collective-permute-start(s16[144,1024]{1,0:T(8,128)(2,1)S(1)} %get-tuple-element.29), channel_id=1, source_target_pairs={{0,8},{4,60},{8,16},{12,4},{16,24},{20,12},{24,32},{28,20},{32,40}... | collective-permute-start | bytes 884744 | tf_op jit(solution)/shard_map/ppermute | solution.py:27
  52.7 18.5 %collective-permute-start.9 = (s16[144,1024]{1,0:T(8,128)(2,1)S(1)}, s16[144,1024]{1,0:T(8,128)(2,1)S(1)}, u32[]{:S(2)}, u32[]{:S(2)}) collective-permute-start(s16[144,1024]{1,0:T(8,128)(2,1)S(1)} %get-tuple-element.30), channel_id=1, source_target_pairs={{0,16},{4,52},{8,24},{12,60},{16,32},{20,4},{24,40},{28,12},{32,48... | collective-permute-start | bytes 884744 | tf_op jit(solution)/shard_map/ppermute | solution.py:27
  54.6 10.6 %collective-permute-start.5 = (bf16[128,1024]{1,0:T(8,128)(2,1)S(1)}, bf16[128,1024]{1,0:T(8,128)(2,1)S(1)}, u32[]{:S(2)}, u32[]{:S(2)}) collective-permute-start(bf16[128,1024]{1,0:T(8,128)(2,1)S(1)} %collective-permute-done.3.g2_ref), channel_id=1, source_target_pairs={{0,4},{4,0},{8,12},{12,8},{16,20},{20,16},{24,28},{28,24},{32,36},... | collective-permute-start | bytes 786440 | tf_op jit(solution)/shard_map/ppermute | solution.py:32
  58.4 12.7 %collective-permute-start.4 = (bf16[128,1024]{1,0:T(8,128)(2,1)S(1)}, bf16[128,1024]{1,0:T(8,128)(2,1)S(1)}, u32[]{:S(2)}, u32[]{:S(2)}) collective-permute-start(bf16[128,1024]{1,0:T(8,128)(2,1)S(1)} %collective-permute-done.1.g1_ref), channel_id=1, source_target_pairs={{0,4},{4,0},{8,12},{12,8},{16,20},{20,16},{24,28},{28,24},{32,36},... | collective-permute-start | bytes 786440 | tf_op jit(solution)/shard_map/ppermute | solution.py:32
  60.4 13.3 %collective-permute-start.12 = (bf16[128,1024]{1,0:T(8,128)(2,1)S(1)}, bf16[128,1024]{1,0:T(8,128)(2,1)S(1)}, u32[]{:S(2)}, u32[]{:S(2)}) collective-permute-start(bf16[128,1024]{1,0:T(8,128)(2,1)S(1)} %collective-permute-done.3.g2_ref), channel_id=1, source_target_pairs={{0,8},{4,60},{8,16},{12,4},{16,24},{20,12},{24,32},{28,20},{32,40}... | collective-permute-start | bytes 786440 | tf_op jit(solution)/shard_map/ppermute | solution.py:27
  65.2 5.9 %copy-start.2 = (bf16[1,4,128,512]{3,2,1,0:T(8,128)(2,1)S(1)}, bf16[1,4,128,512]{3,2,1,0:T(8,128)(2,1)}, u32[]{:S(2)}) copy-start(bf16[1,4,128,512]{3,2,1,0:T(8,128)(2,1)} %param.7) | copy-start | bytes 1572868
  65.3 8.4 %collective-permute-start.13 = (bf16[64,1024]{1,0:T(8,128)(2,1)S(1)}, bf16[64,1024]{1,0:T(8,128)(2,1)S(1)}, u32[]{:S(2)}, u32[]{:S(2)}) collective-permute-start(bf16[64,1024]{1,0:T(8,128)(2,1)S(1)} %slice_select_fusion), channel_id=1, source_target_pairs={{0,16},{4,52},{8,24},{12,60},{16,32},{20,4},{24,40},{28,12},{32,48... | collective-permute-start | bytes 393224 | tf_op jit(solution)/shard_map/ppermute | solution.py:27
  71.7 4.8 %collective-permute-start.10 = (f32[128,512]{1,0:T(8,128)S(1)}, f32[128,512]{1,0:T(8,128)S(1)}, u32[]{:S(2)}, u32[]{:S(2)}) collective-permute-start(f32[128,512]{1,0:T(8,128)S(1)} %get-tuple-element.33), channel_id=1, source_target_pairs={{0,4},{4,0},{8,12},{12,8},{16,20},{20,16},{24,28},{28,24},{32,36},... | collective-permute-start | bytes 786440 | tf_op jit(solution)/shard_map/ppermute | solution.py:32
  73.7 4.8 %collective-permute-start.14 = (bf16[192,1024]{1,0:T(8,128)(2,1)S(1)}, bf16[192,1024]{1,0:T(8,128)(2,1)S(1)}, u32[]{:S(2)}, u32[]{:S(2)}) collective-permute-start(bf16[192,1024]{1,0:T(8,128)(2,1)S(1)} %pad_maximum_fusion), channel_id=1, source_target_pairs={{0,4},{4,0},{8,12},{12,8},{16,20},{20,16},{24,28},{28,24},{32,36},... | collective-permute-start | bytes 1179656 | tf_op jit(solution)/shard_map/ppermute | solution.py:32
  76.6 9.1 %collective-permute-start.11 = (bf16[128,512]{1,0:T(8,128)(2,1)S(1)}, bf16[128,512]{1,0:T(8,128)(2,1)S(1)}, u32[]{:S(2)}, u32[]{:S(2)}) collective-permute-start(bf16[128,512]{1,0:T(8,128)(2,1)S(1)} %add_convert_fusion), channel_id=1, source_target_pairs={{0,64},{4,68},{8,72},{12,76},{16,80},{20,84},{24,88},{28,92},{32,9... | collective-permute-start | bytes 393224 | tf_op jit(solution)/shard_map/ppermute | solution.py:42

commit v5 on v4

--- a/solution.py
+++ b/solution.py
@@ -216,15 +216,15 @@
     )[0]
 
 
-def backproject_rest(place, h1, h2, h34, g3, g4, start, weights, chips):
+def backproject_rest(place, h12, h34, g3, g4, start, weights, chips):
     offsets = (1, 2, 3, -3, 4)
 
-    def body(place_ref, h1_ref, h2_ref, h34_ref, g3_ref, g4_ref, start_ref, w_ref, out_ref, facing, total):
+    def body(place_ref, h12_ref, h34_ref, g3_ref, g4_ref, start_ref, w_ref, out_ref, facing, total):
         core = place_ref[0] % 2
         facing[pl.ds(pl.multiple_of(core * HALF, HALF), HALF)] = g4_ref[...]
         facing[pl.ds(pl.multiple_of((1 - core) * HALF, HALF), HALF)] = h34_ref[ROWS:]
         total[...] = start_ref[...]
-        for slot, x in enumerate((h1_ref, h2_ref, h34_ref.at[:ROWS], g3_ref)):
+        for slot, x in enumerate((h12_ref.at[:ROWS], h12_ref.at[ROWS:], h34_ref.at[:ROWS], g3_ref)):
             total[...] += times_transposed(x[...], chunk_of_weights(w_ref, place_ref[0], offsets[slot], chips))
         last = times_transposed(facing[...], chunk_of_weights(w_ref, place_ref[0], offsets[4], chips))
         out_ref[...] = (total[...] + last).astype(BF16)
@@ -233,8 +233,8 @@
     return call(
         body,
         [((ROWS, heads), BF16)],
-        (place, h1, h2, h34, g3, g4, start, weights),
-        [SMEM] + [VMEM] * 7,
+        (place, h12, h34, g3, g4, start, weights),
+        [SMEM] + [VMEM] * 6,
         [
             pltpu.VMEM((ROWS, WIDE), BF16),
             pltpu.VMEM((ROWS, heads), F32),
@@ -249,14 +249,15 @@
     chips = lax.axis_size("tensor") // 2
     first = at % 2 == 0
 
-    send, keep3, keep2, keep1, keep4, own = project(place, plan, contexts, w_local, chips)
-    arrived = core_swap(send)
     mate = core_swap(upstream[0])
     pair = jnp.where(
         first, jnp.concatenate([upstream[0], mate], 1), jnp.concatenate([mate, upstream[0]], 1)
     )
-    after, pair = lax.optimization_barrier((place, pair))
-    q34 = split_shift(encode_first(after, keep3, keep4, arrived), 2)
+
+    begun, pair = lax.optimization_barrier((place, pair))
+    send, keep3, keep2, keep1, keep4, own = project(begun, plan, contexts, w_local, chips)
+    arrived = core_swap(send)
+    q34 = split_shift(encode_first(place, keep3, keep4, arrived), 2)
     q2, q1 = encode_two(place, keep2, keep1, arrived, q34)
     q2, q1 = split_shift(q2, 2), split_shift(q1, 1)
 
@@ -265,17 +266,15 @@
     g3 = split_shift(g2, 1)
     g4 = split_shift(jnp.where(first, g2[:HALF], g2[HALF:]), 2)
     g0 = next_section(pair, -1)
-    h2 = core_swap(g2)
-    to_mate, g0 = lax.optimization_barrier((g1, g0))
-    h1 = core_swap(to_mate)
+    h12 = core_swap(jnp.concatenate([g1, g2], 0))
     h34 = core_swap(jnp.concatenate([g3, g4], 0))
     early = backproject_first(place, (g0, g1, g2), w_local, chips)
 
-    after, _, _, _ = lax.optimization_barrier((place, early, h1, h2))
+    after, _, _ = lax.optimization_barrier((place, early, h12))
     send, part = gather_home(after, plan, q1, q2, own, arrived, residual)
     hidden = (part + core_swap(send)).astype(BF16)
     boundary = next_section(hidden, 1)
-    gradient = backproject_rest(place, h1, h2, h34, g3, g4, early, w_local, chips)
+    gradient = backproject_rest(place, h12, h34, g3, g4, early, w_local, chips)
     boundary, gradient = lax.optimization_barrier((boundary, gradient))
     return (boundary[None], gradient[None])
 

time: 87 us -> 86.8 us (level)
  waiting for transfers between devices: 12.5 us -> 23.7 us
  starting transfers between devices: 55.6 us -> 49 us
  local copies, waits for them, and re-layouts: 5.19 us -> 1.71 us
  Pallas kernels: 10.3 us -> 9.16 us
    ppermute x4, waiting for transfers between devices: 4.64 us -> 16.5 us  [next_section(): return lax.ppermute(value, ('section', 'tensor'), pairs)]
    ppermute x5, starting transfers between devices: 18.9 us -> 9.85 us  [split_shift(): return lax.ppermute(value, 'tensor', pairs)]
    unnamed x17 -> x9, local copies, waits for them, and re-layouts: 5.19 us -> 1.71 us
    ppermute x6 -> x5, starting transfers between devices: 28.5 us -> 31.4 us  [core_swap(): return lax.ppermute(value, 'tensor', [(i, i ^ 1) for i in range(peers)])]
    ppermute x6 -> x5, waiting for transfers between devices: 2.15 us -> 0.53 us  [core_swap(): return lax.ppermute(value, 'tensor', [(i, i ^ 1) for i in range(peers)])]
    pallas_call x6, Pallas kernels: 10.3 us -> 9.16 us  [call(): pl.pallas_call(body, grid=(1,), in_specs=specs, out_specs=[VMEM] * len(ou...]
    ppermute x5, waiting for transfers between devices: 5.73 us -> 6.7 us  [split_shift(): return lax.ppermute(value, 'tensor', pairs)]
  transfers between devices with their start and end apart: 15 -> 14, of which waited for: 3 -> 6; matrix products, arithmetic and copies ran while one was open for 1% -> 0% of each run, Pallas kernels for 5% -> 6%
where the time goes in v5:
time: 86.8 us; the launch traced here: 86.3 us
  starting transfers between devices  49 us (56%)
  waiting for transfers between devices  23.7 us (27%)
  Pallas kernels  9.16 us (11%)
  local copies, waits for them, and re-layouts  1.71 us (2%)
  between operations  1.59 us (2%)
  other arithmetic  1.16 us (1%)
    ppermute x5, starting transfers between devices, core_swap(): return lax.ppermute(value, 'tensor', [(i, i ^ 1) for i in range(peers)])  31.4 us
    ppermute x4, waiting for transfers between devices, next_section(): return lax.ppermute(value, ('section', 'tensor'), pairs)  16.5 us
    ppermute x5, starting transfers between devices, split_shift(): return lax.ppermute(value, 'tensor', pairs)  9.85 us
    pallas_call x6, Pallas kernels, call(): pl.pallas_call(body, grid=(1,), in_specs=specs, out_specs=[VMEM] * len(ou...  9.16 us
    ppermute x4, starting transfers between devices, next_section(): return lax.ppermute(value, ('section', 'tensor'), pairs)  7.68 us
    ppermute x5, waiting for transfers between devices, split_shift(): return lax.ppermute(value, 'tensor', pairs)  6.7 us
  transfers between devices with their start and end apart: 14, of which 6 were waited for; matrix products, arithmetic and copies ran while one was open for 0% of the time, Pallas kernels for 6%

profile of v5, /device:TPU:1, one launch (start us, length us, event | category | flops | bytes accessed | tf_op | source)
XLA Modules:
  0.0 86.3 jit_solution(17661488014938996271)
XLA Ops:
  0.6 16.1 %collective-permute-start = (bf16[128,512]{1,0:T(8,128)(2,1)}, bf16[128,512]{1,0:T(8,128)(2,1)S(1)}, u32[]{:S(2)}, u32[]{:S(2)}) collective-permute-start(bf16[128,512]{1,0:T(8,128)(2,1)} %bitcast.15), channel_id=1, source_target_pairs={{0,4},{4,0},{8,12},{12,8},{16,20},{20,16},{24,28},{28,24},{32,36},... | collective-permute-start | bytes 393224 | tf_op jit(solution)/shard_map/ppermute | solution.py:32
  17.4 0.5 collective-permute-done
  17.9 1.0 %maximum_select_fusion = bf16[128,1024]{1,0:T(8,128)(2,1)S(1)} fusion(bf16[128,512]{1,0:T(8,128)(2,1)S(1)} %collective-permute-done, bf16[128,512]{1,0:T(8,128)(2,1)} %bitcast.16, pred[]{:T(512)S(6)} %eq.5), kind=kLoop, calls=%fused_computation.2 | loop fusion | flops 1179648 | bytes 524289 | tf_op jit(solution)/shard_map/jit(_where)/select_n | solution.py:253
  18.9 0.0 copy-start
  18.9 1.0 %copy-done = bf16[1,4,128,512]{3,2,1,0:T(8,128)(2,1)S(1)} copy-done((bf16[1,4,128,512]{3,2,1,0:T(8,128)(2,1)S(1)}, bf16[1,4,128,512]{3,2,1,0:T(8,128)(2,1)}, u32[]{:S(2)}) %copy-start) | copy-done | bytes 524312
  20.0 4.3 %shard_map.69 = (f32[512,1024]{1,0:T(8,128)S(1)}, f32[128,1024]{1,0:T(8,128)S(1)}, f32[128,1024]{1,0:T(8,128)S(1)}, f32[128,1024]{1,0:T(8,128)S(1)}, f32[64,1024]{1,0:T(8,128)S(1)}, /*index=5*/f32[64,1024]{1,0:T(8,128)S(1)}) custom-call(s32[1]{0:T(128)} %bitcast.place_ref, s32[1]{0:T(128)S(6)} %copy.8.plan_ref, bf16[4,128,512]{2,1,0:T(8,128)(2,1)S(1)} %bitcast.12, ...), custom_call_target="tpu_custom_call" | custom-call | flops 1 | bytes 1 | tf_op jit(solution)/shard_map/pallas_call | solution.py:46
  24.2 2.3 %collective-permute-start.5 = (f32[512,1024]{1,0:T(8,128)S(1)}, f32[512,1024]{1,0:T(8,128)S(1)}, u32[]{:S(2)}, u32[]{:S(2)}) collective-permute-start(f32[512,1024]{1,0:T(8,128)S(1)} %get-tuple-element.22), channel_id=1, source_target_pairs={{0,4},{4,0},{8,12},{12,8},{16,20},{20,16},{24,28},{28,24},{32,36},... | collective-permute-start | bytes 6291464 | tf_op jit(solution)/shard_map/ppermute | solution.py:32
  26.5 1.9 %collective-permute-start.3 = (bf16[128,1024]{1,0:T(8,128)(2,1)S(1)}, bf16[128,1024]{1,0:T(8,128)(2,1)S(1)}, u32[]{:S(2)}, u32[]{:S(2)}) collective-permute-start(bf16[128,1024]{1,0:T(8,128)(2,1)S(1)} %maximum_select_fusion), channel_id=1, source_target_pairs={{0,976},{4,1012},{8,984},{12,1020},{16,992},{20,964},{24,1000},{28... | collective-permute-start | bytes 786440 | tf_op jit(solution)/shard_map/ppermute | solution.py:42
  28.4 1.9 %collective-permute-start.2 = (bf16[128,1024]{1,0:T(8,128)(2,1)S(1)}, bf16[128,1024]{1,0:T(8,128)(2,1)S(1)}, u32[]{:S(2)}, u32[]{:S(2)}) collective-permute-start(bf16[128,1024]{1,0:T(8,128)(2,1)S(1)} %maximum_select_fusion), channel_id=1, source_target_pairs={{0,968},{4,1020},{8,976},{12,964},{16,984},{20,972},{24,992},{28,9... | collective-permute-start | bytes 786440 | tf_op jit(solution)/shard_map/ppermute | solution.py:42
  30.4 0.0 slice-start.1
  30.4 0.2 shard_map.70
  30.6 2.2 %collective-permute-start.6 = (s16[224,1024]{1,0:T(8,128)(2,1)S(1)}, s16[224,1024]{1,0:T(8,128)(2,1)S(1)}, u32[]{:S(2)}, u32[]{:S(2)}) collective-permute-start(s16[224,1024]{1,0:T(8,128)(2,1)S(1)} %shard_map.70), channel_id=1, source_target_pairs={{0,16},{4,52},{8,24},{12,60},{16,32},{20,4},{24,40},{28,12},{32,48... | collective-permute-start | bytes 1376264 | tf_op jit(solution)/shard_map/ppermute | solution.py:27
  32.8 6.2 %collective-permute-done.3.g2_ref = bf16[128,1024]{1,0:T(8,128)(2,1)S(1)} collective-permute-done((bf16[128,1024]{1,0:T(8,128)(2,1)S(1)}, bf16[128,1024]{1,0:T(8,128)(2,1)S(1)}, u32[]{:S(2)}, u32[]{:S(2)}) %collective-permute-start.3) | collective-permute-done | bytes 262176 | tf_op jit(solution)/shard_map/ppermute | solution.py:42
  39.0 0.9 collective-permute-done.2.g1_ref
  39.9 3.1 %collective-permute-start.4 = (bf16[256,1024]{1,0:T(8,128)(2,1)S(1)}, bf16[256,1024]{1,0:T(8,128)(2,1)S(1)}, u32[]{:S(2)}, u32[]{:S(2)}) collective-permute-start(bf16[256,1024]{1,0:T(8,128)(2,1)S(1)} %pad_maximum_fusion), channel_id=1, source_target_pairs={{0,4},{4,0},{8,12},{12,8},{16,20},{20,16},{24,28},{28,24},{32,36},... | collective-permute-start | bytes 1572872 | tf_op jit(solution)/shard_map/ppermute | solution.py:32
  42.9 6.7 %collective-permute-done.6.q34_ref = s16[224,1024]{1,0:T(8,128)(2,1)S(1)} collective-permute-done((s16[224,1024]{1,0:T(8,128)(2,1)S(1)}, s16[224,1024]{1,0:T(8,128)(2,1)S(1)}, u32[]{:S(2)}, u32[]{:S(2)}) %collective-permute-start.6) | collective-permute-done | bytes 458784 | tf_op jit(solution)/shard_map/ppermute | solution.py:27
  49.6 0.5 shard_map.71
  50.1 1.9 %collective-permute-start.7 = (s16[144,1024]{1,0:T(8,128)(2,1)S(1)}, s16[144,1024]{1,0:T(8,128)(2,1)S(1)}, u32[]{:S(2)}, u32[]{:S(2)}) collective-permute-start(s16[144,1024]{1,0:T(8,128)(2,1)S(1)} %get-tuple-element.25), channel_id=1, source_target_pairs={{0,8},{4,60},{8,16},{12,4},{16,24},{20,12},{24,32},{28,20},{32,40}... | collective-permute-start | bytes 884744 | tf_op jit(solution)/shard_map/ppermute | solution.py:27
  52.0 1.9 %collective-permute-start.8 = (s16[144,1024]{1,0:T(8,128)(2,1)S(1)}, s16[144,1024]{1,0:T(8,128)(2,1)S(1)}, u32[]{:S(2)}, u32[]{:S(2)}) collective-permute-start(s16[144,1024]{1,0:T(8,128)(2,1)S(1)} %get-tuple-element.26), channel_id=1, source_target_pairs={{0,16},{4,52},{8,24},{12,60},{16,32},{20,4},{24,40},{28,12},{32,48... | collective-permute-start | bytes 884744 | tf_op jit(solution)/shard_map/ppermute | solution.py:27
  53.9 1.9 %collective-permute-start.1 = (bf16[128,1024]{1,0:T(8,128)(2,1)S(1)}, bf16[128,1024]{1,0:T(8,128)(2,1)S(1)}, u32[]{:S(2)}, u32[]{:S(2)}) collective-permute-start(bf16[128,1024]{1,0:T(8,128)(2,1)S(1)} %maximum_select_fusion), channel_id=1, source_target_pairs={{0,960},{4,964},{8,968},{12,972},{16,976},{20,980},{24,984},{28,98... | collective-permute-start | bytes 786440 | tf_op jit(solution)/shard_map/ppermute | solution.py:42
  55.9 1.9 %collective-permute-start.11 = (bf16[128,1024]{1,0:T(8,128)(2,1)S(1)}, bf16[128,1024]{1,0:T(8,128)(2,1)S(1)}, u32[]{:S(2)}, u32[]{:S(2)}) collective-permute-start(bf16[128,1024]{1,0:T(8,128)(2,1)S(1)} %collective-permute-done.3.g2_ref), channel_id=1, source_target_pairs={{0,8},{4,60},{8,16},{12,4},{16,24},{20,12},{24,32},{28,20},{32,40}... | collective-permute-start | bytes 786440 | tf_op jit(solution)/shard_map/ppermute | solution.py:27
  57.8 0.0 copy-start.1
  57.8 4.8 %collective-permute-done.1.u_ref = bf16[128,1024]{1,0:T(8,128)(2,1)S(1)} collective-permute-done((bf16[128,1024]{1,0:T(8,128)(2,1)S(1)}, bf16[128,1024]{1,0:T(8,128)(2,1)S(1)}, u32[]{:S(2)}, u32[]{:S(2)}) %collective-permute-start.1) | collective-permute-done | bytes 262176 | tf_op jit(solution)/shard_map/ppermute | solution.py:42
  62.7 1.9 %collective-permute-start.12 = (bf16[64,1024]{1,0:T(8,128)(2,1)S(1)}, bf16[64,1024]{1,0:T(8,128)(2,1)S(1)}, u32[]{:S(2)}, u32[]{:S(2)}) collective-permute-start(bf16[64,1024]{1,0:T(8,128)(2,1)S(1)} %slice_select_fusion), channel_id=1, source_target_pairs={{0,16},{4,52},{8,24},{12,60},{16,32},{20,4},{24,40},{28,12},{32,48... | collective-permute-start | bytes 393224 | tf_op jit(solution)/shard_map/ppermute | solution.py:27
  64.6 1.2 %shard_map.68.start_ref = f32[128,512]{1,0:T(8,128)S(1)} custom-call(s32[1]{0:T(128)} %bitcast.place_ref, bf16[128,1024]{1,0:T(8,128)(2,1)S(1)} %collective-permute-done.1.u_ref, bf16[128,1024]{1,0:T(8,128)(2,1)S(1)} %collective-permute-done.2.g1_ref, bf16[128,1024]{1,0:T(8,128)(2,1)S(1)} %collective-permute-done.3.g2_ref, bf16[512,8192]{1,0:T(8,128)(2,1)S(1)} %bitcast.10), custom_call_target="tpu_custom_call" | custom-call | flops 1 | bytes 1 | tf_op jit(solution)/shard_map/pallas_call | solution.py:46
  65.8 0.5 shard_map.72
  66.4 6.4 %collective-permute-start.9 = (f32[128,512]{1,0:T(8,128)S(1)}, f32[128,512]{1,0:T(8,128)S(1)}, u32[]{:S(2)}, u32[]{:S(2)}) collective-permute-start(f32[128,512]{1,0:T(8,128)S(1)} %get-tuple-element.29), channel_id=1, source_target_pairs={{0,4},{4,0},{8,12},{12,8},{16,20},{20,16},{24,28},{28,24},{32,36},... | collective-permute-start | bytes 786440 | tf_op jit(solution)/shard_map/ppermute | solution.py:32
  72.9 3.6 %collective-permute-start.13 = (bf16[192,1024]{1,0:T(8,128)(2,1)S(1)}, bf16[192,1024]{1,0:T(8,128)(2,1)S(1)}, u32[]{:S(2)}, u32[]{:S(2)}) collective-permute-start(bf16[192,1024]{1,0:T(8,128)(2,1)S(1)} %pad_maximum_fusion.1), channel_id=1, source_target_pairs={{0,4},{4,0},{8,12},{12,8},{16,20},{20,16},{24,28},{28,24},{32,36},... | collective-permute-start | bytes 1179656 | tf_op jit(solution)/shard_map/ppermute | solution.py:32
  76.5 1.9 %collective-permute-start.10 = (bf16[128,512]{1,0:T(8,128)(2,1)S(1)}, bf16[128,512]{1,0:T(8,128)(2,1)S(1)}, u32[]{:S(2)}, u32[]{:S(2)}) collective-permute-start(bf16[128,512]{1,0:T(8,128)(2,1)S(1)} %add_convert_fusion), channel_id=1, source_target_pairs={{0,64},{4,68},{8,72},{12,76},{16,80},{20,84},{24,88},{28,92},{32,9... | collective-permute-start | bytes 393224 | tf_op jit(solution)/shard_map/ppermute | solution.py:42
  78.5 2.5 %shard_map.73 = bf16[128,512]{1,0:T(8,128)(2,1)} custom-call(s32[1]{0:T(128)} %bitcast.place_ref, bf16[256,1024]{1,0:T(8,128)(2,1)S(1)} %collective-permute-done.4.h12_ref, bf16[192,1024]{1,0:T(8,128)(2,1)S(1)} %collective-permute-done.13.h34_ref, bf16[128,1024]{1,0:T(8,128)(2,1)S(1)} %collective-permute-done.11.g3_ref, ...), custom_call_target="tpu_custom_call" | custom-call | flops 1 | bytes 1 | tf_op jit(solution)/shard_map/pallas_call | solution.py:46
  81.0 4.6 %collective-permute-done.10 = bf16[128,512]{1,0:T(8,128)(2,1)S(1)} collective-permute-done((bf16[128,512]{1,0:T(8,128)(2,1)S(1)}, bf16[128,512]{1,0:T(8,128)(2,1)S(1)}, u32[]{:S(2)}, u32[]{:S(2)}) %collective-permute-start.10) | collective-permute-done | bytes 131104 | tf_op jit(solution)/shard_map/ppermute | solution.py:42
  85.6 0.7 copy.9
  (17 shorter events, 0.1 us)
Async XLA Ops:
  0.6 17.2 %collective-permute-start = (bf16[128,512]{1,0:T(8,128)(2,1)}, bf16[128,512]{1,0:T(8,128)(2,1)S(1)}, u32[]{:S(2)}, u32[]{:S(2)}) collective-permute-start(bf16[128,512]{1,0:T(8,128)(2,1)} %bitcast.15), channel_id=1, source_target_pairs={{0,4},{4,0},{8,12},{12,8},{16,20},{20,16},{24,28},{28,24},{32,36},... | collective-permute-start | bytes 393224 | tf_op jit(solution)/shard_map/ppermute | solution.py:32
  18.9 1.0 %copy-start = (bf16[1,4,128,512]{3,2,1,0:T(8,128)(2,1)S(1)}, bf16[1,4,128,512]{3,2,1,0:T(8,128)(2,1)}, u32[]{:S(2)}) copy-start(bf16[1,4,128,512]{3,2,1,0:T(8,128)(2,1)} %param.6) | copy-start | bytes 1572868
  20.0 44.6 %slice-start = ((s8[8388608]{0:T(1024)(128)(4,1)}), s8[4194304]{0:T(1024)(128)(4,1)S(1)}, s32[]{:S(2)}) async-start(s8[8388608]{0:T(1024)(128)(4,1)} %bitcast.8), calls=%async_computation | async-start | bytes 8388608
  24.2 6.1 %collective-permute-start.5 = (f32[512,1024]{1,0:T(8,128)S(1)}, f32[512,1024]{1,0:T(8,128)S(1)}, u32[]{:S(2)}, u32[]{:S(2)}) collective-permute-start(f32[512,1024]{1,0:T(8,128)S(1)} %get-tuple-element.22), channel_id=1, source_target_pairs={{0,4},{4,0},{8,12},{12,8},{16,20},{20,16},{24,28},{28,24},{32,36},... | collective-permute-start | bytes 6291464 | tf_op jit(solution)/shard_map/ppermute | solution.py:32
  26.5 12.5 %collective-permute-start.3 = (bf16[128,1024]{1,0:T(8,128)(2,1)S(1)}, bf16[128,1024]{1,0:T(8,128)(2,1)S(1)}, u32[]{:S(2)}, u32[]{:S(2)}) collective-permute-start(bf16[128,1024]{1,0:T(8,128)(2,1)S(1)} %maximum_select_fusion), channel_id=1, source_target_pairs={{0,976},{4,1012},{8,984},{12,1020},{16,992},{20,964},{24,1000},{28... | collective-permute-start | bytes 786440 | tf_op jit(solution)/shard_map/ppermute | solution.py:42
  28.4 11.4 %collective-permute-start.2 = (bf16[128,1024]{1,0:T(8,128)(2,1)S(1)}, bf16[128,1024]{1,0:T(8,128)(2,1)S(1)}, u32[]{:S(2)}, u32[]{:S(2)}) collective-permute-start(bf16[128,1024]{1,0:T(8,128)(2,1)S(1)} %maximum_select_fusion), channel_id=1, source_target_pairs={{0,968},{4,1020},{8,976},{12,964},{16,984},{20,972},{24,992},{28,9... | collective-permute-start | bytes 786440 | tf_op jit(solution)/shard_map/ppermute | solution.py:42
  30.4 34.2 %slice-start.1 = ((s8[8388608]{0:T(1024)(128)(4,1)}), s8[4194304]{0:T(1024)(128)(4,1)S(1)}, s32[]{:S(2)}) async-start(s8[8388608]{0:T(1024)(128)(4,1)} %bitcast.8), calls=%async_computation.1 | async-start | bytes 8388608
  30.6 19.0 %collective-permute-start.6 = (s16[224,1024]{1,0:T(8,128)(2,1)S(1)}, s16[224,1024]{1,0:T(8,128)(2,1)S(1)}, u32[]{:S(2)}, u32[]{:S(2)}) collective-permute-start(s16[224,1024]{1,0:T(8,128)(2,1)S(1)} %shard_map.70), channel_id=1, source_target_pairs={{0,16},{4,52},{8,24},{12,60},{16,32},{20,4},{24,40},{28,12},{32,48... | collective-permute-start | bytes 1376264 | tf_op jit(solution)/shard_map/ppermute | solution.py:27
  39.9 25.9 %collective-permute-start.4 = (bf16[256,1024]{1,0:T(8,128)(2,1)S(1)}, bf16[256,1024]{1,0:T(8,128)(2,1)S(1)}, u32[]{:S(2)}, u32[]{:S(2)}) collective-permute-start(bf16[256,1024]{1,0:T(8,128)(2,1)S(1)} %pad_maximum_fusion), channel_id=1, source_target_pairs={{0,4},{4,0},{8,12},{12,8},{16,20},{20,16},{24,28},{28,24},{32,36},... | collective-permute-start | bytes 1572872 | tf_op jit(solution)/shard_map/ppermute | solution.py:32
  50.1 15.7 %collective-permute-start.7 = (s16[144,1024]{1,0:T(8,128)(2,1)S(1)}, s16[144,1024]{1,0:T(8,128)(2,1)S(1)}, u32[]{:S(2)}, u32[]{:S(2)}) collective-permute-start(s16[144,1024]{1,0:T(8,128)(2,1)S(1)} %get-tuple-element.25), channel_id=1, source_target_pairs={{0,8},{4,60},{8,16},{12,4},{16,24},{20,12},{24,32},{28,20},{32,40}... | collective-permute-start | bytes 884744 | tf_op jit(solution)/shard_map/ppermute | solution.py:27
  52.0 13.8 %collective-permute-start.8 = (s16[144,1024]{1,0:T(8,128)(2,1)S(1)}, s16[144,1024]{1,0:T(8,128)(2,1)S(1)}, u32[]{:S(2)}, u32[]{:S(2)}) collective-permute-start(s16[144,1024]{1,0:T(8,128)(2,1)S(1)} %get-tuple-element.26), channel_id=1, source_target_pairs={{0,16},{4,52},{8,24},{12,60},{16,32},{20,4},{24,40},{28,12},{32,48... | collective-permute-start | bytes 884744 | tf_op jit(solution)/shard_map/ppermute | solution.py:27
  53.9 8.7 %collective-permute-start.1 = (bf16[128,1024]{1,0:T(8,128)(2,1)S(1)}, bf16[128,1024]{1,0:T(8,128)(2,1)S(1)}, u32[]{:S(2)}, u32[]{:S(2)}) collective-permute-start(bf16[128,1024]{1,0:T(8,128)(2,1)S(1)} %maximum_select_fusion), channel_id=1, source_target_pairs={{0,960},{4,964},{8,968},{12,972},{16,976},{20,980},{24,984},{28,98... | collective-permute-start | bytes 786440 | tf_op jit(solution)/shard_map/ppermute | solution.py:42
  55.9 16.9 %collective-permute-start.11 = (bf16[128,1024]{1,0:T(8,128)(2,1)S(1)}, bf16[128,1024]{1,0:T(8,128)(2,1)S(1)}, u32[]{:S(2)}, u32[]{:S(2)}) collective-permute-start(bf16[128,1024]{1,0:T(8,128)(2,1)S(1)} %collective-permute-done.3.g2_ref), channel_id=1, source_target_pairs={{0,8},{4,60},{8,16},{12,4},{16,24},{20,12},{24,32},{28,20},{32,40}... | collective-permute-start | bytes 786440 | tf_op jit(solution)/shard_map/ppermute | solution.py:27
  57.8 8.0 %copy-start.1 = (bf16[1,4,128,512]{3,2,1,0:T(8,128)(2,1)S(1)}, bf16[1,4,128,512]{3,2,1,0:T(8,128)(2,1)}, u32[]{:S(2)}) copy-start(bf16[1,4,128,512]{3,2,1,0:T(8,128)(2,1)} %param.7) | copy-start | bytes 1572868
  62.7 10.2 %collective-permute-start.12 = (bf16[64,1024]{1,0:T(8,128)(2,1)S(1)}, bf16[64,1024]{1,0:T(8,128)(2,1)S(1)}, u32[]{:S(2)}, u32[]{:S(2)}) collective-permute-start(bf16[64,1024]{1,0:T(8,128)(2,1)S(1)} %slice_select_fusion), channel_id=1, source_target_pairs={{0,16},{4,52},{8,24},{12,60},{16,32},{20,4},{24,40},{28,12},{32,48... | collective-permute-start | bytes 393224 | tf_op jit(solution)/shard_map/ppermute | solution.py:27
  66.4 10.1 %collective-permute-start.9 = (f32[128,512]{1,0:T(8,128)S(1)}, f32[128,512]{1,0:T(8,128)S(1)}, u32[]{:S(2)}, u32[]{:S(2)}) collective-permute-start(f32[128,512]{1,0:T(8,128)S(1)} %get-tuple-element.29), channel_id=1, source_target_pairs={{0,4},{4,0},{8,12},{12,8},{16,20},{20,16},{24,28},{28,24},{32,36},... | collective-permute-start | bytes 786440 | tf_op jit(solution)/shard_map/ppermute | solution.py:32
  72.9 5.6 %collective-permute-start.13 = (bf16[192,1024]{1,0:T(8,128)(2,1)S(1)}, bf16[192,1024]{1,0:T(8,128)(2,1)S(1)}, u32[]{:S(2)}, u32[]{:S(2)}) collective-permute-start(bf16[192,1024]{1,0:T(8,128)(2,1)S(1)} %pad_maximum_fusion.1), channel_id=1, source_target_pairs={{0,4},{4,0},{8,12},{12,8},{16,20},{20,16},{24,28},{28,24},{32,36},... | collective-permute-start | bytes 1179656 | tf_op jit(solution)/shard_map/ppermute | solution.py:32
  76.5 9.1 %collective-permute-start.10 = (bf16[128,512]{1,0:T(8,128)(2,1)S(1)}, bf16[128,512]{1,0:T(8,128)(2,1)S(1)}, u32[]{:S(2)}, u32[]{:S(2)}) collective-permute-start(bf16[128,512]{1,0:T(8,128)(2,1)S(1)} %add_convert_fusion), channel_id=1, source_target_pairs={{0,64},{4,68},{8,72},{12,76},{16,80},{20,84},{24,88},{28,92},{32,9... | collective-permute-start | bytes 393224 | tf_op jit(solution)/shard_map/ppermute | solution.py:42

commit v6 on v4

--- a/solution.py
+++ b/solution.py
@@ -249,26 +249,25 @@
     chips = lax.axis_size("tensor") // 2
     first = at % 2 == 0
 
-    send, keep3, keep2, keep1, keep4, own = project(place, plan, contexts, w_local, chips)
-    arrived = core_swap(send)
     mate = core_swap(upstream[0])
     pair = jnp.where(
         first, jnp.concatenate([upstream[0], mate], 1), jnp.concatenate([mate, upstream[0]], 1)
     )
-    after, pair = lax.optimization_barrier((place, pair))
-    q34 = split_shift(encode_first(after, keep3, keep4, arrived), 2)
+
+    begun, pair = lax.optimization_barrier((place, pair))
+    send, keep3, keep2, keep1, keep4, own = project(begun, plan, contexts, w_local, chips)
+    arrived = core_swap(send)
+    q34 = split_shift(encode_first(place, keep3, keep4, arrived), 2)
     q2, q1 = encode_two(place, keep2, keep1, arrived, q34)
     q2, q1 = split_shift(q2, 2), split_shift(q1, 1)
 
+    g0 = next_section(pair, -1)
     g1 = next_section(pair, -1, 1)
-    g2 = next_section(pair, -1, 2)
+    g2 = split_shift(g1, 1)
     g3 = split_shift(g2, 1)
     g4 = split_shift(jnp.where(first, g2[:HALF], g2[HALF:]), 2)
-    g0 = next_section(pair, -1)
-    h2 = core_swap(g2)
     to_mate, g0 = lax.optimization_barrier((g1, g0))
-    h1 = core_swap(to_mate)
-    h34 = core_swap(jnp.concatenate([g3, g4], 0))
+    h1, h2, h34 = core_swap(to_mate), core_swap(g2), core_swap(jnp.concatenate([g3, g4], 0))
     early = backproject_first(place, (g0, g1, g2), w_local, chips)
 
     after, _, _, _ = lax.optimization_barrier((place, early, h1, h2))

time: 87 us -> 80.1 us (0.921)
  local copies, waits for them, and re-layouts: 5.19 us -> 1.71 us
  starting transfers between devices: 55.6 us -> 54.2 us
  Pallas kernels: 10.3 us -> 9.16 us
    unnamed x17 -> x9, local copies, waits for them, and re-layouts: 5.19 us -> 1.71 us
    ppermute x4 -> x3, starting transfers between devices: 8.24 us -> 5.76 us  [next_section(): return lax.ppermute(value, ('section', 'tensor'), pairs)]
    ppermute x5 -> x6, waiting for transfers between devices: 5.73 us -> 4.48 us  [split_shift(): return lax.ppermute(value, 'tensor', pairs)]
    pallas_call x6, Pallas kernels: 10.3 us -> 9.16 us  [call(): pl.pallas_call(body, grid=(1,), in_specs=specs, out_specs=[VMEM] * len(ou...]
    ppermute x5 -> x6, starting transfers between devices: 18.9 us -> 19.9 us  [split_shift(): return lax.ppermute(value, 'tensor', pairs)]
    ppermute x4 -> x3, waiting for transfers between devices: 4.64 us -> 4.89 us  [next_section(): return lax.ppermute(value, ('section', 'tensor'), pairs)]
  transfers between devices with their start and end apart: 15 -> 15, of which waited for: 3 -> 5; matrix products, arithmetic and copies ran while one was open for 1% -> 0% of each run, Pallas kernels for 5% -> 6%
where the time goes in v6:
time: 80.1 us; the launch traced here: 79.5 us
  starting transfers between devices  54.2 us (68%)
  waiting for transfers between devices  11.7 us (15%)
  Pallas kernels  9.16 us (11%)
  local copies, waits for them, and re-layouts  1.71 us (2%)
  between operations  1.59 us (2%)
  other arithmetic  1.13 us (1%)
    ppermute x6, starting transfers between devices, core_swap(): return lax.ppermute(value, 'tensor', [(i, i ^ 1) for i in range(peers)])  28.5 us
    ppermute x6, starting transfers between devices, split_shift(): return lax.ppermute(value, 'tensor', pairs)  19.9 us
    pallas_call x6, Pallas kernels, call(): pl.pallas_call(body, grid=(1,), in_specs=specs, out_specs=[VMEM] * len(ou...  9.16 us
    ppermute x3, starting transfers between devices, next_section(): return lax.ppermute(value, ('section', 'tensor'), pairs)  5.76 us
    ppermute x3, waiting for transfers between devices, next_section(): return lax.ppermute(value, ('section', 'tensor'), pairs)  4.89 us
    ppermute x6, waiting for transfers between devices, split_shift(): return lax.ppermute(value, 'tensor', pairs)  4.48 us
    ppermute x6, waiting for transfers between devices, core_swap(): return lax.ppermute(value, 'tensor', [(i, i ^ 1) for i in range(peers)])  2.37 us
    unnamed x9, local copies, waits for them, and re-layouts  1.71 us
  transfers between devices with their start and end apart: 15, of which 5 were waited for; matrix products, arithmetic and copies ran while one was open for 0% of the time, Pallas kernels for 6%

profile of v6, /device:TPU:1, one launch (start us, length us, event | category | flops | bytes accessed | tf_op | source)
XLA Modules:
  0.0 79.5 jit_solution(9391777252493458563)
XLA Ops:
  0.6 16.1 %collective-permute-start = (bf16[128,512]{1,0:T(8,128)(2,1)}, bf16[128,512]{1,0:T(8,128)(2,1)S(1)}, u32[]{:S(2)}, u32[]{:S(2)}) collective-permute-start(bf16[128,512]{1,0:T(8,128)(2,1)} %bitcast.15), channel_id=1, source_target_pairs={{0,4},{4,0},{8,12},{12,8},{16,20},{20,16},{24,28},{28,24},{32,36},... | collective-permute-start | bytes 393224 | tf_op jit(solution)/shard_map/ppermute | solution.py:32
  17.4 0.5 collective-permute-done
  17.9 1.0 %maximum_select_fusion = bf16[128,1024]{1,0:T(8,128)(2,1)S(1)} fusion(bf16[128,512]{1,0:T(8,128)(2,1)S(1)} %collective-permute-done, bf16[128,512]{1,0:T(8,128)(2,1)} %bitcast.16, pred[]{:T(512)S(6)} %eq.5), kind=kLoop, calls=%fused_computation.1 | loop fusion | flops 1179648 | bytes 524289 | tf_op jit(solution)/shard_map/jit(_where)/select_n | solution.py:253
  18.9 0.0 copy-start
  18.9 1.0 %copy-done = bf16[1,4,128,512]{3,2,1,0:T(8,128)(2,1)S(1)} copy-done((bf16[1,4,128,512]{3,2,1,0:T(8,128)(2,1)S(1)}, bf16[1,4,128,512]{3,2,1,0:T(8,128)(2,1)}, u32[]{:S(2)}) %copy-start) | copy-done | bytes 524312
  20.0 4.3 %shard_map.69 = (f32[512,1024]{1,0:T(8,128)S(1)}, f32[128,1024]{1,0:T(8,128)S(1)}, f32[128,1024]{1,0:T(8,128)S(1)}, f32[128,1024]{1,0:T(8,128)S(1)}, f32[64,1024]{1,0:T(8,128)S(1)}, /*index=5*/f32[64,1024]{1,0:T(8,128)S(1)}) custom-call(s32[1]{0:T(128)} %bitcast.place_ref, s32[1]{0:T(128)S(6)} %copy.8.plan_ref, bf16[4,128,512]{2,1,0:T(8,128)(2,1)S(1)} %bitcast.12, ...), custom_call_target="tpu_custom_call" | custom-call | flops 1 | bytes 1 | tf_op jit(solution)/shard_map/pallas_call | solution.py:46
  24.2 2.3 %collective-permute-start.6 = (f32[512,1024]{1,0:T(8,128)S(1)}, f32[512,1024]{1,0:T(8,128)S(1)}, u32[]{:S(2)}, u32[]{:S(2)}) collective-permute-start(f32[512,1024]{1,0:T(8,128)S(1)} %get-tuple-element.26), channel_id=1, source_target_pairs={{0,4},{4,0},{8,12},{12,8},{16,20},{20,16},{24,28},{28,24},{32,36},... | collective-permute-start | bytes 6291464 | tf_op jit(solution)/shard_map/ppermute | solution.py:32
  26.5 1.9 %collective-permute-start.1 = (bf16[128,1024]{1,0:T(8,128)(2,1)S(1)}, bf16[128,1024]{1,0:T(8,128)(2,1)S(1)}, u32[]{:S(2)}, u32[]{:S(2)}) collective-permute-start(bf16[128,1024]{1,0:T(8,128)(2,1)S(1)} %maximum_select_fusion), channel_id=1, source_target_pairs={{0,968},{4,1020},{8,976},{12,964},{16,984},{20,972},{24,992},{28,9... | collective-permute-start | bytes 786440 | tf_op jit(solution)/shard_map/ppermute | solution.py:42
  28.4 1.8 %collective-permute-done.6.in3_ref.in4_ref.in2_ref.in1_ref.in_ref = f32[512,1024]{1,0:T(8,128)S(1)} collective-permute-done((f32[512,1024]{1,0:T(8,128)S(1)}, f32[512,1024]{1,0:T(8,128)S(1)}, u32[]{:S(2)}, u32[]{:S(2)}) %collective-permute-start.6) | collective-permute-done | bytes 2097184 | tf_op jit(solution)/shard_map/ppermute | solution.py:32
  30.3 0.2 shard_map.70
  30.5 2.2 %collective-permute-start.7 = (s16[224,1024]{1,0:T(8,128)(2,1)S(1)}, s16[224,1024]{1,0:T(8,128)(2,1)S(1)}, u32[]{:S(2)}, u32[]{:S(2)}) collective-permute-start(s16[224,1024]{1,0:T(8,128)(2,1)S(1)} %shard_map.70), channel_id=1, source_target_pairs={{0,16},{4,52},{8,24},{12,60},{16,32},{20,4},{24,40},{28,12},{32,48... | collective-permute-start | bytes 1376264 | tf_op jit(solution)/shard_map/ppermute | solution.py:27
  32.7 1.9 %collective-permute-start.2 = (bf16[128,1024]{1,0:T(8,128)(2,1)S(1)}, bf16[128,1024]{1,0:T(8,128)(2,1)S(1)}, u32[]{:S(2)}, u32[]{:S(2)}) collective-permute-start(bf16[128,1024]{1,0:T(8,128)(2,1)S(1)} %maximum_select_fusion), channel_id=1, source_target_pairs={{0,960},{4,964},{8,968},{12,972},{16,976},{20,980},{24,984},{28,98... | collective-permute-start | bytes 786440 | tf_op jit(solution)/shard_map/ppermute | solution.py:42
  34.6 0.3 collective-permute-done.1.g1_ref
  34.9 1.9 %collective-permute-start.3 = (bf16[128,1024]{1,0:T(8,128)(2,1)S(1)}, bf16[128,1024]{1,0:T(8,128)(2,1)S(1)}, u32[]{:S(2)}, u32[]{:S(2)}) collective-permute-start(bf16[128,1024]{1,0:T(8,128)(2,1)S(1)} %collective-permute-done.1.g1_ref), channel_id=1, source_target_pairs={{0,8},{4,60},{8,16},{12,4},{16,24},{20,12},{24,32},{28,20},{32,40}... | collective-permute-start | bytes 786440 | tf_op jit(solution)/shard_map/ppermute | solution.py:27
  36.8 4.4 %collective-permute-done.7.q34_ref = s16[224,1024]{1,0:T(8,128)(2,1)S(1)} collective-permute-done((s16[224,1024]{1,0:T(8,128)(2,1)S(1)}, s16[224,1024]{1,0:T(8,128)(2,1)S(1)}, u32[]{:S(2)}, u32[]{:S(2)}) %collective-permute-start.7) | collective-permute-done | bytes 458784 | tf_op jit(solution)/shard_map/ppermute | solution.py:27
  41.2 0.5 shard_map.71
  41.7 6.1 %collective-permute-start.8 = (s16[144,1024]{1,0:T(8,128)(2,1)S(1)}, s16[144,1024]{1,0:T(8,128)(2,1)S(1)}, u32[]{:S(2)}, u32[]{:S(2)}) collective-permute-start(s16[144,1024]{1,0:T(8,128)(2,1)S(1)} %get-tuple-element.29), channel_id=1, source_target_pairs={{0,8},{4,60},{8,16},{12,4},{16,24},{20,12},{24,32},{28,20},{32,40}... | collective-permute-start | bytes 884744 | tf_op jit(solution)/shard_map/ppermute | solution.py:27
  47.8 1.9 %collective-permute-start.9 = (s16[144,1024]{1,0:T(8,128)(2,1)S(1)}, s16[144,1024]{1,0:T(8,128)(2,1)S(1)}, u32[]{:S(2)}, u32[]{:S(2)}) collective-permute-start(s16[144,1024]{1,0:T(8,128)(2,1)S(1)} %get-tuple-element.30), channel_id=1, source_target_pairs={{0,16},{4,52},{8,24},{12,60},{16,32},{20,4},{24,40},{28,12},{32,48... | collective-permute-start | bytes 884744 | tf_op jit(solution)/shard_map/ppermute | solution.py:27
  49.8 1.9 %collective-permute-start.4 = (bf16[128,1024]{1,0:T(8,128)(2,1)S(1)}, bf16[128,1024]{1,0:T(8,128)(2,1)S(1)}, u32[]{:S(2)}, u32[]{:S(2)}) collective-permute-start(bf16[128,1024]{1,0:T(8,128)(2,1)S(1)} %collective-permute-done.1.g1_ref), channel_id=1, source_target_pairs={{0,4},{4,0},{8,12},{12,8},{16,20},{20,16},{24,28},{28,24},{32,36},... | collective-permute-start | bytes 786440 | tf_op jit(solution)/shard_map/ppermute | solution.py:32
  51.7 2.4 %collective-permute-start.5 = (bf16[128,1024]{1,0:T(8,128)(2,1)S(1)}, bf16[128,1024]{1,0:T(8,128)(2,1)S(1)}, u32[]{:S(2)}, u32[]{:S(2)}) collective-permute-start(bf16[128,1024]{1,0:T(8,128)(2,1)S(1)} %collective-permute-done.3.g2_ref), channel_id=1, source_target_pairs={{0,4},{4,0},{8,12},{12,8},{16,20},{20,16},{24,28},{28,24},{32,36},... | collective-permute-start | bytes 786440 | tf_op jit(solution)/shard_map/ppermute | solution.py:32
  54.1 3.1 %collective-permute-start.12 = (bf16[128,1024]{1,0:T(8,128)(2,1)S(1)}, bf16[128,1024]{1,0:T(8,128)(2,1)S(1)}, u32[]{:S(2)}, u32[]{:S(2)}) collective-permute-start(bf16[128,1024]{1,0:T(8,128)(2,1)S(1)} %collective-permute-done.3.g2_ref), channel_id=1, source_target_pairs={{0,8},{4,60},{8,16},{12,4},{16,24},{20,12},{24,32},{28,20},{32,40}... | collective-permute-start | bytes 786440 | tf_op jit(solution)/shard_map/ppermute | solution.py:27
  57.2 0.0 copy-start.1
  57.3 4.7 %collective-permute-start.13 = (bf16[64,1024]{1,0:T(8,128)(2,1)S(1)}, bf16[64,1024]{1,0:T(8,128)(2,1)S(1)}, u32[]{:S(2)}, u32[]{:S(2)}) collective-permute-start(bf16[64,1024]{1,0:T(8,128)(2,1)S(1)} %slice_select_fusion), channel_id=1, source_target_pairs={{0,16},{4,52},{8,24},{12,60},{16,32},{20,4},{24,40},{28,12},{32,48... | collective-permute-start | bytes 393224 | tf_op jit(solution)/shard_map/ppermute | solution.py:27
  62.0 1.2 %shard_map.68.start_ref = f32[128,512]{1,0:T(8,128)S(1)} custom-call(s32[1]{0:T(128)} %bitcast.place_ref, bf16[128,1024]{1,0:T(8,128)(2,1)S(1)} %collective-permute-done.2.u_ref, bf16[128,1024]{1,0:T(8,128)(2,1)S(1)} %collective-permute-done.1.g1_ref, bf16[128,1024]{1,0:T(8,128)(2,1)S(1)} %collective-permute-done.3.g2_ref, bf16[512,8192]{1,0:T(8,128)(2,1)S(1)} %bitcast.10), custom_call_target="tpu_custom_call" | custom-call | flops 1 | bytes 1 | tf_op jit(solution)/shard_map/pallas_call | solution.py:46
  63.2 0.5 shard_map.72
  63.7 1.9 %collective-permute-start.10 = (f32[128,512]{1,0:T(8,128)S(1)}, f32[128,512]{1,0:T(8,128)S(1)}, u32[]{:S(2)}, u32[]{:S(2)}) collective-permute-start(f32[128,512]{1,0:T(8,128)S(1)} %get-tuple-element.33), channel_id=1, source_target_pairs={{0,4},{4,0},{8,12},{12,8},{16,20},{20,16},{24,28},{28,24},{32,36},... | collective-permute-start | bytes 786440 | tf_op jit(solution)/shard_map/ppermute | solution.py:32
  65.7 0.0 collective-permute-done.13.g4_ref
  65.7 3.9 %collective-permute-start.14 = (bf16[192,1024]{1,0:T(8,128)(2,1)S(1)}, bf16[192,1024]{1,0:T(8,128)(2,1)S(1)}, u32[]{:S(2)}, u32[]{:S(2)}) collective-permute-start(bf16[192,1024]{1,0:T(8,128)(2,1)S(1)} %pad_maximum_fusion), channel_id=1, source_target_pairs={{0,4},{4,0},{8,12},{12,8},{16,20},{20,16},{24,28},{28,24},{32,36},... | collective-permute-start | bytes 1179656 | tf_op jit(solution)/shard_map/ppermute | solution.py:32
  69.7 1.9 %collective-permute-start.11 = (bf16[128,512]{1,0:T(8,128)(2,1)S(1)}, bf16[128,512]{1,0:T(8,128)(2,1)S(1)}, u32[]{:S(2)}, u32[]{:S(2)}) collective-permute-start(bf16[128,512]{1,0:T(8,128)(2,1)S(1)} %add_convert_fusion), channel_id=1, source_target_pairs={{0,64},{4,68},{8,72},{12,76},{16,80},{20,84},{24,88},{28,92},{32,9... | collective-permute-start | bytes 393224 | tf_op jit(solution)/shard_map/ppermute | solution.py:42
  71.7 2.5 %shard_map.73 = bf16[128,512]{1,0:T(8,128)(2,1)} custom-call(s32[1]{0:T(128)} %bitcast.place_ref, bf16[128,1024]{1,0:T(8,128)(2,1)S(1)} %collective-permute-done.4.h1_ref, bf16[128,1024]{1,0:T(8,128)(2,1)S(1)} %collective-permute-done.5.h2_ref, bf16[192,1024]{1,0:T(8,128)(2,1)S(1)} %collective-permute-done.14.h34_ref, ...), custom_call_target="tpu_custom_call" | custom-call | flops 1 | bytes 1 | tf_op jit(solution)/shard_map/pallas_call | solution.py:46
  74.2 4.6 %collective-permute-done.11 = bf16[128,512]{1,0:T(8,128)(2,1)S(1)} collective-permute-done((bf16[128,512]{1,0:T(8,128)(2,1)S(1)}, bf16[128,512]{1,0:T(8,128)(2,1)S(1)}, u32[]{:S(2)}, u32[]{:S(2)}) %collective-permute-start.11) | collective-permute-done | bytes 131104 | tf_op jit(solution)/shard_map/ppermute | solution.py:42
  78.9 0.7 copy.9
  (18 shorter events, 0.1 us)
Async XLA Ops:
  0.6 17.2 %collective-permute-start = (bf16[128,512]{1,0:T(8,128)(2,1)}, bf16[128,512]{1,0:T(8,128)(2,1)S(1)}, u32[]{:S(2)}, u32[]{:S(2)}) collective-permute-start(bf16[128,512]{1,0:T(8,128)(2,1)} %bitcast.15), channel_id=1, source_target_pairs={{0,4},{4,0},{8,12},{12,8},{16,20},{20,16},{24,28},{28,24},{32,36},... | collective-permute-start | bytes 393224 | tf_op jit(solution)/shard_map/ppermute | solution.py:32
  18.9 1.0 %copy-start = (bf16[1,4,128,512]{3,2,1,0:T(8,128)(2,1)S(1)}, bf16[1,4,128,512]{3,2,1,0:T(8,128)(2,1)}, u32[]{:S(2)}) copy-start(bf16[1,4,128,512]{3,2,1,0:T(8,128)(2,1)} %param.6) | copy-start | bytes 1572868
  20.0 42.0 %slice-start = ((s8[8388608]{0:T(1024)(128)(4,1)}), s8[4194304]{0:T(1024)(128)(4,1)S(1)}, s32[]{:S(2)}) async-start(s8[8388608]{0:T(1024)(128)(4,1)} %bitcast.8), calls=%async_computation | async-start | bytes 8388608
  24.2 6.1 %collective-permute-start.6 = (f32[512,1024]{1,0:T(8,128)S(1)}, f32[512,1024]{1,0:T(8,128)S(1)}, u32[]{:S(2)}, u32[]{:S(2)}) collective-permute-start(f32[512,1024]{1,0:T(8,128)S(1)} %get-tuple-element.26), channel_id=1, source_target_pairs={{0,4},{4,0},{8,12},{12,8},{16,20},{20,16},{24,28},{28,24},{32,36},... | collective-permute-start | bytes 6291464 | tf_op jit(solution)/shard_map/ppermute | solution.py:32
  26.5 8.4 %collective-permute-start.1 = (bf16[128,1024]{1,0:T(8,128)(2,1)S(1)}, bf16[128,1024]{1,0:T(8,128)(2,1)S(1)}, u32[]{:S(2)}, u32[]{:S(2)}) collective-permute-start(bf16[128,1024]{1,0:T(8,128)(2,1)S(1)} %maximum_select_fusion), channel_id=1, source_target_pairs={{0,968},{4,1020},{8,976},{12,964},{16,984},{20,972},{24,992},{28,9... | collective-permute-start | bytes 786440 | tf_op jit(solution)/shard_map/ppermute | solution.py:42
  30.3 31.7 %slice-start.1 = ((s8[8388608]{0:T(1024)(128)(4,1)}), s8[4194304]{0:T(1024)(128)(4,1)S(1)}, s32[]{:S(2)}) async-start(s8[8388608]{0:T(1024)(128)(4,1)} %bitcast.8), calls=%async_computation.1 | async-start | bytes 8388608
  30.5 10.7 %collective-permute-start.7 = (s16[224,1024]{1,0:T(8,128)(2,1)S(1)}, s16[224,1024]{1,0:T(8,128)(2,1)S(1)}, u32[]{:S(2)}, u32[]{:S(2)}) collective-permute-start(s16[224,1024]{1,0:T(8,128)(2,1)S(1)} %shard_map.70), channel_id=1, source_target_pairs={{0,16},{4,52},{8,24},{12,60},{16,32},{20,4},{24,40},{28,12},{32,48... | collective-permute-start | bytes 1376264 | tf_op jit(solution)/shard_map/ppermute | solution.py:27
  32.7 17.1 %collective-permute-start.2 = (bf16[128,1024]{1,0:T(8,128)(2,1)S(1)}, bf16[128,1024]{1,0:T(8,128)(2,1)S(1)}, u32[]{:S(2)}, u32[]{:S(2)}) collective-permute-start(bf16[128,1024]{1,0:T(8,128)(2,1)S(1)} %maximum_select_fusion), channel_id=1, source_target_pairs={{0,960},{4,964},{8,968},{12,972},{16,976},{20,980},{24,984},{28,98... | collective-permute-start | bytes 786440 | tf_op jit(solution)/shard_map/ppermute | solution.py:42
  34.9 16.8 %collective-permute-start.3 = (bf16[128,1024]{1,0:T(8,128)(2,1)S(1)}, bf16[128,1024]{1,0:T(8,128)(2,1)S(1)}, u32[]{:S(2)}, u32[]{:S(2)}) collective-permute-start(bf16[128,1024]{1,0:T(8,128)(2,1)S(1)} %collective-permute-done.1.g1_ref), channel_id=1, source_target_pairs={{0,8},{4,60},{8,16},{12,4},{16,24},{20,12},{24,32},{28,20},{32,40}... | collective-permute-start | bytes 786440 | tf_op jit(solution)/shard_map/ppermute | solution.py:27
  41.7 21.5 %collective-permute-start.8 = (s16[144,1024]{1,0:T(8,128)(2,1)S(1)}, s16[144,1024]{1,0:T(8,128)(2,1)S(1)}, u32[]{:S(2)}, u32[]{:S(2)}) collective-permute-start(s16[144,1024]{1,0:T(8,128)(2,1)S(1)} %get-tuple-element.29), channel_id=1, source_target_pairs={{0,8},{4,60},{8,16},{12,4},{16,24},{20,12},{24,32},{28,20},{32,40}... | collective-permute-start | bytes 884744 | tf_op jit(solution)/shard_map/ppermute | solution.py:27
  47.8 15.4 %collective-permute-start.9 = (s16[144,1024]{1,0:T(8,128)(2,1)S(1)}, s16[144,1024]{1,0:T(8,128)(2,1)S(1)}, u32[]{:S(2)}, u32[]{:S(2)}) collective-permute-start(s16[144,1024]{1,0:T(8,128)(2,1)S(1)} %get-tuple-element.30), channel_id=1, source_target_pairs={{0,16},{4,52},{8,24},{12,60},{16,32},{20,4},{24,40},{28,12},{32,48... | collective-permute-start | bytes 884744 | tf_op jit(solution)/shard_map/ppermute | solution.py:27
  49.8 7.5 %collective-permute-start.4 = (bf16[128,1024]{1,0:T(8,128)(2,1)S(1)}, bf16[128,1024]{1,0:T(8,128)(2,1)S(1)}, u32[]{:S(2)}, u32[]{:S(2)}) collective-permute-start(bf16[128,1024]{1,0:T(8,128)(2,1)S(1)} %collective-permute-done.1.g1_ref), channel_id=1, source_target_pairs={{0,4},{4,0},{8,12},{12,8},{16,20},{20,16},{24,28},{28,24},{32,36},... | collective-permute-start | bytes 786440 | tf_op jit(solution)/shard_map/ppermute | solution.py:32
  51.7 11.5 %collective-permute-start.5 = (bf16[128,1024]{1,0:T(8,128)(2,1)S(1)}, bf16[128,1024]{1,0:T(8,128)(2,1)S(1)}, u32[]{:S(2)}, u32[]{:S(2)}) collective-permute-start(bf16[128,1024]{1,0:T(8,128)(2,1)S(1)} %collective-permute-done.3.g2_ref), channel_id=1, source_target_pairs={{0,4},{4,0},{8,12},{12,8},{16,20},{20,16},{24,28},{28,24},{32,36},... | collective-permute-start | bytes 786440 | tf_op jit(solution)/shard_map/ppermute | solution.py:32
  54.1 11.6 %collective-permute-start.12 = (bf16[128,1024]{1,0:T(8,128)(2,1)S(1)}, bf16[128,1024]{1,0:T(8,128)(2,1)S(1)}, u32[]{:S(2)}, u32[]{:S(2)}) collective-permute-start(bf16[128,1024]{1,0:T(8,128)(2,1)S(1)} %collective-permute-done.3.g2_ref), channel_id=1, source_target_pairs={{0,8},{4,60},{8,16},{12,4},{16,24},{20,12},{24,32},{28,20},{32,40}... | collective-permute-start | bytes 786440 | tf_op jit(solution)/shard_map/ppermute | solution.py:27
  57.2 6.0 %copy-start.1 = (bf16[1,4,128,512]{3,2,1,0:T(8,128)(2,1)S(1)}, bf16[1,4,128,512]{3,2,1,0:T(8,128)(2,1)}, u32[]{:S(2)}) copy-start(bf16[1,4,128,512]{3,2,1,0:T(8,128)(2,1)} %param.7) | copy-start | bytes 1572868
  57.3 8.4 %collective-permute-start.13 = (bf16[64,1024]{1,0:T(8,128)(2,1)S(1)}, bf16[64,1024]{1,0:T(8,128)(2,1)S(1)}, u32[]{:S(2)}, u32[]{:S(2)}) collective-permute-start(bf16[64,1024]{1,0:T(8,128)(2,1)S(1)} %slice_select_fusion), channel_id=1, source_target_pairs={{0,16},{4,52},{8,24},{12,60},{16,32},{20,4},{24,40},{28,12},{32,48... | collective-permute-start | bytes 393224 | tf_op jit(solution)/shard_map/ppermute | solution.py:27
  63.7 6.0 %collective-permute-start.10 = (f32[128,512]{1,0:T(8,128)S(1)}, f32[128,512]{1,0:T(8,128)S(1)}, u32[]{:S(2)}, u32[]{:S(2)}) collective-permute-start(f32[128,512]{1,0:T(8,128)S(1)} %get-tuple-element.33), channel_id=1, source_target_pairs={{0,4},{4,0},{8,12},{12,8},{16,20},{20,16},{24,28},{28,24},{32,36},... | collective-permute-start | bytes 786440 | tf_op jit(solution)/shard_map/ppermute | solution.py:32
  65.7 5.9 %collective-permute-start.14 = (bf16[192,1024]{1,0:T(8,128)(2,1)S(1)}, bf16[192,1024]{1,0:T(8,128)(2,1)S(1)}, u32[]{:S(2)}, u32[]{:S(2)}) collective-permute-start(bf16[192,1024]{1,0:T(8,128)(2,1)S(1)} %pad_maximum_fusion), channel_id=1, source_target_pairs={{0,4},{4,0},{8,12},{12,8},{16,20},{20,16},{24,28},{28,24},{32,36},... | collective-permute-start | bytes 1179656 | tf_op jit(solution)/shard_map/ppermute | solution.py:32
  69.7 9.1 %collective-permute-start.11 = (bf16[128,512]{1,0:T(8,128)(2,1)S(1)}, bf16[128,512]{1,0:T(8,128)(2,1)S(1)}, u32[]{:S(2)}, u32[]{:S(2)}) collective-permute-start(bf16[128,512]{1,0:T(8,128)(2,1)S(1)} %add_convert_fusion), channel_id=1, source_target_pairs={{0,64},{4,68},{8,72},{12,76},{16,80},{20,84},{24,88},{28,92},{32,9... | collective-permute-start | bytes 393224 | tf_op jit(solution)/shard_map/ppermute | solution.py:42

commit v7 on v6

--- a/solution.py
+++ b/solution.py
@@ -224,7 +224,7 @@
         facing[pl.ds(pl.multiple_of(core * HALF, HALF), HALF)] = g4_ref[...]
         facing[pl.ds(pl.multiple_of((1 - core) * HALF, HALF), HALF)] = h34_ref[ROWS:]
         total[...] = start_ref[...]
-        for slot, x in enumerate((h1_ref, h2_ref, h34_ref.at[:ROWS], g3_ref)):
+        for slot, x in enumerate((h1_ref.at[:ROWS], h2_ref, h34_ref.at[:ROWS], g3_ref)):
             total[...] += times_transposed(x[...], chunk_of_weights(w_ref, place_ref[0], offsets[slot], chips))
         last = times_transposed(facing[...], chunk_of_weights(w_ref, place_ref[0], offsets[4], chips))
         out_ref[...] = (total[...] + last).astype(BF16)
@@ -266,8 +266,9 @@
     g2 = split_shift(g1, 1)
     g3 = split_shift(g2, 1)
     g4 = split_shift(jnp.where(first, g2[:HALF], g2[HALF:]), 2)
-    to_mate, g0 = lax.optimization_barrier((g1, g0))
-    h1, h2, h34 = core_swap(to_mate), core_swap(g2), core_swap(jnp.concatenate([g3, g4], 0))
+    h1 = core_swap(jnp.concatenate([g1, g1[: HALF // 2]], 0))
+    to_mate, g0 = lax.optimization_barrier((g2, g0))
+    h2, h34 = core_swap(to_mate), core_swap(jnp.concatenate([g3, g4], 0))
     early = backproject_first(place, (g0, g1, g2), w_local, chips)
 
     after, _, _, _ = lax.optimization_barrier((place, early, h1, h2))

time: 80.1 us -> 79.9 us (level)
  waiting for transfers between devices: 11.7 us -> 9.1 us
  starting transfers between devices: 54.2 us -> 56.6 us
    ppermute x6, starting transfers between devices: 28.5 us -> 33 us  [core_swap(): return lax.ppermute(value, 'tensor', [(i, i ^ 1) for i in range(peers)])]
    ppermute x6, waiting for transfers between devices: 4.48 us -> 1.84 us  [split_shift(): return lax.ppermute(value, 'tensor', pairs)]
    ppermute x6, starting transfers between devices: 19.9 us -> 17.8 us  [split_shift(): return lax.ppermute(value, 'tensor', pairs)]
where the time goes in v7:
time: 79.9 us; the launch traced here: 79.3 us
  starting transfers between devices  56.6 us (71%)
  Pallas kernels  9.16 us (11%)
  waiting for transfers between devices  9.1 us (11%)
  local copies, waits for them, and re-layouts  1.71 us (2%)
  between operations  1.61 us (2%)
  other arithmetic  1.15 us (1%)
    ppermute x6, starting transfers between devices, core_swap(): return lax.ppermute(value, 'tensor', [(i, i ^ 1) for i in range(peers)])  33 us
    ppermute x6, starting transfers between devices, split_shift(): return lax.ppermute(value, 'tensor', pairs)  17.8 us
    pallas_call x6, Pallas kernels, call(): pl.pallas_call(body, grid=(1,), in_specs=specs, out_specs=[VMEM] * len(ou...  9.16 us
    ppermute x3, starting transfers between devices, next_section(): return lax.ppermute(value, ('section', 'tensor'), pairs)  5.76 us
    ppermute x3, waiting for transfers between devices, next_section(): return lax.ppermute(value, ('section', 'tensor'), pairs)  4.89 us
    ppermute x6, waiting for transfers between devices, core_swap(): return lax.ppermute(value, 'tensor', [(i, i ^ 1) for i in range(peers)])  2.37 us
    ppermute x6, waiting for transfers between devices, split_shift(): return lax.ppermute(value, 'tensor', pairs)  1.84 us
    unnamed x9, local copies, waits for them, and re-layouts  1.71 us
  transfers between devices with their start and end apart: 15, of which 5 were waited for; matrix products, arithmetic and copies ran while one was open for 0% of the time, Pallas kernels for 6%

profile of v7, /device:TPU:1, one launch (start us, length us, event | category | flops | bytes accessed | tf_op | source)
XLA Modules:
  0.0 79.3 jit_solution(14015964785555490711)
XLA Ops:
  0.6 16.1 %collective-permute-start = (bf16[128,512]{1,0:T(8,128)(2,1)}, bf16[128,512]{1,0:T(8,128)(2,1)S(1)}, u32[]{:S(2)}, u32[]{:S(2)}) collective-permute-start(bf16[128,512]{1,0:T(8,128)(2,1)} %bitcast.15), channel_id=1, source_target_pairs={{0,4},{4,0},{8,12},{12,8},{16,20},{20,16},{24,28},{28,24},{32,36},... | collective-permute-start | bytes 393224 | tf_op jit(solution)/shard_map/ppermute | solution.py:32
  17.4 0.5 collective-permute-done
  17.9 1.0 %maximum_select_fusion = bf16[128,1024]{1,0:T(8,128)(2,1)S(1)} fusion(bf16[128,512]{1,0:T(8,128)(2,1)S(1)} %collective-permute-done, bf16[128,512]{1,0:T(8,128)(2,1)} %bitcast.16, pred[]{:T(512)S(6)} %eq.5), kind=kLoop, calls=%fused_computation.2 | loop fusion | flops 1179648 | bytes 524289 | tf_op jit(solution)/shard_map/jit(_where)/select_n | solution.py:253
  18.9 0.0 copy-start
  18.9 1.0 %copy-done = bf16[1,4,128,512]{3,2,1,0:T(8,128)(2,1)S(1)} copy-done((bf16[1,4,128,512]{3,2,1,0:T(8,128)(2,1)S(1)}, bf16[1,4,128,512]{3,2,1,0:T(8,128)(2,1)}, u32[]{:S(2)}) %copy-start) | copy-done | bytes 524312
  20.0 4.3 %shard_map.69 = (f32[512,1024]{1,0:T(8,128)S(1)}, f32[128,1024]{1,0:T(8,128)S(1)}, f32[128,1024]{1,0:T(8,128)S(1)}, f32[128,1024]{1,0:T(8,128)S(1)}, f32[64,1024]{1,0:T(8,128)S(1)}, /*index=5*/f32[64,1024]{1,0:T(8,128)S(1)}) custom-call(s32[1]{0:T(128)} %bitcast.place_ref, s32[1]{0:T(128)S(6)} %copy.8.plan_ref, bf16[4,128,512]{2,1,0:T(8,128)(2,1)S(1)} %bitcast.12, ...), custom_call_target="tpu_custom_call" | custom-call | flops 1 | bytes 1 | tf_op jit(solution)/shard_map/pallas_call | solution.py:46
  24.2 2.3 %collective-permute-start.6 = (f32[512,1024]{1,0:T(8,128)S(1)}, f32[512,1024]{1,0:T(8,128)S(1)}, u32[]{:S(2)}, u32[]{:S(2)}) collective-permute-start(f32[512,1024]{1,0:T(8,128)S(1)} %get-tuple-element.26), channel_id=1, source_target_pairs={{0,4},{4,0},{8,12},{12,8},{16,20},{20,16},{24,28},{28,24},{32,36},... | collective-permute-start | bytes 6291464 | tf_op jit(solution)/shard_map/ppermute | solution.py:32
  26.5 1.9 %collective-permute-start.1 = (bf16[128,1024]{1,0:T(8,128)(2,1)S(1)}, bf16[128,1024]{1,0:T(8,128)(2,1)S(1)}, u32[]{:S(2)}, u32[]{:S(2)}) collective-permute-start(bf16[128,1024]{1,0:T(8,128)(2,1)S(1)} %maximum_select_fusion), channel_id=1, source_target_pairs={{0,968},{4,1020},{8,976},{12,964},{16,984},{20,972},{24,992},{28,9... | collective-permute-start | bytes 786440 | tf_op jit(solution)/shard_map/ppermute | solution.py:42
  28.4 1.8 %collective-permute-done.6.in3_ref.in4_ref.in2_ref.in1_ref.in_ref = f32[512,1024]{1,0:T(8,128)S(1)} collective-permute-done((f32[512,1024]{1,0:T(8,128)S(1)}, f32[512,1024]{1,0:T(8,128)S(1)}, u32[]{:S(2)}, u32[]{:S(2)}) %collective-permute-start.6) | collective-permute-done | bytes 2097184 | tf_op jit(solution)/shard_map/ppermute | solution.py:32
  30.3 0.2 shard_map.70
  30.5 2.2 %collective-permute-start.7 = (s16[224,1024]{1,0:T(8,128)(2,1)S(1)}, s16[224,1024]{1,0:T(8,128)(2,1)S(1)}, u32[]{:S(2)}, u32[]{:S(2)}) collective-permute-start(s16[224,1024]{1,0:T(8,128)(2,1)S(1)} %shard_map.70), channel_id=1, source_target_pairs={{0,16},{4,52},{8,24},{12,60},{16,32},{20,4},{24,40},{28,12},{32,48... | collective-permute-start | bytes 1376264 | tf_op jit(solution)/shard_map/ppermute | solution.py:27
  32.7 1.9 %collective-permute-start.3 = (bf16[128,1024]{1,0:T(8,128)(2,1)S(1)}, bf16[128,1024]{1,0:T(8,128)(2,1)S(1)}, u32[]{:S(2)}, u32[]{:S(2)}) collective-permute-start(bf16[128,1024]{1,0:T(8,128)(2,1)S(1)} %maximum_select_fusion), channel_id=1, source_target_pairs={{0,960},{4,964},{8,968},{12,972},{16,976},{20,980},{24,984},{28,98... | collective-permute-start | bytes 786440 | tf_op jit(solution)/shard_map/ppermute | solution.py:42
  34.6 0.3 collective-permute-done.1.g1_ref
  34.9 1.9 %collective-permute-start.2 = (bf16[128,1024]{1,0:T(8,128)(2,1)S(1)}, bf16[128,1024]{1,0:T(8,128)(2,1)S(1)}, u32[]{:S(2)}, u32[]{:S(2)}) collective-permute-start(bf16[128,1024]{1,0:T(8,128)(2,1)S(1)} %collective-permute-done.1.g1_ref), channel_id=1, source_target_pairs={{0,8},{4,60},{8,16},{12,4},{16,24},{20,12},{24,32},{28,20},{32,40}... | collective-permute-start | bytes 786440 | tf_op jit(solution)/shard_map/ppermute | solution.py:27
  36.8 6.9 %collective-permute-start.4 = (bf16[160,1024]{1,0:T(8,128)(2,1)S(1)}, bf16[160,1024]{1,0:T(8,128)(2,1)S(1)}, u32[]{:S(2)}, u32[]{:S(2)}) collective-permute-start(bf16[160,1024]{1,0:T(8,128)(2,1)S(1)} %pad_maximum_fusion.1), channel_id=1, source_target_pairs={{0,4},{4,0},{8,12},{12,8},{16,20},{20,16},{24,28},{28,24},{32,36},... | collective-permute-start | bytes 983048 | tf_op jit(solution)/shard_map/ppermute | solution.py:32
  43.8 0.0 collective-permute-done.7.q34_ref
  43.8 0.5 shard_map.71
  44.3 4.9 %collective-permute-start.8 = (s16[144,1024]{1,0:T(8,128)(2,1)S(1)}, s16[144,1024]{1,0:T(8,128)(2,1)S(1)}, u32[]{:S(2)}, u32[]{:S(2)}) collective-permute-start(s16[144,1024]{1,0:T(8,128)(2,1)S(1)} %get-tuple-element.29), channel_id=1, source_target_pairs={{0,8},{4,60},{8,16},{12,4},{16,24},{20,12},{24,32},{28,20},{32,40}... | collective-permute-start | bytes 884744 | tf_op jit(solution)/shard_map/ppermute | solution.py:27
  49.1 1.9 %collective-permute-start.9 = (s16[144,1024]{1,0:T(8,128)(2,1)S(1)}, s16[144,1024]{1,0:T(8,128)(2,1)S(1)}, u32[]{:S(2)}, u32[]{:S(2)}) collective-permute-start(s16[144,1024]{1,0:T(8,128)(2,1)S(1)} %get-tuple-element.30), channel_id=1, source_target_pairs={{0,16},{4,52},{8,24},{12,60},{16,32},{20,4},{24,40},{28,12},{32,48... | collective-permute-start | bytes 884744 | tf_op jit(solution)/shard_map/ppermute | solution.py:27
  51.1 1.9 %collective-permute-start.5 = (bf16[128,1024]{1,0:T(8,128)(2,1)S(1)}, bf16[128,1024]{1,0:T(8,128)(2,1)S(1)}, u32[]{:S(2)}, u32[]{:S(2)}) collective-permute-start(bf16[128,1024]{1,0:T(8,128)(2,1)S(1)} %collective-permute-done.2.g2_ref), channel_id=1, source_target_pairs={{0,4},{4,0},{8,12},{12,8},{16,20},{20,16},{24,28},{28,24},{32,36},... | collective-permute-start | bytes 786440 | tf_op jit(solution)/shard_map/ppermute | solution.py:32
  53.0 2.3 %collective-permute-start.12 = (bf16[128,1024]{1,0:T(8,128)(2,1)S(1)}, bf16[128,1024]{1,0:T(8,128)(2,1)S(1)}, u32[]{:S(2)}, u32[]{:S(2)}) collective-permute-start(bf16[128,1024]{1,0:T(8,128)(2,1)S(1)} %collective-permute-done.2.g2_ref), channel_id=1, source_target_pairs={{0,8},{4,60},{8,16},{12,4},{16,24},{20,12},{24,32},{28,20},{32,40}... | collective-permute-start | bytes 786440 | tf_op jit(solution)/shard_map/ppermute | solution.py:27
  55.3 0.0 copy-start.1
  55.3 4.7 %collective-permute-start.13 = (bf16[64,1024]{1,0:T(8,128)(2,1)S(1)}, bf16[64,1024]{1,0:T(8,128)(2,1)S(1)}, u32[]{:S(2)}, u32[]{:S(2)}) collective-permute-start(bf16[64,1024]{1,0:T(8,128)(2,1)S(1)} %slice_select_fusion), channel_id=1, source_target_pairs={{0,16},{4,52},{8,24},{12,60},{16,32},{20,4},{24,40},{28,12},{32,48... | collective-permute-start | bytes 393224 | tf_op jit(solution)/shard_map/ppermute | solution.py:27
  60.0 1.2 %shard_map.68.start_ref = f32[128,512]{1,0:T(8,128)S(1)} custom-call(s32[1]{0:T(128)} %bitcast.place_ref, bf16[128,1024]{1,0:T(8,128)(2,1)S(1)} %collective-permute-done.3.u_ref, bf16[128,1024]{1,0:T(8,128)(2,1)S(1)} %collective-permute-done.1.g1_ref, bf16[128,1024]{1,0:T(8,128)(2,1)S(1)} %collective-permute-done.2.g2_ref, bf16[512,8192]{1,0:T(8,128)(2,1)S(1)} %bitcast.10), custom_call_target="tpu_custom_call" | custom-call | flops 1 | bytes 1 | tf_op jit(solution)/shard_map/pallas_call | solution.py:46
  61.3 0.5 shard_map.72
  61.8 2.6 %collective-permute-start.10 = (f32[128,512]{1,0:T(8,128)S(1)}, f32[128,512]{1,0:T(8,128)S(1)}, u32[]{:S(2)}, u32[]{:S(2)}) collective-permute-start(f32[128,512]{1,0:T(8,128)S(1)} %get-tuple-element.33), channel_id=1, source_target_pairs={{0,4},{4,0},{8,12},{12,8},{16,20},{20,16},{24,28},{28,24},{32,36},... | collective-permute-start | bytes 786440 | tf_op jit(solution)/shard_map/ppermute | solution.py:32
  64.4 1.8 %collective-permute-done.13.g4_ref = bf16[64,1024]{1,0:T(8,128)(2,1)S(1)} collective-permute-done((bf16[64,1024]{1,0:T(8,128)(2,1)S(1)}, bf16[64,1024]{1,0:T(8,128)(2,1)S(1)}, u32[]{:S(2)}, u32[]{:S(2)}) %collective-permute-start.13) | collective-permute-done | bytes 131104 | tf_op jit(solution)/shard_map/ppermute | solution.py:27
  66.3 3.2 %collective-permute-start.14 = (bf16[192,1024]{1,0:T(8,128)(2,1)S(1)}, bf16[192,1024]{1,0:T(8,128)(2,1)S(1)}, u32[]{:S(2)}, u32[]{:S(2)}) collective-permute-start(bf16[192,1024]{1,0:T(8,128)(2,1)S(1)} %pad_maximum_fusion), channel_id=1, source_target_pairs={{0,4},{4,0},{8,12},{12,8},{16,20},{20,16},{24,28},{28,24},{32,36},... | collective-permute-start | bytes 1179656 | tf_op jit(solution)/shard_map/ppermute | solution.py:32
  69.5 1.9 %collective-permute-start.11 = (bf16[128,512]{1,0:T(8,128)(2,1)S(1)}, bf16[128,512]{1,0:T(8,128)(2,1)S(1)}, u32[]{:S(2)}, u32[]{:S(2)}) collective-permute-start(bf16[128,512]{1,0:T(8,128)(2,1)S(1)} %add_convert_fusion), channel_id=1, source_target_pairs={{0,64},{4,68},{8,72},{12,76},{16,80},{20,84},{24,88},{28,92},{32,9... | collective-permute-start | bytes 393224 | tf_op jit(solution)/shard_map/ppermute | solution.py:42
  71.5 2.5 %shard_map.73 = bf16[128,512]{1,0:T(8,128)(2,1)} custom-call(s32[1]{0:T(128)} %bitcast.place_ref, bf16[160,1024]{1,0:T(8,128)(2,1)S(1)} %collective-permute-done.4.h1_ref, bf16[128,1024]{1,0:T(8,128)(2,1)S(1)} %collective-permute-done.5.h2_ref, bf16[192,1024]{1,0:T(8,128)(2,1)S(1)} %collective-permute-done.14.h34_ref, ...), custom_call_target="tpu_custom_call" | custom-call | flops 1 | bytes 1 | tf_op jit(solution)/shard_map/pallas_call | solution.py:46
  74.0 4.6 %collective-permute-done.11 = bf16[128,512]{1,0:T(8,128)(2,1)S(1)} collective-permute-done((bf16[128,512]{1,0:T(8,128)(2,1)S(1)}, bf16[128,512]{1,0:T(8,128)(2,1)S(1)}, u32[]{:S(2)}, u32[]{:S(2)}) %collective-permute-start.11) | collective-permute-done | bytes 131104 | tf_op jit(solution)/shard_map/ppermute | solution.py:42
  78.7 0.7 copy.9
  (20 shorter events, 0.1 us)
Async XLA Ops:
  0.6 17.2 %collective-permute-start = (bf16[128,512]{1,0:T(8,128)(2,1)}, bf16[128,512]{1,0:T(8,128)(2,1)S(1)}, u32[]{:S(2)}, u32[]{:S(2)}) collective-permute-start(bf16[128,512]{1,0:T(8,128)(2,1)} %bitcast.15), channel_id=1, source_target_pairs={{0,4},{4,0},{8,12},{12,8},{16,20},{20,16},{24,28},{28,24},{32,36},... | collective-permute-start | bytes 393224 | tf_op jit(solution)/shard_map/ppermute | solution.py:32
  18.9 1.0 %copy-start = (bf16[1,4,128,512]{3,2,1,0:T(8,128)(2,1)S(1)}, bf16[1,4,128,512]{3,2,1,0:T(8,128)(2,1)}, u32[]{:S(2)}) copy-start(bf16[1,4,128,512]{3,2,1,0:T(8,128)(2,1)} %param.6) | copy-start | bytes 1572868
  20.0 40.0 %slice-start = ((s8[8388608]{0:T(1024)(128)(4,1)}), s8[4194304]{0:T(1024)(128)(4,1)S(1)}, s32[]{:S(2)}) async-start(s8[8388608]{0:T(1024)(128)(4,1)} %bitcast.8), calls=%async_computation | async-start | bytes 8388608
  24.2 6.1 %collective-permute-start.6 = (f32[512,1024]{1,0:T(8,128)S(1)}, f32[512,1024]{1,0:T(8,128)S(1)}, u32[]{:S(2)}, u32[]{:S(2)}) collective-permute-start(f32[512,1024]{1,0:T(8,128)S(1)} %get-tuple-element.26), channel_id=1, source_target_pairs={{0,4},{4,0},{8,12},{12,8},{16,20},{20,16},{24,28},{28,24},{32,36},... | collective-permute-start | bytes 6291464 | tf_op jit(solution)/shard_map/ppermute | solution.py:32
  26.5 8.4 %collective-permute-start.1 = (bf16[128,1024]{1,0:T(8,128)(2,1)S(1)}, bf16[128,1024]{1,0:T(8,128)(2,1)S(1)}, u32[]{:S(2)}, u32[]{:S(2)}) collective-permute-start(bf16[128,1024]{1,0:T(8,128)(2,1)S(1)} %maximum_select_fusion), channel_id=1, source_target_pairs={{0,968},{4,1020},{8,976},{12,964},{16,984},{20,972},{24,992},{28,9... | collective-permute-start | bytes 786440 | tf_op jit(solution)/shard_map/ppermute | solution.py:42
  30.3 29.7 %slice-start.1 = ((s8[8388608]{0:T(1024)(128)(4,1)}), s8[4194304]{0:T(1024)(128)(4,1)S(1)}, s32[]{:S(2)}) async-start(s8[8388608]{0:T(1024)(128)(4,1)} %bitcast.8), calls=%async_computation.1 | async-start | bytes 8388608
  30.5 13.3 %collective-permute-start.7 = (s16[224,1024]{1,0:T(8,128)(2,1)S(1)}, s16[224,1024]{1,0:T(8,128)(2,1)S(1)}, u32[]{:S(2)}, u32[]{:S(2)}) collective-permute-start(s16[224,1024]{1,0:T(8,128)(2,1)S(1)} %shard_map.70), channel_id=1, source_target_pairs={{0,16},{4,52},{8,24},{12,60},{16,32},{20,4},{24,40},{28,12},{32,48... | collective-permute-start | bytes 1376264 | tf_op jit(solution)/shard_map/ppermute | solution.py:27
  32.7 18.4 %collective-permute-start.3 = (bf16[128,1024]{1,0:T(8,128)(2,1)S(1)}, bf16[128,1024]{1,0:T(8,128)(2,1)S(1)}, u32[]{:S(2)}, u32[]{:S(2)}) collective-permute-start(bf16[128,1024]{1,0:T(8,128)(2,1)S(1)} %maximum_select_fusion), channel_id=1, source_target_pairs={{0,960},{4,964},{8,968},{12,972},{16,976},{20,980},{24,984},{28,98... | collective-permute-start | bytes 786440 | tf_op jit(solution)/shard_map/ppermute | solution.py:42
  34.9 16.2 %collective-permute-start.2 = (bf16[128,1024]{1,0:T(8,128)(2,1)S(1)}, bf16[128,1024]{1,0:T(8,128)(2,1)S(1)}, u32[]{:S(2)}, u32[]{:S(2)}) collective-permute-start(bf16[128,1024]{1,0:T(8,128)(2,1)S(1)} %collective-permute-done.1.g1_ref), channel_id=1, source_target_pairs={{0,8},{4,60},{8,16},{12,4},{16,24},{20,12},{24,32},{28,20},{32,40}... | collective-permute-start | bytes 786440 | tf_op jit(solution)/shard_map/ppermute | solution.py:27
  36.8 18.5 %collective-permute-start.4 = (bf16[160,1024]{1,0:T(8,128)(2,1)S(1)}, bf16[160,1024]{1,0:T(8,128)(2,1)S(1)}, u32[]{:S(2)}, u32[]{:S(2)}) collective-permute-start(bf16[160,1024]{1,0:T(8,128)(2,1)S(1)} %pad_maximum_fusion.1), channel_id=1, source_target_pairs={{0,4},{4,0},{8,12},{12,8},{16,20},{20,16},{24,28},{28,24},{32,36},... | collective-permute-start | bytes 983048 | tf_op jit(solution)/shard_map/ppermute | solution.py:32
  44.3 17.0 %collective-permute-start.8 = (s16[144,1024]{1,0:T(8,128)(2,1)S(1)}, s16[144,1024]{1,0:T(8,128)(2,1)S(1)}, u32[]{:S(2)}, u32[]{:S(2)}) collective-permute-start(s16[144,1024]{1,0:T(8,128)(2,1)S(1)} %get-tuple-element.29), channel_id=1, source_target_pairs={{0,8},{4,60},{8,16},{12,4},{16,24},{20,12},{24,32},{28,20},{32,40}... | collective-permute-start | bytes 884744 | tf_op jit(solution)/shard_map/ppermute | solution.py:27
  49.1 12.1 %collective-permute-start.9 = (s16[144,1024]{1,0:T(8,128)(2,1)S(1)}, s16[144,1024]{1,0:T(8,128)(2,1)S(1)}, u32[]{:S(2)}, u32[]{:S(2)}) collective-permute-start(s16[144,1024]{1,0:T(8,128)(2,1)S(1)} %get-tuple-element.30), channel_id=1, source_target_pairs={{0,16},{4,52},{8,24},{12,60},{16,32},{20,4},{24,40},{28,12},{32,48... | collective-permute-start | bytes 884744 | tf_op jit(solution)/shard_map/ppermute | solution.py:27
  51.1 10.2 %collective-permute-start.5 = (bf16[128,1024]{1,0:T(8,128)(2,1)S(1)}, bf16[128,1024]{1,0:T(8,128)(2,1)S(1)}, u32[]{:S(2)}, u32[]{:S(2)}) collective-permute-start(bf16[128,1024]{1,0:T(8,128)(2,1)S(1)} %collective-permute-done.2.g2_ref), channel_id=1, source_target_pairs={{0,4},{4,0},{8,12},{12,8},{16,20},{20,16},{24,28},{28,24},{32,36},... | collective-permute-start | bytes 786440 | tf_op jit(solution)/shard_map/ppermute | solution.py:32
  53.0 13.3 %collective-permute-start.12 = (bf16[128,1024]{1,0:T(8,128)(2,1)S(1)}, bf16[128,1024]{1,0:T(8,128)(2,1)S(1)}, u32[]{:S(2)}, u32[]{:S(2)}) collective-permute-start(bf16[128,1024]{1,0:T(8,128)(2,1)S(1)} %collective-permute-done.2.g2_ref), channel_id=1, source_target_pairs={{0,8},{4,60},{8,16},{12,4},{16,24},{20,12},{24,32},{28,20},{32,40}... | collective-permute-start | bytes 786440 | tf_op jit(solution)/shard_map/ppermute | solution.py:27
  55.3 6.0 %copy-start.1 = (bf16[1,4,128,512]{3,2,1,0:T(8,128)(2,1)S(1)}, bf16[1,4,128,512]{3,2,1,0:T(8,128)(2,1)}, u32[]{:S(2)}) copy-start(bf16[1,4,128,512]{3,2,1,0:T(8,128)(2,1)} %param.7) | copy-start | bytes 1572868
  55.3 10.9 %collective-permute-start.13 = (bf16[64,1024]{1,0:T(8,128)(2,1)S(1)}, bf16[64,1024]{1,0:T(8,128)(2,1)S(1)}, u32[]{:S(2)}, u32[]{:S(2)}) collective-permute-start(bf16[64,1024]{1,0:T(8,128)(2,1)S(1)} %slice_select_fusion), channel_id=1, source_target_pairs={{0,16},{4,52},{8,24},{12,60},{16,32},{20,4},{24,40},{28,12},{32,48... | collective-permute-start | bytes 393224 | tf_op jit(solution)/shard_map/ppermute | solution.py:27
  61.8 7.7 %collective-permute-start.10 = (f32[128,512]{1,0:T(8,128)S(1)}, f32[128,512]{1,0:T(8,128)S(1)}, u32[]{:S(2)}, u32[]{:S(2)}) collective-permute-start(f32[128,512]{1,0:T(8,128)S(1)} %get-tuple-element.33), channel_id=1, source_target_pairs={{0,4},{4,0},{8,12},{12,8},{16,20},{20,16},{24,28},{28,24},{32,36},... | collective-permute-start | bytes 786440 | tf_op jit(solution)/shard_map/ppermute | solution.py:32
  66.3 5.2 %collective-permute-start.14 = (bf16[192,1024]{1,0:T(8,128)(2,1)S(1)}, bf16[192,1024]{1,0:T(8,128)(2,1)S(1)}, u32[]{:S(2)}, u32[]{:S(2)}) collective-permute-start(bf16[192,1024]{1,0:T(8,128)(2,1)S(1)} %pad_maximum_fusion), channel_id=1, source_target_pairs={{0,4},{4,0},{8,12},{12,8},{16,20},{20,16},{24,28},{28,24},{32,36},... | collective-permute-start | bytes 1179656 | tf_op jit(solution)/shard_map/ppermute | solution.py:32
  69.5 9.1 %collective-permute-start.11 = (bf16[128,512]{1,0:T(8,128)(2,1)S(1)}, bf16[128,512]{1,0:T(8,128)(2,1)S(1)}, u32[]{:S(2)}, u32[]{:S(2)}) collective-permute-start(bf16[128,512]{1,0:T(8,128)(2,1)S(1)} %add_convert_fusion), channel_id=1, source_target_pairs={{0,64},{4,68},{8,72},{12,76},{16,80},{20,84},{24,88},{28,92},{32,9... | collective-permute-start | bytes 393224 | tf_op jit(solution)/shard_map/ppermute | solution.py:42
